TPU v7x, 32 devices: a whole 2x2x4 slice. The times are simulated.
32 devices in a mesh: flop: 4 (over z), turn: 4 (over y, core), river: 2 (over x).
Axes of the slice: x: 2, y: 2, z: 4, core: 2. Of those that a mesh axis runs over, the one named last changes fastest.
Arguments:
- regrets: float32 [4, 256, 1326], P('flop', ('turn', 'river')), may hold values from -6 to 6
- opp_reach: bfloat16 [4, 256, 1326], P('flop', ('turn', 'river')), may hold values from 0 to 1
- pot_size: int32 [4, 256], P('flop', ('turn', 'river')), may hold values from 1 to 8
- line_kind: int32 [4, 256], P('flop', ('turn', 'river')), may hold values from 0 to 2
- board_lines: int32 [4, 4, 4, 256], P('flop', 'turn', 'river'), may hold values from 0 to 255, as said below
- board_count: int32 [4, 4, 4], P('flop', 'turn', 'river'), may hold values from 64 to 256, as said below
- hand_ranks: int32 [4, 4, 4, 1326], P('flop', 'turn', 'river'), may hold values from 0 to 7461
- live_hands: int32 [4, 4, 4, 1326], P('flop', 'turn', 'river'), may hold values 0 or 1
Outputs:
- new_regrets: float32 [4, 256, 1326], P('flop', ('turn', 'river'))
- chance_values: float32 [128, 1326], P(('turn', 'river'))
Inputs may be any that keep to these rules, and one draw needn't show every extreme that they name: `board_lines`: each board lists 256 different lines of its flop; its first board_count slots hold the lines live on it, the other slots add nothing. `board_count`: in every flop one board has all 256 slots live and another only 64.
All inputs are finite; a program needn't handle non-finite values. No bound on the sum of `live_hands` on one device may be relied on, other than what follows from the above.
Results may differ from a plain program's by a relative error of at most 0.0003.
Values may be sent and summed in bfloat16 or wider, within the bound.
No kernel may reach another device: no remote copies, remote signals or barrier semaphores. Data moves between devices by JAX's collectives and lax.ppermute only.
A program may use at most 64 MiB of HBM per device.

v0:
```python
import jax
import jax.numpy as jnp
import numpy as np
from jax import lax
from jax.sharding import PartitionSpec as P

CARDS = 52
ACTS = 2


floor_share = 0.1


def disjoint_table(card_count):
    card_first, card_second = np.triu_indices(card_count, 1)
    first_cards = jnp.asarray(card_first.astype(np.int32))
    second_cards = jnp.asarray(card_second.astype(np.int32))
    apart = (first_cards[:, None] != first_cards[None, :]) & (
        first_cards[:, None] != second_cards[None, :]
    )
    apart = (
        apart
        & (second_cards[:, None] != first_cards[None, :])
        & (second_cards[:, None] != second_cards[None, :])
    )
    return apart


def payoff_matrix(board_ranks, board_live, apart):
    both_live = apart & (board_live[:, None] > 0) & (board_live[None, :] > 0)
    fold_part = both_live.astype(jnp.float32)
    ordering = jnp.sign(board_ranks[None, :] - board_ranks[:, None]).astype(jnp.float32)
    return jnp.concatenate([fold_part * ordering, fold_part], axis=1).astype(jnp.bfloat16)


def on_device(
    regrets, opp_reach, pot_size, line_kind, board_lines, board_count, hand_ranks, live_hands
):
    hand_count = opp_reach.shape[2]
    boards_here = board_lines.shape[2]
    board_total = lax.axis_size("turn") * lax.axis_size("river") * boards_here
    pot_float = pot_size.astype(jnp.float32)
    show_coef = jnp.where(line_kind == 0, pot_float, 0.0)
    fold_coef = jnp.where(line_kind == 1, -pot_float, jnp.where(line_kind == 2, pot_float, 0.0))
    line_coef = jnp.stack([show_coef, fold_coef], axis=2).astype(jnp.bfloat16)
    reach_whole, coef_whole = (
        lax.all_gather(opp_reach, ("turn", "river"), axis=1, tiled=True),
        lax.all_gather(line_coef, ("turn", "river"), axis=1, tiled=True),
    )
    reach_whole = reach_whole[0]
    coef_whole = coef_whole[0]
    line_total = reach_whole.shape[0]
    slot_total = board_lines.shape[3]
    apart = disjoint_table(CARDS)
    chance_scale = 1.0 / (board_total * hand_count)
    line_table = jnp.zeros((line_total, hand_count), jnp.float32)
    for board_index in range(boards_here):
        slot_lines = board_lines[0, 0, board_index]
        live_count = board_count[0, 0, board_index]
        slot_reach = jnp.take(reach_whole, slot_lines, axis=0)
        slot_coef = jnp.take(coef_whole, slot_lines, axis=0).astype(jnp.float32)
        matrix = payoff_matrix(hand_ranks[0, 0, board_index], live_hands[0, 0, board_index], apart)

        def evaluate(
            first_row,
            row_count,
            slot_reach=slot_reach,
            slot_coef=slot_coef,
            matrix=matrix,
            live_count=live_count,
        ):
            products = jnp.dot(slot_reach, matrix, preferred_element_type=jnp.float32)
            slot_ids = first_row + jnp.arange(row_count, dtype=jnp.int32)
            keep_mask = (slot_ids < live_count).astype(jnp.float32)
            board_value = (
                slot_coef[:, 0:1] * products[:, :hand_count]
                + slot_coef[:, 1:2] * products[:, hand_count:]
            )
            return board_value * (chance_scale * keep_mask)[:, None]

        values = evaluate(0, slot_total)
        position = (
            jnp.full((line_total,), slot_total, jnp.int32)
            .at[slot_lines]
            .set(jnp.arange(slot_total, dtype=jnp.int32))
        )
        padded_values = jnp.concatenate([values, jnp.zeros((1, hand_count), jnp.float32)], axis=0)
        line_table = line_table + jnp.take(padded_values, position, axis=0)
    line_values = lax.psum_scatter(
        lax.slice_in_dim(
            line_table, 0, regrets.shape[1] * lax.axis_size(("turn", "river")), axis=0
        ),
        ("turn", "river"),
        scatter_dimension=0,
        tiled=True,
    )
    held_regret = regrets[0]
    group_total = held_regret.shape[0] // ACTS
    grouped = held_regret.reshape(group_total, ACTS, hand_count)
    worth_lines = line_values.reshape(group_total, ACTS, hand_count)
    positive = jnp.maximum(grouped, 0.0)
    strategy = (positive + floor_share) / (
        jnp.sum(positive, axis=1, keepdims=True) + ACTS * floor_share
    )
    node_values = jnp.sum(strategy * worth_lines, axis=1)
    updated = jnp.maximum(grouped + worth_lines - node_values[:, None, :], 0.0).reshape(
        held_regret.shape
    )
    chance_values = lax.psum(node_values, "flop") / lax.axis_size("flop")
    return (updated[None], chance_values)


def solution(mesh):
    placed = (
        P("flop", ("turn", "river"), None),
        P("flop", ("turn", "river"), None),
        P("flop", ("turn", "river")),
        P("flop", ("turn", "river")),
        P("flop", "turn", "river", None),
        P("flop", "turn", "river"),
        P("flop", "turn", "river", None),
        P("flop", "turn", "river", None),
    )
    return jax.shard_map(
        on_device,
        mesh=mesh,
        in_specs=placed,
        out_specs=(P("flop", ("turn", "river"), None), P(("turn", "river"), None)),
        check_vma=False,
    )
```

profile of v0, /device:TPU:0, one launch (start us, length us, event | category | flops | bytes accessed | tf_op | source)
XLA Modules:
  0.0 181.3 jit_solution(128480036967856347)
XLA Ops:
  7.2 0.0 reduce-scatter.2.cloned.1.call-start
  7.2 0.8 fusion.33
  8.0 0.8 compare_select_fusion.1
  8.8 19.1 %all_gather.7 = bf16[1,256,1326]{2,1,0:T(8,128)(2,1)S(1)} all-gather(bf16[1,32,1326]{2,1,0:T(8,128)(2,1)} %param.17), channel_id=1, replica_groups=mesh['flop'=4,'turn'=4,'river'=2] {'turn','river'}, dimensions={1}, use_global_device_ids=true | all-gather | bytes 763776 | tf_op jit(solution)/shard_map/all_gather | solution.py:47
  27.9 0.7 fusion.22
  28.6 0.1 copy.20
  28.7 16.1 %all_gather.6 = bf16[1,256,2]{2,1,0:T(8,128)(2,1)S(1)} all-gather(bf16[1,32,2]{2,1,0:T(8,128)(2,1)S(1)} %copy.20), channel_id=1, replica_groups=mesh['flop'=4,'turn'=4,'river'=2] {'turn','river'}, dimensions={1}, use_global_device_ids=true | all-gather | bytes 1152 | tf_op jit(solution)/shard_map/all_gather | solution.py:48
  44.7 1.3 gather_fusion.1
  46.0 0.9 gather_fusion
  46.9 0.0 copy-start.7
  46.9 0.0 copy-start.6
  46.9 0.0 copy-start.8
  46.9 0.0 copy-start.4
  46.9 0.0 copy-start.5
  47.0 2.1 %gather_fusion.4 = bf16[256,1326]{1,0:T(8,128)(2,1)} fusion(bf16[256,1326]{1,0:T(8,128)(2,1)S(1)} %bitcast.23, s32[1024]{0:T(1024)S(1)} %pad_clamp_fusion.1), kind=kCustom, calls=%fused_computation.4.clone | custom fusion | bytes 1358848 | tf_op jit(solution)/shard_map/jit(_take)/gather | solution.py:60
  49.1 0.9 gather_fusion.3
  49.9 1.4 scatter_custom_fusion
  51.4 1.4 scatter_custom_fusion.1
  52.8 0.0 copy-done.7
  52.8 0.1 compare_reduce_fusion.1
  52.9 0.0 copy-done.6
  52.9 0.1 select_convert_fusion.3
  53.0 0.2 slice_reduce_fusion.3
  53.2 0.0 copy-done.8
  53.2 0.6 fusion.34
  53.8 0.6 compare_select_fusion.7
  54.5 0.0 copy-done.4
  54.5 0.0 copy-done.5
  54.5 5.2 %convert_convert_fusion.1 = (bf16[1326,1326]{1,0:T(8,128)(2,1)S(1)}, bf16[1326,1326]{1,0:T(8,128)(2,1)}) fusion(pred[1326]{0:T(1024)(128)(4,1)S(1)} %get-tuple-element.11, s32[1326]{0:T(1024)S(1)} %copy-done.5, s32[1326]{0:T(1024)S(1)} %copy-done.4, pred[1326]{0:T(1024)(128)(4,1)S(1)} %get-tuple-element.12), kind=kLoop, calls=%fused_computation.10 | loop fusion | flops 26374140 | bytes 7046364 | tf_op jit(solution)/shard_map/convert.3
  59.7 8.7 %select_convert_fusion.1 = (bf16[1326,1326]{1,0:T(8,128)(2,1)S(1)}, bf16[1326,1326]{1,0:T(8,128)(2,1)}) fusion(s32[1326]{0:T(1024)S(1)} %get-tuple-element.9, pred[1326]{0:T(1024)(128)(4,1)S(1)} %get-tuple-element.11, s32[1326]{0:T(1024)S(1)} %copy-done.5, s32[1326]{0:T(1024)S(1)} %copy-done.4, s32[1326]{0:T(1024)S(1)} %get-tuple-element.10, ...), kind=kLoop, calls=%fused_computation.11 | loop fusion | flops 36923796 | bytes 7056972 | tf_op jit(solution)/shard_map/convert.2
  68.4 5.3 %fusion = f32[256,2652]{0,1:T(8,128)S(1)} fusion(bf16[1326,1326]{1,0:T(8,128)(2,1)S(1)} %get-tuple-element.15, bf16[1326,1326]{1,0:T(8,128)(2,1)S(1)} %get-tuple-element.13, bf16[256,1326]{1,0:T(8,128)(2,1)S(1)} %gather_fusion.1, pred[256]{0:T(512)(128)(4,1)S(1)} %compare_and_fusion.4), kind=kOutput, calls=%fused_computation.15 | convolution fusion | flops 1814880256 | bytes 10427920 | tf_op jit(solution)/shard_map/dot_general | solution.py:72
  73.8 0.3 fusion.11
  74.1 0.4 copy.23
  74.5 0.1 select_convert_fusion.2
  74.6 0.2 slice_reduce_fusion.1
  74.8 0.7 compare_select_fusion.6
  75.5 8.6 %fusion.4 = f32[256,2652]{0,1:T(8,128)S(1)} fusion(bf16[1326,1326]{1,0:T(8,128)(2,1)} %get-tuple-element.16, bf16[1326,1326]{1,0:T(8,128)(2,1)} %get-tuple-element.14, bf16[256,1326]{1,0:T(8,128)(2,1)} %gather_fusion.4, pred[256]{0:T(512)(128)(4,1)S(1)} %compare_and_fusion.2), kind=kOutput, calls=%fused_computation.19 | convolution fusion | flops 1814880256 | bytes 10427920 | tf_op jit(solution)/shard_map/dot_general | solution.py:72
  84.0 0.3 fusion.9
  84.3 1.6 copy.24
  85.9 0.0 copy-start.1
  85.9 0.1 concatenate.24.clone
  86.0 1.3 copy-done.1
  87.2 0.1 concatenate.26.clone
  87.3 0.2 pad_clamp_fusion
  87.6 2.3 %gather_fusion.2 = f32[256,1326]{1,0:T(8,128)} fusion(f32[257,1326]{1,0:T(8,128)S(1)} %concatenate.24.clone, s32[1024]{0:T(1024)S(1)} %pad_clamp_fusion.2), kind=kCustom, calls=%fused_computation.2.clone | custom fusion | bytes 2716672 | tf_op jit(solution)/shard_map/jit(_take)/gather | solution.py:88
  89.9 2.3 %gather_fusion.5 = f32[256,1326]{1,0:T(8,128)} fusion(f32[257,1326]{1,0:T(8,128)S(1)} %concatenate.26.clone, s32[1024]{0:T(1024)S(1)} %pad_clamp_fusion), kind=kCustom, calls=%fused_computation.5.clone | custom fusion | bytes 2716672 | tf_op jit(solution)/shard_map/jit(_take)/gather | solution.py:88
  92.2 0.0 copy-done
  92.2 2.8 %select_add_fusion = f32[256,1326]{1,0:T(8,128)} fusion(f32[256,1326]{1,0:T(8,128)} %gather_fusion.5, f32[256,1326]{1,0:T(8,128)S(1)} %copy-done, pred[256]{0:T(512)(128)(4,1)S(1)} %get-tuple-element.25, pred[256]{0:T(512)(128)(4,1)S(1)} %get-tuple-element.26), kind=kLoop, calls=%fused_computation.23 | loop fusion | flops 1018368 | bytes 4073984 | tf_op jit(solution)/shard_map/add | solution.py:88
  94.9 0.0 reduce-scatter.2.cloned.1.call-update
  95.0 0.0 copy-done.3
  95.0 0.1 max.15
  95.1 0.2 reduce_sum.18
  95.3 38.3 %reduce-scatter.2.cloned.1.call-done = f32[32,1326]{1,0:T(8,128)} async-done(((f32[256,1326]{1,0:T(8,128)}), f32[32,1326]{1,0:T(8,128)}) %reduce-scatter.2.cloned.1.call-update) | async-done | bytes 169744 | tf_op jit(solution)/shard_map/reduce_scatter | solution.py:89
  133.6 1.0 reshape.180
  134.7 0.3 fusion.20
  135.0 0.0 copy-start.2
  135.0 0.1 sub.49
  135.1 0.0 all-reduce.4.cloned.1.call-start
  135.1 0.1 sub.50
  135.3 0.4 copy-done.2
  135.6 0.2 all-reduce.4.cloned.1.call-update
  135.8 1.6 fusion.19
  137.5 35.4 %all-reduce.4.cloned.1.call-done = f32[16,1326]{1,0:T(8,128)} async-done(((f32[16,1326]{1,0:T(8,128)}), f32[16,1326]{1,0:T(8,128)}) %all-reduce.4.cloned.1.call-update) | async-done | bytes 84880 | tf_op jit(solution)/shard_map/psum | solution.py:109
  172.9 1.5 broadcast_multiply_fusion
  (18 shorter events, 0.1 us)
Async XLA Ops:
  7.2 126.5 %reduce-scatter.2.cloned.1.call-start = ((), (), s32[]{:S(2)}) async-start(), calls=%async_computation.1 | async-start | bytes 1622016 | tf_op jit(solution)/shard_map/reduce_scatter | solution.py:89
  46.9 5.9 %copy-start.7 = (s32[1,1,2,1326]{3,2,1,0:T(2,128)S(1)}, s32[1,1,2,1326]{3,2,1,0:T(2,128)}, u32[]{:S(2)}) copy-start(s32[1,1,2,1326]{3,2,1,0:T(2,128)} %param.23) | copy-start | bytes 31828
  46.9 6.0 %copy-start.6 = (s32[1,1,2,1326]{3,2,1,0:T(2,128)S(1)}, s32[1,1,2,1326]{3,2,1,0:T(2,128)}, u32[]{:S(2)}) copy-start(s32[1,1,2,1326]{3,2,1,0:T(2,128)} %param.22) | copy-start | bytes 31828
  46.9 6.3 %copy-start.8 = (s32[1,1,2]{2,1,0:T(1,128)S(1)}, s32[1,1,2]{2,1,0:T(1,128)}, u32[]{:S(2)}) copy-start(s32[1,1,2]{2,1,0:T(1,128)} %param.21) | copy-start | bytes 28
  46.9 7.5 %copy-start.4 = (s32[1326]{0:T(1024)S(1)}, s32[1326]{0:T(1024)}, u32[]{:S(2)}) copy-start(s32[1326]{0:T(1024)} %constant.44.clone) | copy-start | bytes 15916
  46.9 7.5 %copy-start.5 = (s32[1326]{0:T(1024)S(1)}, s32[1326]{0:T(1024)}, u32[]{:S(2)}) copy-start(s32[1326]{0:T(1024)} %constant.45.clone) | copy-start | bytes 15916
  85.9 1.4 copy-start.1
  89.9 2.3 %copy-start = (f32[256,1326]{1,0:T(8,128)S(1)}, f32[256,1326]{1,0:T(8,128)}, u32[]{:S(2)}) copy-start(f32[256,1326]{1,0:T(8,128)} %gather_fusion.2) | copy-start | bytes 4073476
  92.2 2.8 %copy-start.3 = (f32[1,32,1326]{2,1,0:T(8,128)S(1)}, f32[1,32,1326]{2,1,0:T(8,128)}, u32[]{:S(2)}) copy-start(f32[1,32,1326]{2,1,0:T(8,128)} %param.16) | copy-start | bytes 509188
  135.0 0.6 copy-start.2
  135.1 37.8 %all-reduce.4.cloned.1.call-start = ((), (), s32[]{:S(2)}) async-start(), calls=%async_computation.2 | async-start | bytes 180224 | tf_op jit(solution)/shard_map/psum | solution.py:109
Sparse Core Ops, SparseCore 0:
  95.1 38.5 reduce-scatter.1
  138.9 33.9 all-reduce.3
where the time goes:
time: 182 us; the launch traced here: 181 us
  waiting for transfers between devices  73.9 us (41%)
  blocking collectives  35.2 us (19%)
  other arithmetic  24.3 us (13%)
  local copies, waits for them, and re-layouts  19.6 us (11%)
  between operations  14.4 us (8%)
  matrix products  13.9 us (8%)
    reduce_scatter x1, waiting for transfers between devices, on_device(): lax.psum_scatter(lax.slice_in_dim(line_table, 0, regrets.shape[1] * lax.a...  38.3 us
    psum x1, waiting for transfers between devices, on_device(): chance_values = lax.psum(node_values, 'flop') / lax.axis_size('flop')  35.4 us
    all_gather x1, blocking collectives, on_device(): lax.all_gather(opp_reach, ('turn', 'river'), axis=1, tiled=True)  19.1 us
    all_gather x1, blocking collectives, on_device(): lax.all_gather(line_coef, ('turn', 'river'), axis=1, tiled=True)  16.1 us
    another operation x2, other arithmetic  14 us
    dot_general x2, matrix products, evaluate(): products = jnp.dot(slot_reach, matrix, preferred_element_type=jnp.float32)  13.9 us
    gather x2, local copies, waits for them, and re-layouts, on_device(): line_table = line_table + jnp.take(padded_values, position, axis=0)  4.59 us
    unnamed x20, local copies, waits for them, and re-layouts  3.67 us
  transfers between devices with their start and end apart: 2, of which 2 were waited for; matrix products, arithmetic and copies ran while one was open for 1% of the time, Pallas kernels for 0%

commit v1 on v0

v1 whole, which is shorter than its diff:
```python
import functools

import jax
import jax.numpy as jnp
import numpy as np
from jax import lax
from jax.experimental import pallas as pl
from jax.experimental.pallas import tpu as pltpu
from jax.sharding import PartitionSpec as P

CARDS = 52
ACTS = 2
LANE = 128
SUB = 16
RANK_SPAN = 8192
ROW_TILE = 128
COL_TILE = 512

floor_share = 0.1


def up(value, unit):
    return -(-value // unit) * unit


def tiles(total, size):
    return [(first, min(size, total - first)) for first in range(0, total, size)]


@functools.cache
def tables(hand_count):
    wide, deep = up(hand_count, LANE), up(hand_count, SUB)
    first, second = np.triu_indices(CARDS, 1)
    cards = np.zeros((hand_count, CARDS), np.float32)
    cards[np.arange(hand_count), first] = 1
    cards[np.arange(hand_count), second] = 1
    apart = np.zeros((deep, wide), np.float32)
    apart[:hand_count, :hand_count] = (cards @ cards.T) == 0
    sums = np.concatenate([np.ones((hand_count, 1), np.float32), cards], axis=1)
    parts = sums.shape[1]
    collect = np.zeros((wide, LANE), np.float32)
    spread = np.zeros((LANE, wide), np.float32)
    signed = sums.copy()
    signed[:, 1:] *= -1
    for copy in range(2):
        collect[:hand_count, copy * parts : (copy + 1) * parts] = sums
        spread[copy * parts : (copy + 1) * parts, :hand_count] = signed.T
    dtype = jnp.bfloat16
    return apart.astype(dtype), (-apart).astype(dtype), collect.astype(dtype), spread.astype(dtype)


def boards_kernel(hand_count, line_count, base_ref, own_ref, mate_ref, *refs, boards_in):
    board_refs, refs = refs[:boards_in], refs[boards_in:]
    apart_ref, minus_ref, collect_ref, spread_ref, own_out, mate_out, column_ref, board_ref = refs
    wide = up(hand_count, LANE)
    deep = apart_ref.shape[0]
    rows = own_ref.shape[0]
    parts = 1 + CARDS
    reach = jnp.concatenate([own_ref[...], mate_ref[...]], axis=0)
    kind = reach[:, hand_count : hand_count + 1].astype(jnp.float32)
    row = lax.broadcasted_iota(jnp.int32, (2 * rows, 1), 0)
    within = jnp.where(row < rows, row, row - rows)
    line = jnp.where(row < rows, base_ref[0], base_ref[1]) + within
    line = jnp.where(within < line_count, line, -2)
    lane = lax.broadcasted_iota(jnp.int32, (2 * rows, LANE), 1)
    own_out[...] = jnp.zeros_like(own_out)
    mate_out[...] = jnp.zeros_like(mate_out)

    first = 0
    for ref in board_refs:
        board_ref[first : first + ref.shape[0]] = ref[...]
        first += ref.shape[0]

    @pl.loop(0, first)
    def add_board(board):
        keys = board_ref[pl.ds(board, 1), :wide]
        slots = board_ref[pl.ds(board, 1), wide:]
        ranks = (keys & (RANK_SPAN - 1)).astype(jnp.float32)
        live = (keys >> (RANK_SPAN.bit_length() - 1)).astype(jnp.float32)
        keep = jnp.max(jnp.where(slots == line, 1.0, 0.0), axis=1, keepdims=True)
        show_keep = jnp.where(kind == 0, keep, 0.0).astype(jnp.bfloat16)
        fold_keep = jnp.where(kind == 0, 0.0, keep).astype(jnp.bfloat16)
        held = reach * live.astype(jnp.bfloat16)
        show_reach = held * show_keep
        fold_reach = held * fold_keep
        sums = jnp.dot(fold_reach, collect_ref[...], preferred_element_type=jnp.float32)
        high = sums.astype(jnp.bfloat16)
        low = (sums - high.astype(jnp.float32)).astype(jnp.bfloat16)
        sums = jnp.where(lane < parts, high.astype(jnp.float32), low.astype(jnp.float32)).astype(jnp.bfloat16)
        column_ref[...] = jnp.transpose(jnp.broadcast_to(ranks, (LANE, wide)))[:deep]
        for first, count in tiles(wide, COL_TILE):
            at = slice(first, first + count)
            total = jnp.dot(sums, spread_ref[:, at], preferred_element_type=jnp.float32)
            for top, height in tiles(deep, ROW_TILE):
                down = slice(top, top + height)
                column = jnp.concatenate([column_ref[down]] * (count // LANE), axis=1)
                order = (ranks[:, at] - column).astype(jnp.bfloat16)
                matrix = jnp.minimum(jnp.maximum(order, minus_ref[down, at]), apart_ref[down, at])
                total += jnp.dot(show_reach[:, down], matrix, preferred_element_type=jnp.float32)
            total = (total + fold_reach[:, at].astype(jnp.float32)) * live[:, at]
            own_out[:, at] += total[:rows]
            mate_out[:, at] += total[rows:]


def board_sums(hand_count, line_count, base, own, mate, boards):
    rows, wide = own.shape
    consts = [jnp.asarray(table) for table in tables(hand_count)]
    whole = pl.BlockSpec(memory_space=pltpu.VMEM)
    out = jax.ShapeDtypeStruct((rows, wide), jnp.float32)
    return pl.pallas_call(
        functools.partial(boards_kernel, hand_count, line_count, boards_in=len(boards)),
        out_shape=(out, out),
        in_specs=[pl.BlockSpec(memory_space=pltpu.SMEM)] + [whole] * (2 + len(boards) + len(consts)),
        out_specs=(whole, whole),
        scratch_shapes=[
            pltpu.VMEM((consts[0].shape[0], LANE), jnp.float32),
            pltpu.VMEM((sum(board.shape[0] for board in boards), boards[0].shape[1]), jnp.int32),
        ],
        compiler_params=pltpu.CompilerParams(vmem_limit_bytes=40 << 20),
        name="board_sums",
    )(base, own, mate, *boards, *consts)


def update_kernel(hand_count, scale, own_ref, mate_ref, reach_ref, regret_ref, regret_out, node_out, node_ref):
    coef = reach_ref[:, hand_count + 1 : hand_count + 2].astype(jnp.float32) * scale
    values = (own_ref[:, :hand_count] + mate_ref[:, :hand_count]) * coef
    regrets = regret_ref[...]
    rows = regrets.shape[0]
    even = lax.broadcasted_iota(jnp.int32, (rows, 1), 0) % ACTS == 0

    def both(array):
        other = jnp.where(even, pltpu.roll(array, rows - 1, 0), pltpu.roll(array, 1, 0))
        return array + other

    positive = jnp.maximum(regrets, 0.0)
    strategy = (positive + floor_share) / (both(positive) + ACTS * floor_share)
    node = both(strategy * values)
    regret_out[...] = jnp.maximum(regrets + values - node, 0.0)
    for tile, (first, count) in enumerate(tiles(hand_count, LANE)):
        node_ref[tile, :, :count] = node[:, first : first + count]
        picked = node_ref[tile, pl.ds(0, rows // ACTS, stride=ACTS), :]
        node_out[:, first : first + count] = picked[:, :count]


def update(hand_count, scale, own, mate, reach, regrets):
    rows = regrets.shape[0]
    whole = pl.BlockSpec(memory_space=pltpu.VMEM)
    return pl.pallas_call(
        functools.partial(update_kernel, hand_count, scale),
        out_shape=(
            jax.ShapeDtypeStruct((rows, hand_count), jnp.float32),
            jax.ShapeDtypeStruct((rows // ACTS, hand_count), jnp.float32),
        ),
        in_specs=[whole] * 4,
        out_specs=(whole, whole),
        scratch_shapes=[pltpu.VMEM((-(-hand_count // LANE), rows, LANE), jnp.float32)],
        name="regret_update",
    )(own, mate, reach, regrets)


def swap(array, axes, mask):
    return lax.ppermute(array, axes, [(index, index ^ mask) for index in range(lax.axis_size(axes))])


def on_device(
    regrets, opp_reach, pot_size, line_kind, board_lines, board_count, hand_ranks, live_hands
):
    hand_count = opp_reach.shape[2]
    line_count = opp_reach.shape[1]
    group = ("turn", "river")
    group_size = lax.axis_size(group)
    core = lax.axis_size("river")
    board_total = group_size * board_lines.shape[2]
    rows, wide = up(line_count, SUB), up(hand_count, LANE)

    keys = hand_ranks[0, 0] + RANK_SPAN * live_hands[0, 0]
    slot = lax.broadcasted_iota(jnp.int32, board_lines.shape[2:], 1)
    slots = jnp.where(slot < board_count[0, 0][:, None], board_lines[0, 0], -1)
    boards = jnp.concatenate([jnp.pad(keys, ((0, 0), (0, wide - hand_count))), slots], axis=1)
    coef = jnp.where(line_kind == 1, -pot_size, pot_size)
    terms = jnp.concatenate([line_kind, coef], axis=0).astype(jnp.bfloat16).T
    reach = jnp.concatenate([opp_reach[0], terms], axis=1)
    reach = jnp.pad(reach, ((0, rows - line_count), (0, wide - reach.shape[1])))

    mate_reach = swap(reach, group, core)
    masks = [mask for mask in range(1, group_size) if not mask & core]
    if len(masks) < 4:
        boards = [boards] + [swap(boards, group, mask) for mask in masks]
    else:
        for mask in masks:
            if mask & (mask - 1) == 0:
                boards = jnp.concatenate([boards, swap(boards, group, mask)], axis=0)
        boards = [boards]
    index = lax.axis_index(group)
    base = jnp.stack([index, index ^ core]).astype(jnp.int32) * line_count
    own, for_mate = board_sums(hand_count, line_count, base, reach, mate_reach, boards)
    mate = swap(for_mate, group, core)
    held = jnp.pad(regrets[0], ((0, rows - line_count), (0, 0)))
    updated, node = update(hand_count, 1.0 / (board_total * hand_count), own, mate, reach, held)
    updated, node = updated[:line_count], node[: line_count // ACTS]
    flops = lax.axis_size("flop")
    total = node + swap(node, "flop", 1)
    for mask in range(2, flops, 2):
        total += swap(node, "flop", mask) + swap(node, "flop", mask + 1)
    return (updated[None], total / flops)


def solution(mesh):
    placed = (
        P("flop", ("turn", "river"), None),
        P("flop", ("turn", "river"), None),
        P("flop", ("turn", "river")),
        P("flop", ("turn", "river")),
        P("flop", "turn", "river", None),
        P("flop", "turn", "river"),
        P("flop", "turn", "river", None),
        P("flop", "turn", "river", None),
    )
    return jax.shard_map(
        on_device,
        mesh=mesh,
        in_specs=placed,
        out_specs=(P("flop", ("turn", "river"), None), P(("turn", "river"), None)),
        check_vma=False,
    )
```

time: 182 us -> 47 us (0.26)
  waiting for transfers between devices: 73.9 us -> 10.3 us
  blocking collectives: 35.2 us -> 0 us
  other arithmetic: 24.3 us -> 4.85 us
  Pallas kernels: 0 us -> 14.1 us
  matrix products: 13.9 us -> 0 us
  between operations: 14.4 us -> 0.69 us
  local copies, waits for them, and re-layouts: 19.6 us -> 7.53 us
  starting transfers between devices: 0.08 us -> 9.02 us
    reduce_scatter x1 -> x0, waiting for transfers between devices: 38.3 us -> none  [on_device(): lax.psum_scatter(lax.slice_in_dim(line_table, 0, regrets.shape[1] * lax.a...]
    psum x1 -> x0, waiting for transfers between devices: 35.4 us -> none  [on_device(): chance_values = lax.psum(node_values, 'flop') / lax.axis_size('flop')]
    all_gather x2 -> x0, blocking collectives: 35.2 us -> none  [the longest x1 19.1 us: on_device(): lax.all_gather(opp_reach, ('turn', 'river'), axis=1, tiled=True)]
    pallas_call x0 -> x2, Pallas kernels: none -> 14.1 us  [the longest x1 12 us: board_sums(): pl.pallas_call(functools.partial(boards_kernel, hand_count, line_count, b...]
    another operation x4 -> x1, other arithmetic: 14.6 us -> 0.74 us
    dot_general x2 -> x0, matrix products: 13.9 us -> none  [evaluate(): products = jnp.dot(slot_reach, matrix, preferred_element_type=jnp.float32)]
    ppermute x0 -> x8, waiting for transfers between devices: none -> 10.3 us  [swap(): lax.ppermute(array, axes, [(index, index ^ mask) for index in range(lax.a...]
    gather x6 -> x0, local copies, waits for them, and re-layouts: 9.72 us -> none  [the longest x2 4.59 us: on_device(): line_table = line_table + jnp.take(padded_values, position, axis=0)]
  transfers between devices with their start and end apart: 2 -> 8, of which waited for: 2 -> 5; matrix products, arithmetic and copies ran while one was open for 1% -> 4% of each run, Pallas kernels for 0% -> 0%
where the time goes in v1:
time: 47 us; the launch traced here: 46.5 us
  Pallas kernels  14.1 us (30%)
  waiting for transfers between devices  10.3 us (22%)
  starting transfers between devices  9.02 us (19%)
  local copies, waits for them, and re-layouts  7.53 us (16%)
  other arithmetic  4.85 us (10%)
  between operations  0.69 us (1%)
    pallas_call x1, Pallas kernels, board_sums(): pl.pallas_call(functools.partial(boards_kernel, hand_count, line_count, b...  12 us
    ppermute x8, waiting for transfers between devices, swap(): lax.ppermute(array, axes, [(index, index ^ mask) for index in range(lax.a...  10.3 us
    ppermute x8, starting transfers between devices, swap(): lax.ppermute(array, axes, [(index, index ^ mask) for index in range(lax.a...  9.02 us
    unnamed x14, local copies, waits for them, and re-layouts  7.43 us
    pallas_call x1, Pallas kernels, update(): pl.pallas_call(functools.partial(update_kernel, hand_count, scale), out_s...  2.04 us
    div x1, other arithmetic, on_device(): return (updated[None], total / flops)  1.56 us
    concatenate x1, other arithmetic, on_device(): reach = jnp.concatenate([opp_reach[0], terms], axis=1)  0.97 us
  transfers between devices with their start and end apart: 8, of which 5 were waited for; matrix products, arithmetic and copies ran while one was open for 4% of the time, Pallas kernels for 0%

profile of v1, /device:TPU:0, one launch (start us, length us, event | category | flops | bytes accessed | tf_op | source)
XLA Modules:
  0.0 46.5 jit_solution(11892097771739222277)
XLA Ops:
  0.6 0.8 %compare_select_fusion = s32[2,256]{1,0:T(2,128)S(1)} fusion(s32[1,1,2,256]{3,2,1,0:T(2,128)} %param.16, s32[2]{0:T(128)} %bitcast.14), kind=kLoop, calls=%fused_computation.7 | loop fusion | flops 1024 | bytes 4104 | tf_op jit(solution)/shard_map/jit(_where)/select_n | solution.py:178
  1.4 0.7 %add_bitcast_fusion = s32[2,1326]{1,0:T(2,128)S(1)} fusion(s32[1,1,2,1326]{3,2,1,0:T(2,128)} %param.18, s32[1,1,2,1326]{3,2,1,0:T(2,128)} %param.19), kind=kLoop, calls=%fused_computation.6 | loop fusion | flops 5304 | bytes 31824 | tf_op jit(solution)/shard_map/add | solution.py:176
  2.1 4.0 %collective-permute-start.3 = (s32[2,1664]{1,0:T(2,128)S(1)}, s32[2,1664]{1,0:T(2,128)S(1)}, u32[]{:S(2)}, u32[]{:S(2)}) collective-permute-start(s32[2,1664]{1,0:T(2,128)S(1)} %pad_add_fusion.refs_0_), channel_id=1, source_target_pairs={{0,5},{1,4},{2,7},{3,6},{4,1},{5,0},{6,3},{7,2},{8,13},{9,12},{10,... | collective-permute-start | bytes 39944 | tf_op jit(solution)/shard_map/ppermute | solution.py:162
  6.1 0.5 %collective-permute-start.2 = (s32[2,1664]{1,0:T(2,128)S(1)}, s32[2,1664]{1,0:T(2,128)S(1)}, u32[]{:S(2)}, u32[]{:S(2)}) collective-permute-start(s32[2,1664]{1,0:T(2,128)S(1)} %pad_add_fusion.refs_0_), channel_id=1, source_target_pairs={{0,4},{1,5},{2,6},{3,7},{4,0},{5,1},{6,2},{7,3},{8,12},{9,13},{10,... | collective-permute-start | bytes 39944 | tf_op jit(solution)/shard_map/ppermute | solution.py:162
  6.6 0.1 collective-permute-start.1
  6.7 0.7 %fusion.4 = (bf16[1,32]{1,0:T(2,128)(2,1)S(1)}, bf16[1,32]{1,0:T(2,128)(2,1)S(1)}) fusion(s32[1,32]{1,0:T(1,128)} %param.15, s32[1,32]{1,0:T(1,128)} %param.14), kind=kLoop, calls=%fused_computation.12 | loop fusion | flops 160 | bytes 384 | tf_op jit(solution)/shard_map/convert
  7.5 0.1 copy.19
  7.6 1.0 %fusion.2.own_ref.reach_ref = bf16[32,1408]{1,0:T(8,128)(2,1)S(1)} fusion(bf16[32,2]{1,0:T(8,128)(2,1)S(1)} %bitcast.13, bf16[32,1326]{1,0:T(8,128)(2,1)} %bitcast.12), kind=kLoop, calls=%fused_computation.3 | loop fusion | flops 315392 | bytes 175104 | tf_op jit(solution)/shard_map/concatenate | solution.py:182
  8.6 0.0 copy-start.2
  8.6 0.0 collective-permute-start
  8.6 0.1 add_multiply_fusion.1.base_ref
  8.7 0.0 collective-permute-done.3.refs_3_
  8.7 1.1 %collective-permute-done.2.refs_2_ = s32[2,1664]{1,0:T(2,128)S(1)} collective-permute-done((s32[2,1664]{1,0:T(2,128)S(1)}, s32[2,1664]{1,0:T(2,128)S(1)}, u32[]{:S(2)}, u32[]{:S(2)}) %collective-permute-start.2) | collective-permute-done | bytes 13344 | tf_op jit(solution)/shard_map/ppermute | solution.py:162
  9.8 0.5 %collective-permute-done.1.refs_1_ = s32[2,1664]{1,0:T(2,128)S(1)} collective-permute-done((s32[2,1664]{1,0:T(2,128)S(1)}, s32[2,1664]{1,0:T(2,128)S(1)}, u32[]{:S(2)}, u32[]{:S(2)}) %collective-permute-start.1) | collective-permute-done | bytes 13344 | tf_op jit(solution)/shard_map/ppermute | solution.py:162
  10.3 0.0 collective-permute-done.mate_ref
  10.3 0.0 copy-start
  10.3 2.1 %copy-done = bf16[1328,1408]{1,0:T(8,128)(2,1)S(1)} copy-done((bf16[1328,1408]{1,0:T(8,128)(2,1)S(1)}, bf16[1328,1408]{1,0:T(8,128)(2,1)}, u32[]{:S(2)}) %copy-start) | copy-done | bytes 3739672
  12.4 0.0 copy-start.1
  12.4 2.1 %copy-done.1 = bf16[1328,1408]{1,0:T(8,128)(2,1)S(1)} copy-done((bf16[1328,1408]{1,0:T(8,128)(2,1)S(1)}, bf16[1328,1408]{1,0:T(8,128)(2,1)}, u32[]{:S(2)}) %copy-start.1) | copy-done | bytes 3739672
  14.4 0.0 copy-start.3
  14.4 1.0 %copy-done.3 = bf16[128,1408]{1,0:T(8,128)(2,1)S(1)} copy-done((bf16[128,1408]{1,0:T(8,128)(2,1)S(1)}, bf16[128,1408]{1,0:T(8,128)(2,1)}, u32[]{:S(2)}) %copy-start.3) | copy-done | bytes 360472
  15.4 0.0 copy-start.4
  15.4 1.0 %copy-done.4 = bf16[1408,128]{1,0:T(8,128)(2,1)S(1)} copy-done((bf16[1408,128]{1,0:T(8,128)(2,1)S(1)}, bf16[1408,128]{1,0:T(8,128)(2,1)}, u32[]{:S(2)}) %copy-start.4) | copy-done | bytes 360472
  16.4 12.0 %board_sums.1 = (f32[32,1408]{1,0:T(8,128)S(1)}, f32[32,1408]{1,0:T(8,128)S(1)}) custom-call(s32[2]{0:T(128)S(1)} %add_multiply_fusion.1.base_ref, bf16[32,1408]{1,0:T(8,128)(2,1)S(1)} %fusion.2.own_ref.reach_ref, bf16[32,1408]{1,0:T(8,128)(2,1)S(1)} %collective-permute-done.mate_ref, s32[2,1664]{1,0:T(2,128)S(1)} %pad_add_fusion.refs_0_, ...), custom_call_target="tpu_custom_call" | custom-call | tf_op jit(solution)/shard_map/board_sums/pallas_call | solution.py:110
  28.4 0.0 copy-done.2
  28.5 0.0 copy-start.5
  28.5 0.7 %copy-done.5 = f32[32,1408]{1,0:T(8,128)} copy-done((f32[32,1408]{1,0:T(8,128)}, f32[32,1408]{1,0:T(8,128)S(1)}, u32[]{:S(2)}) %copy-start.5) | copy-done | bytes 180248
  29.1 0.0 collective-permute-start.4
  29.1 1.4 %collective-permute-done.4.mate_ref = f32[32,1408]{1,0:T(8,128)S(1)} collective-permute-done((f32[32,1408]{1,0:T(8,128)S(1)}, f32[32,1408]{1,0:T(8,128)S(1)}, u32[]{:S(2)}, u32[]{:S(2)}) %collective-permute-start.4) | collective-permute-done | bytes 180256 | tf_op jit(solution)/shard_map/ppermute | solution.py:162
  30.5 0.0 copy-start.6
  30.5 0.7 %copy-done.6 = f32[32,1408]{1,0:T(8,128)} copy-done((f32[32,1408]{1,0:T(8,128)}, f32[32,1408]{1,0:T(8,128)S(1)}, u32[]{:S(2)}) %copy-start.6) | copy-done | bytes 180248
  31.2 2.0 %regret_update.1 = (f32[32,1326]{1,0:T(8,128)}, f32[16,1326]{1,0:T(8,128)}) custom-call(f32[32,1408]{1,0:T(8,128)} %copy-done.5, f32[32,1408]{1,0:T(8,128)} %copy-done.6, bf16[32,1408]{1,0:T(8,128)(2,1)} %copy-done.2, f32[32,1326]{1,0:T(8,128)} %bitcast.11), custom_call_target="tpu_custom_call" | custom-call | tf_op jit(solution)/shard_map/regret_update/pallas_call | solution.py:148
  33.3 3.6 %collective-permute-start.7 = (f32[16,1326]{1,0:T(8,128)}, f32[16,1326]{1,0:T(8,128)S(1)}, u32[]{:S(2)}, u32[]{:S(2)}) collective-permute-start(f32[16,1326]{1,0:T(8,128)} %get-tuple-element.9), channel_id=1, source_target_pairs={{0,24},{8,16},{16,8},{24,0},{1,25},{9,17},{17,9},{25,1},{2,26},{10... | collective-permute-start | bytes 254600 | tf_op jit(solution)/shard_map/ppermute | solution.py:162
  36.9 0.0 collective-permute-start.6
  36.9 0.8 %collective-permute-start.5 = (f32[16,1326]{1,0:T(8,128)}, f32[16,1326]{1,0:T(8,128)S(1)}, u32[]{:S(2)}, u32[]{:S(2)}) collective-permute-start(f32[16,1326]{1,0:T(8,128)} %get-tuple-element.9), channel_id=1, source_target_pairs={{0,8},{8,0},{16,24},{24,16},{1,9},{9,1},{17,25},{25,17},{2,10},{10... | collective-permute-start | bytes 254600 | tf_op jit(solution)/shard_map/ppermute | solution.py:162
  37.6 3.1 %collective-permute-done.7 = f32[16,1326]{1,0:T(8,128)S(1)} collective-permute-done((f32[16,1326]{1,0:T(8,128)}, f32[16,1326]{1,0:T(8,128)S(1)}, u32[]{:S(2)}, u32[]{:S(2)}) %collective-permute-start.7) | collective-permute-done | bytes 84896 | tf_op jit(solution)/shard_map/ppermute | solution.py:162
  40.7 4.2 %collective-permute-done.6 = f32[16,1326]{1,0:T(8,128)S(1)} collective-permute-done((f32[16,1326]{1,0:T(8,128)}, f32[16,1326]{1,0:T(8,128)S(1)}, u32[]{:S(2)}, u32[]{:S(2)}) %collective-permute-start.6) | collective-permute-done | bytes 84896 | tf_op jit(solution)/shard_map/ppermute | solution.py:162
  45.0 0.0 collective-permute-done.5
  45.0 1.6 %add_multiply_fusion = f32[16,1326]{1,0:T(8,128)} fusion(f32[16,1326]{1,0:T(8,128)S(1)} %collective-permute-done.6, f32[16,1326]{1,0:T(8,128)S(1)} %collective-permute-done.7, f32[16,1326]{1,0:T(8,128)} %get-tuple-element.9, f32[16,1326]{1,0:T(8,128)S(1)} %collective-permute-done.5), kind=kLoop, calls=%fused_computation.4 | loop fusion | flops 84864 | bytes 424320 | tf_op jit(solution)/shard_map/div | solution.py:205
  (2 shorter events, 0.0 us)
Async XLA Ops:
  2.1 6.6 %collective-permute-start.3 = (s32[2,1664]{1,0:T(2,128)S(1)}, s32[2,1664]{1,0:T(2,128)S(1)}, u32[]{:S(2)}, u32[]{:S(2)}) collective-permute-start(s32[2,1664]{1,0:T(2,128)S(1)} %pad_add_fusion.refs_0_), channel_id=1, source_target_pairs={{0,5},{1,4},{2,7},{3,6},{4,1},{5,0},{6,3},{7,2},{8,13},{9,12},{10,... | collective-permute-start | bytes 39944 | tf_op jit(solution)/shard_map/ppermute | solution.py:162
  6.1 3.7 %collective-permute-start.2 = (s32[2,1664]{1,0:T(2,128)S(1)}, s32[2,1664]{1,0:T(2,128)S(1)}, u32[]{:S(2)}, u32[]{:S(2)}) collective-permute-start(s32[2,1664]{1,0:T(2,128)S(1)} %pad_add_fusion.refs_0_), channel_id=1, source_target_pairs={{0,4},{1,5},{2,6},{3,7},{4,0},{5,1},{6,2},{7,3},{8,12},{9,13},{10,... | collective-permute-start | bytes 39944 | tf_op jit(solution)/shard_map/ppermute | solution.py:162
  6.6 3.7 %collective-permute-start.1 = (s32[2,1664]{1,0:T(2,128)S(1)}, s32[2,1664]{1,0:T(2,128)S(1)}, u32[]{:S(2)}, u32[]{:S(2)}) collective-permute-start(s32[2,1664]{1,0:T(2,128)S(1)} %pad_add_fusion.refs_0_), channel_id=1, source_target_pairs={{0,1},{1,0},{2,3},{3,2},{4,5},{5,4},{6,7},{7,6},{8,9},{9,8},{10,11... | collective-permute-start | bytes 39944 | tf_op jit(solution)/shard_map/ppermute | solution.py:162
  8.6 19.9 %copy-start.2 = (bf16[32,1408]{1,0:T(8,128)(2,1)}, bf16[32,1408]{1,0:T(8,128)(2,1)S(1)}, u32[]{:S(2)}) copy-start(bf16[32,1408]{1,0:T(8,128)(2,1)S(1)} %fusion.2.own_ref.reach_ref) | copy-start | bytes 270340
  8.6 1.7 %collective-permute-start = (bf16[32,1408]{1,0:T(8,128)(2,1)S(1)}, bf16[32,1408]{1,0:T(8,128)(2,1)S(1)}, u32[]{:S(2)}, u32[]{:S(2)}) collective-permute-start(bf16[32,1408]{1,0:T(8,128)(2,1)S(1)} %fusion.2.own_ref.reach_ref), channel_id=1, source_target_pairs={{0,2},{1,3},{2,0},{3,1},{4,6},{5,7},{6,4},{7,5},{8,10},{9,11},{10,... | collective-permute-start | bytes 270344 | tf_op jit(solution)/shard_map/ppermute | solution.py:162
  10.3 2.1 %copy-start = (bf16[1328,1408]{1,0:T(8,128)(2,1)S(1)}, bf16[1328,1408]{1,0:T(8,128)(2,1)}, u32[]{:S(2)}) copy-start(bf16[1328,1408]{1,0:T(8,128)(2,1)} %constant.34.clone.refs_5_) | copy-start | bytes 11218948
  12.4 2.1 %copy-start.1 = (bf16[1328,1408]{1,0:T(8,128)(2,1)S(1)}, bf16[1328,1408]{1,0:T(8,128)(2,1)}, u32[]{:S(2)}) copy-start(bf16[1328,1408]{1,0:T(8,128)(2,1)} %constant.33.clone.refs_4_) | copy-start | bytes 11218948
  14.4 1.0 %copy-start.3 = (bf16[128,1408]{1,0:T(8,128)(2,1)S(1)}, bf16[128,1408]{1,0:T(8,128)(2,1)}, u32[]{:S(2)}) copy-start(bf16[128,1408]{1,0:T(8,128)(2,1)} %constant.36.clone.refs_7_) | copy-start | bytes 1081348
  15.4 1.0 %copy-start.4 = (bf16[1408,128]{1,0:T(8,128)(2,1)S(1)}, bf16[1408,128]{1,0:T(8,128)(2,1)}, u32[]{:S(2)}) copy-start(bf16[1408,128]{1,0:T(8,128)(2,1)} %constant.35.clone.refs_6_) | copy-start | bytes 1081348
  28.5 0.7 %copy-start.5 = (f32[32,1408]{1,0:T(8,128)}, f32[32,1408]{1,0:T(8,128)S(1)}, u32[]{:S(2)}) copy-start(f32[32,1408]{1,0:T(8,128)S(1)} %get-tuple-element.6.own_ref) | copy-start | bytes 540676
  29.1 1.4 %collective-permute-start.4 = (f32[32,1408]{1,0:T(8,128)S(1)}, f32[32,1408]{1,0:T(8,128)S(1)}, u32[]{:S(2)}, u32[]{:S(2)}) collective-permute-start(f32[32,1408]{1,0:T(8,128)S(1)} %get-tuple-element.7), channel_id=1, source_target_pairs={{0,2},{1,3},{2,0},{3,1},{4,6},{5,7},{6,4},{7,5},{8,10},{9,11},{10,... | collective-permute-start | bytes 540680 | tf_op jit(solution)/shard_map/ppermute | solution.py:162
  30.5 0.7 %copy-start.6 = (f32[32,1408]{1,0:T(8,128)}, f32[32,1408]{1,0:T(8,128)S(1)}, u32[]{:S(2)}) copy-start(f32[32,1408]{1,0:T(8,128)S(1)} %collective-permute-done.4.mate_ref) | copy-start | bytes 540676
  33.3 7.5 %collective-permute-start.7 = (f32[16,1326]{1,0:T(8,128)}, f32[16,1326]{1,0:T(8,128)S(1)}, u32[]{:S(2)}, u32[]{:S(2)}) collective-permute-start(f32[16,1326]{1,0:T(8,128)} %get-tuple-element.9), channel_id=1, source_target_pairs={{0,24},{8,16},{16,8},{24,0},{1,25},{9,17},{17,9},{25,1},{2,26},{10... | collective-permute-start | bytes 254600 | tf_op jit(solution)/shard_map/ppermute | solution.py:162
  36.9 8.1 %collective-permute-start.6 = (f32[16,1326]{1,0:T(8,128)}, f32[16,1326]{1,0:T(8,128)S(1)}, u32[]{:S(2)}, u32[]{:S(2)}) collective-permute-start(f32[16,1326]{1,0:T(8,128)} %get-tuple-element.9), channel_id=1, source_target_pairs={{0,16},{8,24},{16,0},{24,8},{1,17},{9,25},{17,1},{25,9},{2,18},{10... | collective-permute-start | bytes 254600 | tf_op jit(solution)/shard_map/ppermute | solution.py:162
  36.9 8.1 %collective-permute-start.5 = (f32[16,1326]{1,0:T(8,128)}, f32[16,1326]{1,0:T(8,128)S(1)}, u32[]{:S(2)}, u32[]{:S(2)}) collective-permute-start(f32[16,1326]{1,0:T(8,128)} %get-tuple-element.9), channel_id=1, source_target_pairs={{0,8},{8,0},{16,24},{24,16},{1,9},{9,1},{17,25},{25,17},{2,10},{10... | collective-permute-start | bytes 254600 | tf_op jit(solution)/shard_map/ppermute | solution.py:162

commit v2 on v1

v2 whole, which is shorter than its diff:
```python
import functools

import jax
import jax.numpy as jnp
import numpy as np
from jax import lax
from jax.experimental import pallas as pl
from jax.experimental.pallas import tpu as pltpu
from jax.sharding import PartitionSpec as P

CARDS = 52
ACTS = 2
LANE = 128
SUB = 32
RANK_SPAN = 8192
MANTISSA = 128
ROW_TILE = 128
COL_TILE = 768
UNROLL = 8
STEPS = 32767.0
LOWEST = 100
WHOLE = pl.BlockSpec(memory_space=pltpu.VMEM)
SCALARS = pl.BlockSpec(memory_space=pltpu.SMEM)

floor_share = 0.1


def up(value, unit):
    return -(-value // unit) * unit


def tiles(total, size):
    return [(first, min(size, total - first)) for first in range(0, total, size)]


def params(mebibytes):
    return pltpu.CompilerParams(vmem_limit_bytes=mebibytes << 20)


@functools.cache
def tables(hand_count):
    wide, deep = up(hand_count, LANE), up(hand_count, 16)
    first, second = np.triu_indices(CARDS, 1)
    cards = np.zeros((hand_count, CARDS), np.float32)
    cards[np.arange(hand_count), first] = 1
    cards[np.arange(hand_count), second] = 1
    apart = np.zeros((deep, wide), np.float32)
    apart[:hand_count, :hand_count] = (cards @ cards.T) == 0
    sums = np.concatenate([np.ones((hand_count, 1), np.float32), cards], axis=1)
    parts = sums.shape[1]
    collect = np.zeros((wide, LANE), np.float32)
    spread = np.zeros((LANE, wide), np.float32)
    signed = sums.copy()
    signed[:, 1:] *= -1
    for copy in range(2):
        collect[:hand_count, copy * parts : (copy + 1) * parts] = sums
        spread[copy * parts : (copy + 1) * parts, :hand_count] = signed.T
    return [table.astype(jnp.bfloat16) for table in (apart, collect, spread)]


def as_column(row):
    size = row.shape[1]
    at = lax.broadcasted_iota(jnp.int32, (size, size), 0) == lax.broadcasted_iota(jnp.int32, (size, size), 1)
    return jnp.sum(jnp.where(at, row.astype(jnp.float32), 0.0), axis=1, keepdims=True)


def pack_kernel(hand_count, count_ref, slots_ref, ranks_ref, live_ref, out_ref):
    wide = up(hand_count, LANE)
    boards = out_ref.shape[0]
    out_ref[:, wide - LANE : wide] = jnp.zeros((boards, LANE), jnp.int32)
    out_ref[:, :hand_count] = ranks_ref[...] + RANK_SPAN * live_ref[...]
    slot = lax.broadcasted_iota(jnp.int32, (1, slots_ref.shape[1]), 1)
    for board in range(boards):
        lines = slots_ref[board : board + 1]
        out_ref[board : board + 1, wide:] = jnp.where(slot < count_ref[board], lines, -1)


def pack(counts, slots, ranks, live):
    hand_count = ranks.shape[1]
    return pl.pallas_call(
        functools.partial(pack_kernel, hand_count),
        out_shape=jax.ShapeDtypeStruct((slots.shape[0], up(hand_count, LANE) + slots.shape[1]), jnp.int32),
        in_specs=[SCALARS] + [WHOLE] * 3,
        out_specs=WHOLE,
        compiler_params=params(4),
        name="pack_boards",
    )(counts, slots, ranks, live)


def fetch_kernel(after_ref, table_ref, out_ref, sem):
    copy = pltpu.make_async_copy(table_ref, out_ref, sem)
    copy.start()
    copy.wait()


def fetch(table, after):
    return pl.pallas_call(
        fetch_kernel,
        out_shape=jax.ShapeDtypeStruct(table.shape, table.dtype),
        in_specs=[WHOLE, pl.BlockSpec(memory_space=pl.ANY)],
        out_specs=WHOLE,
        scratch_shapes=[pltpu.SemaphoreType.DMA],
        compiler_params=params(8),
        name="fetch_table",
        cost_estimate=pl.CostEstimate(flops=0, bytes_accessed=2 * table.size * 2, transcendentals=0),
    )(after, table)


def boards_kernel(hand_count, line_count, base_ref, own_ref, mate_ref, own_kind_ref, mate_kind_ref, *refs, boards_in):
    board_refs, refs = refs[:boards_in], refs[boards_in:]
    apart_ref, collect_ref, spread_ref, own_out, mate_out, column_ref, board_ref, reach_ref = refs
    wide = up(hand_count, LANE)
    deep = apart_ref.shape[0]
    rows = own_ref.shape[0]
    parts = 1 + CARDS
    reach_ref[...] = jnp.zeros_like(reach_ref)
    reach_ref[:rows, :hand_count] = own_ref[...]
    reach_ref[rows:, :hand_count] = mate_ref[...]
    kind = jnp.concatenate([as_column(own_kind_ref[...]), as_column(mate_kind_ref[...])], axis=0)
    row = lax.broadcasted_iota(jnp.int32, (2 * rows, 1), 0)
    within = jnp.where(row < rows, row, row - rows)
    line = jnp.where(row < rows, base_ref[0], base_ref[1]) + within
    line = jnp.where(within < line_count, line, -2)
    lane = lax.broadcasted_iota(jnp.int32, (2 * rows, LANE), 1)
    own_out[...] = jnp.zeros_like(own_out)
    mate_out[...] = jnp.zeros_like(mate_out)
    board_total = 0
    for ref in board_refs:
        board_ref[board_total : board_total + ref.shape[0]] = ref[...]
        board_total += ref.shape[0]

    def add_board(board):
        keys = board_ref[pl.ds(board, 1), :wide]
        slots = board_ref[pl.ds(board, 1), wide:]
        ranks = keys & (RANK_SPAN - 1)
        live = (keys >> (RANK_SPAN.bit_length() - 1)).astype(jnp.float32)
        power = ranks >> (MANTISSA.bit_length() - 1)
        near = jnp.left_shift(1, jnp.minimum(power, 29)).astype(jnp.float32)
        far = jnp.left_shift(1, jnp.maximum(power - 29, 0)).astype(jnp.float32)
        order = ((ranks & (MANTISSA - 1)) + MANTISSA).astype(jnp.float32) * near * far
        column_ref[...] = jnp.transpose(jnp.broadcast_to(order, (LANE, wide)))[:deep].astype(jnp.bfloat16)
        order = order.astype(jnp.bfloat16)
        keep = jnp.max(jnp.where(slots == line, 1.0, 0.0), axis=1, keepdims=True)
        show_keep = jnp.where(kind == 0, keep, 0.0).astype(jnp.bfloat16)
        fold_keep = jnp.where(kind == 0, 0.0, keep).astype(jnp.bfloat16)
        held = reach_ref[...] * live.astype(jnp.bfloat16)
        show_reach = held * show_keep
        fold_reach = held * fold_keep
        sums = jnp.dot(fold_reach, collect_ref[...], preferred_element_type=jnp.float32)
        high = sums.astype(jnp.bfloat16).astype(jnp.float32)
        sums = jnp.where(lane < parts, high, sums - high).astype(jnp.bfloat16)
        one = jnp.bfloat16(1)
        for first, count in tiles(wide, COL_TILE):
            at = slice(first, first + count)
            total = jnp.dot(sums, spread_ref[:, at], preferred_element_type=jnp.float32)
            for top, height in tiles(deep, ROW_TILE):
                down = slice(top, top + height)
                column = jnp.concatenate([column_ref[down]] * (count // LANE), axis=1)
                matrix = jnp.clip(order[:, at] - column, -one, one) * apart_ref[down, at]
                total += jnp.dot(show_reach[:, down], matrix, preferred_element_type=jnp.float32)
            total = (total + fold_reach[:, at].astype(jnp.float32)) * live[:, at]
            own_out[:, at] += total[:rows]
            mate_out[:, at] += total[rows:]

    if board_total <= UNROLL:
        for board in range(board_total):
            add_board(board)
    else:
        pl.loop(0, board_total)(add_board)


def board_sums(hand_count, line_count, base, reach, kinds, boards, apart, collect, spread):
    rows, wide = reach[0].shape[0], up(hand_count, LANE)
    out = jax.ShapeDtypeStruct((rows, wide), jnp.float32)
    total = sum(board.shape[0] for board in boards)
    return pl.pallas_call(
        functools.partial(boards_kernel, hand_count, line_count, boards_in=len(boards)),
        out_shape=(out, out),
        in_specs=[SCALARS] + [WHOLE] * (7 + len(boards)),
        out_specs=(WHOLE, WHOLE),
        scratch_shapes=[
            pltpu.VMEM((apart.shape[0], LANE), jnp.bfloat16),
            pltpu.VMEM((total, boards[0].shape[1]), jnp.int32),
            pltpu.VMEM((2 * rows, wide), jnp.bfloat16),
        ],
        compiler_params=params(32),
        name="board_sums",
        cost_estimate=pl.CostEstimate(flops=4 * total * rows * wide * wide, bytes_accessed=0, transcendentals=0),
    )(base, *reach, *kinds, *boards, apart, collect, spread)


def powers():
    lane = lax.broadcasted_iota(jnp.int32, (1, LANE), 1)
    up_size, down_size = jnp.ones((1, LANE), jnp.float32), jnp.ones((1, LANE), jnp.float32)
    bit = 1
    while bit < LANE:
        chosen = (jnp.abs(lane - LOWEST) & bit) != 0
        up_size = jnp.where(chosen, up_size * 2.0**bit, up_size)
        down_size = jnp.where(chosen, down_size * 0.5**bit, down_size)
        bit *= 2
    return jnp.where(lane < LOWEST, down_size, up_size), jnp.where(lane < LOWEST, up_size, down_size)


def update_kernel(hand_count, scale, own_ref, mate_ref, pot_ref, kind_ref, regret_ref, regret_out, code_out, node_ref):
    pot = as_column(pot_ref[...])
    coef = jnp.where(as_column(kind_ref[...]) == 1, -pot, pot) * scale
    values = (own_ref[:, :hand_count] + mate_ref[:, :hand_count]) * coef
    regrets = regret_ref[...]
    rows = regrets.shape[0]
    even = lax.broadcasted_iota(jnp.int32, (rows, 1), 0) % ACTS == 0

    def both(array):
        other = jnp.where(even, pltpu.roll(array, rows - 1, 0), pltpu.roll(array, 1, 0))
        return array + other

    positive = jnp.maximum(regrets, 0.0)
    strategy = (positive + floor_share) / (both(positive) + ACTS * floor_share)
    node = both(strategy * values)
    regret_out[...] = jnp.maximum(regrets + values - node, 0.0)
    size, flip = powers()
    largest = jnp.max(jnp.abs(node), axis=1, keepdims=True)
    place = jnp.sum(jnp.where(size < largest, 1.0, 0.0), axis=1, keepdims=True)
    lane = lax.broadcasted_iota(jnp.int32, (rows, LANE), 1).astype(jnp.float32)
    gain = jnp.sum(jnp.where(lane == place, flip, 0.0), axis=1, keepdims=True) * STEPS
    codes = node * gain
    for tile, (first, count) in enumerate(tiles(hand_count, LANE)):
        node_ref[tile, :, :count] = codes[:, first : first + count]
        if count < LANE:
            node_ref[tile, :, count:] = jnp.broadcast_to(place, (rows, LANE - count))
        picked = node_ref[tile, pl.ds(0, rows // ACTS, stride=ACTS), :]
        code_out[:, first : first + LANE] = jnp.floor(picked + 0.5).astype(jnp.int32).astype(jnp.int16)


def update(hand_count, scale, own, mate, pots, kinds, regrets):
    rows = regrets.shape[0]
    return pl.pallas_call(
        functools.partial(update_kernel, hand_count, scale),
        out_shape=(
            jax.ShapeDtypeStruct((rows, hand_count), jnp.float32),
            jax.ShapeDtypeStruct((rows // ACTS, up(hand_count, LANE)), jnp.int16),
        ),
        in_specs=[WHOLE] * 5,
        out_specs=(WHOLE, WHOLE),
        scratch_shapes=[pltpu.VMEM((up(hand_count, LANE) // LANE, rows, LANE), jnp.float32)],
        compiler_params=params(8),
        name="regret_update",
    )(own, mate, pots, kinds, regrets)


def chance_kernel(hand_count, *refs):
    code_refs, out_ref = refs[:-1], refs[-1]
    size, _ = powers()
    lane = lax.broadcasted_iota(jnp.int32, (out_ref.shape[0], LANE), 1)

    def value(ref):
        codes = ref[...].astype(jnp.int32)
        place = codes[:, hand_count : hand_count + 1]
        gain = jnp.sum(jnp.where(lane == place, size, 0.0), axis=1, keepdims=True)
        return codes[:, :hand_count].astype(jnp.float32) * (gain * (1.0 / (STEPS * len(code_refs))))

    total = None
    for first, second in zip(code_refs[::2], code_refs[1::2]):
        pair = value(first) + value(second)
        total = pair if total is None else total + pair
    out_ref[...] = total


def chance(hand_count, codes):
    return pl.pallas_call(
        functools.partial(chance_kernel, hand_count),
        out_shape=jax.ShapeDtypeStruct((codes[0].shape[0], hand_count), jnp.float32),
        in_specs=[WHOLE] * len(codes),
        out_specs=WHOLE,
        compiler_params=params(8),
        name="chance_sum",
    )(*codes)


def swap(array, axes, mask):
    return lax.ppermute(array, axes, [(index, index ^ mask) for index in range(lax.axis_size(axes))])


def on_device(
    regrets, opp_reach, pot_size, line_kind, board_lines, board_count, hand_ranks, live_hands
):
    hand_count = opp_reach.shape[2]
    line_count = opp_reach.shape[1]
    group = ("turn", "river")
    group_size = lax.axis_size(group)
    core = lax.axis_size("river")
    board_total = group_size * board_lines.shape[2]
    extra = up(line_count, SUB) - line_count
    apart, collect, spread = [jnp.asarray(table) for table in tables(hand_count)]

    boards = pack(board_count[0, 0], board_lines[0, 0], hand_ranks[0, 0], live_hands[0, 0])
    masks = [mask for mask in range(1, group_size) if not mask & core]
    if len(masks) < 4:
        parts = [boards] + [swap(boards, group, mask) for mask in masks]
    else:
        parts = boards
        for mask in masks:
            if mask & (mask - 1) == 0:
                parts = jnp.concatenate([parts, swap(parts, group, mask)], axis=0)
        parts = [parts]
    reach = jnp.pad(opp_reach[0], ((0, extra), (0, 0)))
    kinds = jnp.pad(line_kind, ((0, 0), (0, extra)))
    pots = jnp.pad(pot_size, ((0, 0), (0, extra)))
    held = jnp.pad(regrets[0], ((0, extra), (0, 0)))
    mate_reach, mate_kinds = swap(reach, group, core), swap(kinds, group, core)
    apart = fetch(apart, boards)
    index = lax.axis_index(group)
    base = jnp.stack([index, index ^ core]).astype(jnp.int32) * line_count
    own, for_mate = board_sums(
        hand_count, line_count, base, (reach, mate_reach), (kinds, mate_kinds), parts, apart, collect, spread
    )
    mate = swap(for_mate, group, core)
    updated, codes = update(hand_count, 1.0 / (board_total * hand_count), own, mate, pots, kinds, held)
    flops = lax.axis_size("flop")
    total = chance(hand_count, [codes] + [swap(codes, "flop", mask) for mask in range(1, flops)])
    return (updated[None, :line_count], total[: line_count // ACTS])


def solution(mesh):
    placed = (
        P("flop", ("turn", "river"), None),
        P("flop", ("turn", "river"), None),
        P("flop", ("turn", "river")),
        P("flop", ("turn", "river")),
        P("flop", "turn", "river", None),
        P("flop", "turn", "river"),
        P("flop", "turn", "river", None),
        P("flop", "turn", "river", None),
    )
    return jax.shard_map(
        on_device,
        mesh=mesh,
        in_specs=placed,
        out_specs=(P("flop", ("turn", "river"), None), P(("turn", "river"), None)),
        check_vma=False,
    )
```

time: 47 us -> 31.8 us (0.68)
  other arithmetic: 4.85 us -> 0.08 us
  Pallas kernels: 14.1 us -> 9.54 us
  waiting for transfers between devices: 10.3 us -> 6.29 us
  local copies, waits for them, and re-layouts: 7.53 us -> 5.04 us
  starting transfers between devices: 9.02 us -> 9.75 us
    pallas_call x1, Pallas kernels: 12 us -> 6.98 us  [board_sums(): pl.pallas_call(functools.partial(boards_kernel, hand_count, line_count, b...]
    ppermute x8 -> x9, waiting for transfers between devices: 10.3 us -> 6.29 us  [swap(): lax.ppermute(array, axes, [(index, index ^ mask) for index in range(lax.a...]
    unnamed x14 -> x22, local copies, waits for them, and re-layouts: 7.43 us -> 5.04 us
    pallas_call x0 -> x3, Pallas kernels: none -> 1.72 us  [the longest x1 0.81 us: chance(): pl.pallas_call(functools.partial(chance_kernel, hand_count), out_shape=ja...]
    div x1 -> x0, other arithmetic: 1.56 us -> none  [on_device(): return (updated[None], total / flops)]
    pallas_call x1, Pallas kernels: 2.04 us -> 0.85 us  [update(): pl.pallas_call(functools.partial(update_kernel, hand_count, scale), out_s...]
    concatenate x3 -> x0, other arithmetic: 0.99 us -> none  [the longest x1 0.97 us: on_device(): reach = jnp.concatenate([opp_reach[0], terms], axis=1)]
    select_n x1 -> x0, other arithmetic: 0.75 us -> none  [on_device(): slots = jnp.where(slot < board_count[0, 0][:, None], board_lines[0, 0], -1)]
  transfers between devices with their start and end apart: 8 -> 9, of which waited for: 5 -> 4; matrix products, arithmetic and copies ran while one was open for 4% -> 0% of each run, Pallas kernels for 0% -> 1%
where the time goes in v2:
time: 31.8 us; the launch traced here: 31.4 us
  starting transfers between devices  9.75 us (31%)
  Pallas kernels  9.54 us (30%)
  waiting for transfers between devices  6.29 us (20%)
  local copies, waits for them, and re-layouts  5.04 us (16%)
  between operations  0.73 us (2%)
    ppermute x9, starting transfers between devices, swap(): lax.ppermute(array, axes, [(index, index ^ mask) for index in range(lax.a...  9.75 us
    pallas_call x1, Pallas kernels, board_sums(): pl.pallas_call(functools.partial(boards_kernel, hand_count, line_count, b...  6.98 us
    ppermute x9, waiting for transfers between devices, swap(): lax.ppermute(array, axes, [(index, index ^ mask) for index in range(lax.a...  6.29 us
    unnamed x22, local copies, waits for them, and re-layouts  5.04 us
    pallas_call x1, Pallas kernels, update(): pl.pallas_call(functools.partial(update_kernel, hand_count, scale), out_s...  0.85 us
    pallas_call x1, Pallas kernels, chance(): pl.pallas_call(functools.partial(chance_kernel, hand_count), out_shape=ja...  0.81 us
  transfers between devices with their start and end apart: 9, of which 4 were waited for; matrix products, arithmetic and copies ran while one was open for 0% of the time, Pallas kernels for 1%

profile of v2, /device:TPU:0, one launch (start us, length us, event | category | flops | bytes accessed | tf_op | source)
XLA Modules:
  0.0 31.4 jit_solution(11041762071519972195)
XLA Ops:
  0.6 0.0 copy-start.2
  0.6 0.7 %copy-done.2 = s32[1,1,2,1326]{3,2,1,0:T(2,128)S(1)} copy-done((s32[1,1,2,1326]{3,2,1,0:T(2,128)S(1)}, s32[1,1,2,1326]{3,2,1,0:T(2,128)}, u32[]{:S(2)}) %copy-start.2) | copy-done | bytes 10632
  1.3 0.0 copy-start.3
  1.3 0.7 %copy-done.3 = s32[1,1,2,1326]{3,2,1,0:T(2,128)S(1)} copy-done((s32[1,1,2,1326]{3,2,1,0:T(2,128)S(1)}, s32[1,1,2,1326]{3,2,1,0:T(2,128)}, u32[]{:S(2)}) %copy-start.3) | copy-done | bytes 10632
  2.0 0.0 copy-start.4
  2.0 0.7 %copy-done.4 = s32[1,1,2,256]{3,2,1,0:T(2,128)S(1)} copy-done((s32[1,1,2,256]{3,2,1,0:T(2,128)S(1)}, s32[1,1,2,256]{3,2,1,0:T(2,128)}, u32[]{:S(2)}) %copy-start.4) | copy-done | bytes 2072
  2.7 0.0 copy-start.5
  2.7 0.7 %copy-done.5 = s32[1,1,2]{2,1,0:T(1,128)S(1)} copy-done((s32[1,1,2]{2,1,0:T(1,128)S(1)}, s32[1,1,2]{2,1,0:T(1,128)}, u32[]{:S(2)}) %copy-start.5) | copy-done | bytes 32
  3.4 0.5 %pack_boards.1.after_ref.refs_0_ = s32[2,1664]{1,0:T(2,128)S(1)} custom-call(s32[2]{0:T(128)S(1)} %bitcast.13, s32[2,256]{1,0:T(2,128)S(1)} %bitcast.12, s32[2,1326]{1,0:T(2,128)S(1)} %bitcast.10, s32[2,1326]{1,0:T(2,128)S(1)} %bitcast.11), custom_call_target="tpu_custom_call" | custom-call | tf_op jit(solution)/shard_map/pack_boards/pallas_call | solution.py:80
  3.9 4.0 %collective-permute-start.4 = (s32[2,1664]{1,0:T(2,128)S(1)}, s32[2,1664]{1,0:T(2,128)S(1)}, u32[]{:S(2)}, u32[]{:S(2)}) collective-permute-start(s32[2,1664]{1,0:T(2,128)S(1)} %pack_boards.1.after_ref.refs_0_), channel_id=1, source_target_pairs={{0,5},{1,4},{2,7},{3,6},{4,1},{5,0},{6,3},{7,2},{8,13},{9,12},{10,... | collective-permute-start | bytes 39944 | tf_op jit(solution)/shard_map/ppermute | solution.py:280
  7.9 0.5 %collective-permute-start.3 = (s32[2,1664]{1,0:T(2,128)S(1)}, s32[2,1664]{1,0:T(2,128)S(1)}, u32[]{:S(2)}, u32[]{:S(2)}) collective-permute-start(s32[2,1664]{1,0:T(2,128)S(1)} %pack_boards.1.after_ref.refs_0_), channel_id=1, source_target_pairs={{0,4},{1,5},{2,6},{3,7},{4,0},{5,1},{6,2},{7,3},{8,12},{9,13},{10,... | collective-permute-start | bytes 39944 | tf_op jit(solution)/shard_map/ppermute | solution.py:280
  8.4 0.1 collective-permute-start.2
  8.5 0.0 collective-permute-start.1
  8.5 0.5 %collective-permute-start = (bf16[32,1326]{1,0:T(8,128)(2,1)}, bf16[32,1326]{1,0:T(8,128)(2,1)S(1)}, u32[]{:S(2)}, u32[]{:S(2)}) collective-permute-start(bf16[32,1326]{1,0:T(8,128)(2,1)} %bitcast.14), channel_id=1, source_target_pairs={{0,2},{1,3},{2,0},{3,1},{4,6},{5,7},{6,4},{7,5},{8,10},{9,11},{10,... | collective-permute-start | bytes 254600 | tf_op jit(solution)/shard_map/ppermute | solution.py:280
  9.1 0.1 add_multiply_fusion.base_ref
  9.1 0.0 copy-start
  9.1 2.1 %copy-done = bf16[1328,1408]{1,0:T(8,128)(2,1)S(1)} copy-done((bf16[1328,1408]{1,0:T(8,128)(2,1)S(1)}, bf16[1328,1408]{1,0:T(8,128)(2,1)}, u32[]{:S(2)}) %copy-start) | copy-done | bytes 3739672
  11.2 0.0 copy-start.6
  11.2 0.0 copy-start.8
  11.2 0.0 copy-start.9
  11.2 0.0 copy-start.10
  11.2 0.4 %fetch_table.1.refs_4_ = bf16[1328,1408]{1,0:T(8,128)(2,1)S(1)} custom-call(s32[2,1664]{1,0:T(2,128)S(1)} %pack_boards.1.after_ref.refs_0_, bf16[1328,1408]{1,0:T(8,128)(2,1)S(1)} %copy-done), custom_call_target="tpu_custom_call" | custom-call | bytes 7479296 | tf_op jit(solution)/shard_map/fetch_table/pallas_call | solution.py:97
  11.6 0.0 copy-start.1
  11.6 0.0 copy-start.7
  11.6 0.0 collective-permute-done.1.mate_kind_ref
  11.6 0.0 collective-permute-done.4.refs_3_
  11.6 0.0 collective-permute-done.3.refs_2_
  11.6 0.5 %collective-permute-done.2.refs_1_ = s32[2,1664]{1,0:T(2,128)S(1)} collective-permute-done((s32[2,1664]{1,0:T(2,128)S(1)}, s32[2,1664]{1,0:T(2,128)S(1)}, u32[]{:S(2)}, u32[]{:S(2)}) %collective-permute-start.2) | collective-permute-done | bytes 13344 | tf_op jit(solution)/shard_map/ppermute | solution.py:280
  12.1 0.0 collective-permute-done.mate_ref
  12.1 0.0 copy-done.6
  12.1 0.0 copy-done.8
  12.1 0.1 copy-done.9
  12.2 0.1 copy-done.10
  12.3 7.0 %board_sums.1 = (f32[32,1408]{1,0:T(8,128)S(1)}, f32[32,1408]{1,0:T(8,128)S(1)}) custom-call(s32[2]{0:T(128)S(1)} %add_multiply_fusion.base_ref, bf16[32,1326]{1,0:T(8,128)(2,1)S(1)} %bitcast.15, bf16[32,1326]{1,0:T(8,128)(2,1)S(1)} %collective-permute-done.mate_ref, s32[1,32]{1,0:T(1,128)S(1)} %copy-done.6, ...), custom_call_target="tpu_custom_call" | custom-call | flops 2030043136 | tf_op jit(solution)/shard_map/board_sums/pallas_call | solution.py:176
  19.3 0.1 collective-permute-start.5
  19.4 1.4 %collective-permute-done.5.mate_ref = f32[32,1408]{1,0:T(8,128)S(1)} collective-permute-done((f32[32,1408]{1,0:T(8,128)S(1)}, f32[32,1408]{1,0:T(8,128)S(1)}, u32[]{:S(2)}, u32[]{:S(2)}) %collective-permute-start.5) | collective-permute-done | bytes 180256 | tf_op jit(solution)/shard_map/ppermute | solution.py:280
  20.8 0.0 copy-done.1
  20.8 0.0 copy-done.7
  20.8 0.8 %regret_update.1 = (f32[32,1326]{1,0:T(8,128)}, s16[16,1408]{1,0:T(8,128)(2,1)S(1)}) custom-call(f32[32,1408]{1,0:T(8,128)S(1)} %get-tuple-element.6.own_ref, f32[32,1408]{1,0:T(8,128)S(1)} %collective-permute-done.5.mate_ref, s32[1,32]{1,0:T(1,128)S(1)} %copy-done.7, s32[1,32]{1,0:T(1,128)S(1)} %copy-done.6, f32[32,1326]{1,0:T(8,128)S(1)} %bitcast.9), custom_call_target="tpu_custom_call" | custom-call | tf_op jit(solution)/shard_map/regret_update/pallas_call | solution.py:236
  21.7 4.0 %collective-permute-start.8 = (s16[16,1408]{1,0:T(8,128)(2,1)S(1)}, s16[16,1408]{1,0:T(8,128)(2,1)S(1)}, u32[]{:S(2)}, u32[]{:S(2)}) collective-permute-start(s16[16,1408]{1,0:T(8,128)(2,1)S(1)} %get-tuple-element.9.refs_0_), channel_id=1, source_target_pairs={{0,24},{8,16},{16,8},{24,0},{1,25},{9,17},{17,9},{25,1},{2,26},{10... | collective-permute-start | bytes 135176 | tf_op jit(solution)/shard_map/ppermute | solution.py:280
  25.7 0.0 collective-permute-start.7
  25.7 0.6 %collective-permute-start.6 = (s16[16,1408]{1,0:T(8,128)(2,1)S(1)}, s16[16,1408]{1,0:T(8,128)(2,1)S(1)}, u32[]{:S(2)}, u32[]{:S(2)}) collective-permute-start(s16[16,1408]{1,0:T(8,128)(2,1)S(1)} %get-tuple-element.9.refs_0_), channel_id=1, source_target_pairs={{0,8},{8,0},{16,24},{24,16},{1,9},{9,1},{17,25},{25,17},{2,10},{10... | collective-permute-start | bytes 135176 | tf_op jit(solution)/shard_map/ppermute | solution.py:280
  26.2 1.5 %collective-permute-done.8.refs_3_ = s16[16,1408]{1,0:T(8,128)(2,1)S(1)} collective-permute-done((s16[16,1408]{1,0:T(8,128)(2,1)S(1)}, s16[16,1408]{1,0:T(8,128)(2,1)S(1)}, u32[]{:S(2)}, u32[]{:S(2)}) %collective-permute-start.8) | collective-permute-done | bytes 45088 | tf_op jit(solution)/shard_map/ppermute | solution.py:280
  27.8 2.9 %collective-permute-done.7.refs_2_ = s16[16,1408]{1,0:T(8,128)(2,1)S(1)} collective-permute-done((s16[16,1408]{1,0:T(8,128)(2,1)S(1)}, s16[16,1408]{1,0:T(8,128)(2,1)S(1)}, u32[]{:S(2)}, u32[]{:S(2)}) %collective-permute-start.7) | collective-permute-done | bytes 45088 | tf_op jit(solution)/shard_map/ppermute | solution.py:280
  30.6 0.0 collective-permute-done.6.refs_1_
  30.6 0.8 %chance_sum.1 = f32[16,1326]{1,0:T(8,128)} custom-call(s16[16,1408]{1,0:T(8,128)(2,1)S(1)} %get-tuple-element.9.refs_0_, s16[16,1408]{1,0:T(8,128)(2,1)S(1)} %collective-permute-done.6.refs_1_, s16[16,1408]{1,0:T(8,128)(2,1)S(1)} %collective-permute-done.7.refs_2_, s16[16,1408]{1,0:T(8,128)(2,1)S(1)} %collective-permute-done.8.refs_3_), custom_call_target="tpu_custom_call" | custom-call | tf_op jit(solution)/shard_map/chance_sum/pallas_call | solution.py:269
Async XLA Ops:
  0.6 0.7 %copy-start.2 = (s32[1,1,2,1326]{3,2,1,0:T(2,128)S(1)}, s32[1,1,2,1326]{3,2,1,0:T(2,128)}, u32[]{:S(2)}) copy-start(s32[1,1,2,1326]{3,2,1,0:T(2,128)} %param.17) | copy-start | bytes 31828
  1.3 0.7 %copy-start.3 = (s32[1,1,2,1326]{3,2,1,0:T(2,128)S(1)}, s32[1,1,2,1326]{3,2,1,0:T(2,128)}, u32[]{:S(2)}) copy-start(s32[1,1,2,1326]{3,2,1,0:T(2,128)} %param.18) | copy-start | bytes 31828
  2.0 0.7 %copy-start.4 = (s32[1,1,2,256]{3,2,1,0:T(2,128)S(1)}, s32[1,1,2,256]{3,2,1,0:T(2,128)}, u32[]{:S(2)}) copy-start(s32[1,1,2,256]{3,2,1,0:T(2,128)} %param.15) | copy-start | bytes 6148
  2.7 0.7 %copy-start.5 = (s32[1,1,2]{2,1,0:T(1,128)S(1)}, s32[1,1,2]{2,1,0:T(1,128)}, u32[]{:S(2)}) copy-start(s32[1,1,2]{2,1,0:T(1,128)} %param.16) | copy-start | bytes 28
  3.9 7.7 %collective-permute-start.4 = (s32[2,1664]{1,0:T(2,128)S(1)}, s32[2,1664]{1,0:T(2,128)S(1)}, u32[]{:S(2)}, u32[]{:S(2)}) collective-permute-start(s32[2,1664]{1,0:T(2,128)S(1)} %pack_boards.1.after_ref.refs_0_), channel_id=1, source_target_pairs={{0,5},{1,4},{2,7},{3,6},{4,1},{5,0},{6,3},{7,2},{8,13},{9,12},{10,... | collective-permute-start | bytes 39944 | tf_op jit(solution)/shard_map/ppermute | solution.py:280
  7.9 3.7 %collective-permute-start.3 = (s32[2,1664]{1,0:T(2,128)S(1)}, s32[2,1664]{1,0:T(2,128)S(1)}, u32[]{:S(2)}, u32[]{:S(2)}) collective-permute-start(s32[2,1664]{1,0:T(2,128)S(1)} %pack_boards.1.after_ref.refs_0_), channel_id=1, source_target_pairs={{0,4},{1,5},{2,6},{3,7},{4,0},{5,1},{6,2},{7,3},{8,12},{9,13},{10,... | collective-permute-start | bytes 39944 | tf_op jit(solution)/shard_map/ppermute | solution.py:280
  8.4 3.7 %collective-permute-start.2 = (s32[2,1664]{1,0:T(2,128)S(1)}, s32[2,1664]{1,0:T(2,128)S(1)}, u32[]{:S(2)}, u32[]{:S(2)}) collective-permute-start(s32[2,1664]{1,0:T(2,128)S(1)} %pack_boards.1.after_ref.refs_0_), channel_id=1, source_target_pairs={{0,1},{1,0},{2,3},{3,2},{4,5},{5,4},{6,7},{7,6},{8,9},{9,8},{10,11... | collective-permute-start | bytes 39944 | tf_op jit(solution)/shard_map/ppermute | solution.py:280
  8.5 3.0 %collective-permute-start.1 = (s32[1,32]{1,0:T(1,128)}, s32[1,32]{1,0:T(1,128)S(1)}, u32[]{:S(2)}, u32[]{:S(2)}) collective-permute-start(s32[1,32]{1,0:T(1,128)} %kind_ref.1), channel_id=1, source_target_pairs={{0,2},{1,3},{2,0},{3,1},{4,6},{5,7},{6,4},{7,5},{8,10},{9,11},{10,... | collective-permute-start | bytes 392 | tf_op jit(solution)/shard_map/ppermute | solution.py:280
  8.5 3.6 %collective-permute-start = (bf16[32,1326]{1,0:T(8,128)(2,1)}, bf16[32,1326]{1,0:T(8,128)(2,1)S(1)}, u32[]{:S(2)}, u32[]{:S(2)}) collective-permute-start(bf16[32,1326]{1,0:T(8,128)(2,1)} %bitcast.14), channel_id=1, source_target_pairs={{0,2},{1,3},{2,0},{3,1},{4,6},{5,7},{6,4},{7,5},{8,10},{9,11},{10,... | collective-permute-start | bytes 254600 | tf_op jit(solution)/shard_map/ppermute | solution.py:280
  9.1 2.1 %copy-start = (bf16[1328,1408]{1,0:T(8,128)(2,1)S(1)}, bf16[1328,1408]{1,0:T(8,128)(2,1)}, u32[]{:S(2)}) copy-start(bf16[1328,1408]{1,0:T(8,128)(2,1)} %constant.19.clone.table_ref) | copy-start | bytes 11218948
  11.2 0.9 %copy-start.6 = (s32[1,32]{1,0:T(1,128)S(1)}, s32[1,32]{1,0:T(1,128)}, u32[]{:S(2)}) copy-start(s32[1,32]{1,0:T(1,128)} %kind_ref.1) | copy-start | bytes 388
  11.2 0.9 %copy-start.8 = (bf16[1,32,1326]{2,1,0:T(8,128)(2,1)S(1)}, bf16[1,32,1326]{2,1,0:T(8,128)(2,1)}, u32[]{:S(2)}) copy-start(bf16[1,32,1326]{2,1,0:T(8,128)(2,1)} %param.12) | copy-start | bytes 254596
  11.2 1.0 %copy-start.9 = (bf16[128,1408]{1,0:T(8,128)(2,1)S(1)}, bf16[128,1408]{1,0:T(8,128)(2,1)}, u32[]{:S(2)}) copy-start(bf16[128,1408]{1,0:T(8,128)(2,1)} %constant.21.clone.refs_6_) | copy-start | bytes 1081348
  11.2 1.1 %copy-start.10 = (bf16[1408,128]{1,0:T(8,128)(2,1)S(1)}, bf16[1408,128]{1,0:T(8,128)(2,1)}, u32[]{:S(2)}) copy-start(bf16[1408,128]{1,0:T(8,128)(2,1)} %constant.20.clone.refs_5_) | copy-start | bytes 1081348
  11.6 9.3 %copy-start.1 = (f32[1,32,1326]{2,1,0:T(8,128)S(1)}, f32[1,32,1326]{2,1,0:T(8,128)}, u32[]{:S(2)}) copy-start(f32[1,32,1326]{2,1,0:T(8,128)} %param.11) | copy-start | bytes 509188
  11.6 9.2 %copy-start.7 = (s32[1,32]{1,0:T(1,128)S(1)}, s32[1,32]{1,0:T(1,128)}, u32[]{:S(2)}) copy-start(s32[1,32]{1,0:T(1,128)} %pot_ref.1) | copy-start | bytes 388
  19.3 1.5 %collective-permute-start.5 = (f32[32,1408]{1,0:T(8,128)S(1)}, f32[32,1408]{1,0:T(8,128)S(1)}, u32[]{:S(2)}, u32[]{:S(2)}) collective-permute-start(f32[32,1408]{1,0:T(8,128)S(1)} %get-tuple-element.7), channel_id=1, source_target_pairs={{0,2},{1,3},{2,0},{3,1},{4,6},{5,7},{6,4},{7,5},{8,10},{9,11},{10,... | collective-permute-start | bytes 540680 | tf_op jit(solution)/shard_map/ppermute | solution.py:280
  21.7 6.1 %collective-permute-start.8 = (s16[16,1408]{1,0:T(8,128)(2,1)S(1)}, s16[16,1408]{1,0:T(8,128)(2,1)S(1)}, u32[]{:S(2)}, u32[]{:S(2)}) collective-permute-start(s16[16,1408]{1,0:T(8,128)(2,1)S(1)} %get-tuple-element.9.refs_0_), channel_id=1, source_target_pairs={{0,24},{8,16},{16,8},{24,0},{1,25},{9,17},{17,9},{25,1},{2,26},{10... | collective-permute-start | bytes 135176 | tf_op jit(solution)/shard_map/ppermute | solution.py:280
  25.7 4.9 %collective-permute-start.7 = (s16[16,1408]{1,0:T(8,128)(2,1)S(1)}, s16[16,1408]{1,0:T(8,128)(2,1)S(1)}, u32[]{:S(2)}, u32[]{:S(2)}) collective-permute-start(s16[16,1408]{1,0:T(8,128)(2,1)S(1)} %get-tuple-element.9.refs_0_), channel_id=1, source_target_pairs={{0,16},{8,24},{16,0},{24,8},{1,17},{9,25},{17,1},{25,9},{2,18},{10... | collective-permute-start | bytes 135176 | tf_op jit(solution)/shard_map/ppermute | solution.py:280
  25.7 4.9 %collective-permute-start.6 = (s16[16,1408]{1,0:T(8,128)(2,1)S(1)}, s16[16,1408]{1,0:T(8,128)(2,1)S(1)}, u32[]{:S(2)}, u32[]{:S(2)}) collective-permute-start(s16[16,1408]{1,0:T(8,128)(2,1)S(1)} %get-tuple-element.9.refs_0_), channel_id=1, source_target_pairs={{0,8},{8,0},{16,24},{24,16},{1,9},{9,1},{17,25},{25,17},{2,10},{10... | collective-permute-start | bytes 135176 | tf_op jit(solution)/shard_map/ppermute | solution.py:280

commit v3 on v2

--- a/solution.py
+++ b/solution.py
@@ -19,8 +19,10 @@
 UNROLL = 8
 STEPS = 32767.0
 LOWEST = 100
+FETCH_ROWS = 176
 WHOLE = pl.BlockSpec(memory_space=pltpu.VMEM)
 SCALARS = pl.BlockSpec(memory_space=pltpu.SMEM)
+REMAIN = pl.BlockSpec(memory_space=pltpu.HBM)
 
 floor_share = 0.1
 
@@ -64,9 +66,18 @@
     return jnp.sum(jnp.where(at, row.astype(jnp.float32), 0.0), axis=1, keepdims=True)
 
 
-def pack_kernel(hand_count, count_ref, slots_ref, ranks_ref, live_ref, out_ref):
+def copy_all(pairs, sems):
+    copies = [pltpu.make_async_copy(source, target, sems.at[at]) for at, (source, target) in enumerate(pairs)]
+    for copy in copies:
+        copy.start()
+    for copy in copies:
+        copy.wait()
+
+
+def pack_kernel(hand_count, count_ref, slots_hbm, ranks_hbm, live_hbm, out_ref, slots_ref, ranks_ref, live_ref, sems):
     wide = up(hand_count, LANE)
     boards = out_ref.shape[0]
+    copy_all([(slots_hbm, slots_ref), (ranks_hbm, ranks_ref), (live_hbm, live_ref)], sems)
     out_ref[:, wide - LANE : wide] = jnp.zeros((boards, LANE), jnp.int32)
     out_ref[:, :hand_count] = ranks_ref[...] + RANK_SPAN * live_ref[...]
     slot = lax.broadcasted_iota(jnp.int32, (1, slots_ref.shape[1]), 1)
@@ -77,33 +88,41 @@
 
 def pack(counts, slots, ranks, live):
     hand_count = ranks.shape[1]
+    inputs = (slots, ranks, live)
     return pl.pallas_call(
         functools.partial(pack_kernel, hand_count),
         out_shape=jax.ShapeDtypeStruct((slots.shape[0], up(hand_count, LANE) + slots.shape[1]), jnp.int32),
-        in_specs=[SCALARS] + [WHOLE] * 3,
+        in_specs=[SCALARS] + [REMAIN] * 3,
         out_specs=WHOLE,
+        scratch_shapes=[pltpu.VMEM(array.shape, array.dtype) for array in inputs] + [pltpu.SemaphoreType.DMA((3,))],
         compiler_params=params(4),
         name="pack_boards",
-    )(counts, slots, ranks, live)
-
-
-def fetch_kernel(after_ref, table_ref, out_ref, sem):
-    copy = pltpu.make_async_copy(table_ref, out_ref, sem)
-    copy.start()
-    copy.wait()
-
-
-def fetch(table, after):
+    )(counts, *inputs)
+
+
+def fetch_kernel(after_ref, *refs):
+    tables_in, tables_out, sems = refs[:3], refs[3:6], refs[6]
+    pairs = []
+    for source, target in zip(tables_in, tables_out):
+        for first, count in tiles(source.shape[0], FETCH_ROWS):
+            pairs.append((source.at[pl.ds(first, count)], target.at[pl.ds(first, count)]))
+    copy_all(pairs, sems)
+
+
+def fetch(arrays, after):
+    copies = sum(len(tiles(array.shape[0], FETCH_ROWS)) for array in arrays)
     return pl.pallas_call(
         fetch_kernel,
-        out_shape=jax.ShapeDtypeStruct(table.shape, table.dtype),
-        in_specs=[WHOLE, pl.BlockSpec(memory_space=pl.ANY)],
-        out_specs=WHOLE,
-        scratch_shapes=[pltpu.SemaphoreType.DMA],
-        compiler_params=params(8),
-        name="fetch_table",
-        cost_estimate=pl.CostEstimate(flops=0, bytes_accessed=2 * table.size * 2, transcendentals=0),
-    )(after, table)
+        out_shape=[jax.ShapeDtypeStruct(array.shape, array.dtype) for array in arrays],
+        in_specs=[WHOLE] + [REMAIN] * len(arrays),
+        out_specs=[WHOLE] * len(arrays),
+        scratch_shapes=[pltpu.SemaphoreType.DMA((copies,))],
+        compiler_params=params(12),
+        name="fetch_tables",
+        cost_estimate=pl.CostEstimate(
+            flops=0, bytes_accessed=sum(2 * array.nbytes for array in arrays), transcendentals=0
+        ),
+    )(after, *arrays)
 
 
 def boards_kernel(hand_count, line_count, base_ref, own_ref, mate_ref, own_kind_ref, mate_kind_ref, *refs, boards_in):
@@ -290,8 +309,6 @@
     core = lax.axis_size("river")
     board_total = group_size * board_lines.shape[2]
     extra = up(line_count, SUB) - line_count
-    apart, collect, spread = [jnp.asarray(table) for table in tables(hand_count)]
-
     boards = pack(board_count[0, 0], board_lines[0, 0], hand_ranks[0, 0], live_hands[0, 0])
     masks = [mask for mask in range(1, group_size) if not mask & core]
     if len(masks) < 4:
@@ -307,16 +324,17 @@
     pots = jnp.pad(pot_size, ((0, 0), (0, extra)))
     held = jnp.pad(regrets[0], ((0, extra), (0, 0)))
     mate_reach, mate_kinds = swap(reach, group, core), swap(kinds, group, core)
-    apart = fetch(apart, boards)
+    held_tables = fetch([jnp.asarray(table) for table in tables(hand_count)], boards)
     index = lax.axis_index(group)
     base = jnp.stack([index, index ^ core]).astype(jnp.int32) * line_count
     own, for_mate = board_sums(
-        hand_count, line_count, base, (reach, mate_reach), (kinds, mate_kinds), parts, apart, collect, spread
+        hand_count, line_count, base, (reach, mate_reach), (kinds, mate_kinds), parts, *held_tables
     )
     mate = swap(for_mate, group, core)
     updated, codes = update(hand_count, 1.0 / (board_total * hand_count), own, mate, pots, kinds, held)
     flops = lax.axis_size("flop")
-    total = chance(hand_count, [codes] + [swap(codes, "flop", mask) for mask in range(1, flops)])
+    arrived = {mask: swap(codes, "flop", mask) for mask in (flops - 1, *range(1, flops - 1))}
+    total = chance(hand_count, [codes] + [arrived[mask] for mask in range(1, flops)])
     return (updated[None, :line_count], total[: line_count // ACTS])
 
 

time: 31.8 us -> 35.9 us (1.13)
  Pallas kernels: 9.54 us -> 12.3 us
  local copies, waits for them, and re-layouts: 5.04 us -> 6.79 us
  waiting for transfers between devices: 6.29 us -> 5.8 us
    pallas_call x1, Pallas kernels: 0.35 us -> 3.04 us  [fetch(): pl.pallas_call(fetch_kernel, out_shape=[jax.ShapeDtypeStruct(array.shape,...]
    unnamed x22, local copies, waits for them, and re-layouts: 5.04 us -> 6.79 us
    ppermute x9, waiting for transfers between devices: 6.29 us -> 5.8 us  [swap(): lax.ppermute(array, axes, [(index, index ^ mask) for index in range(lax.a...]
  transfers between devices with their start and end apart: 9 -> 9, of which waited for: 4 -> 3; matrix products, arithmetic and copies ran while one was open for 0% -> 0% of each run, Pallas kernels for 1% -> 9%
where the time goes in v3:
time: 35.9 us; the launch traced here: 35.5 us
  Pallas kernels  12.3 us (34%)
  starting transfers between devices  9.76 us (27%)
  local copies, waits for them, and re-layouts  6.79 us (19%)
  waiting for transfers between devices  5.8 us (16%)
  between operations  0.77 us (2%)
    ppermute x9, starting transfers between devices, swap(): lax.ppermute(array, axes, [(index, index ^ mask) for index in range(lax.a...  9.76 us
    pallas_call x1, Pallas kernels, board_sums(): pl.pallas_call(functools.partial(boards_kernel, hand_count, line_count, b...  7.05 us
    unnamed x22, local copies, waits for them, and re-layouts  6.79 us
    ppermute x9, waiting for transfers between devices, swap(): lax.ppermute(array, axes, [(index, index ^ mask) for index in range(lax.a...  5.8 us
    pallas_call x1, Pallas kernels, fetch(): pl.pallas_call(fetch_kernel, out_shape=[jax.ShapeDtypeStruct(array.shape,...  3.04 us
    pallas_call x1, Pallas kernels, update(): pl.pallas_call(functools.partial(update_kernel, hand_count, scale), out_s...  0.85 us
    pallas_call x1, Pallas kernels, chance(): pl.pallas_call(functools.partial(chance_kernel, hand_count), out_shape=ja...  0.81 us
  transfers between devices with their start and end apart: 9, of which 3 were waited for; matrix products, arithmetic and copies ran while one was open for 0% of the time, Pallas kernels for 9%

profile of v3, /device:TPU:0, one launch (start us, length us, event | category | flops | bytes accessed | tf_op | source)
XLA Modules:
  0.0 35.5 jit_solution(14285279948213924308)
XLA Ops:
  0.6 0.0 copy-start.8
  0.6 0.0 copy-start.4
  0.7 0.7 %copy-done.4 = s32[1,1,2,1326]{3,2,1,0:T(2,128)S(1)} copy-done((s32[1,1,2,1326]{3,2,1,0:T(2,128)S(1)}, s32[1,1,2,1326]{3,2,1,0:T(2,128)}, u32[]{:S(2)}) %copy-start.4) | copy-done | bytes 10632
  1.4 0.0 copy-start.5
  1.4 0.7 %copy-done.5 = s32[1,1,2,1326]{3,2,1,0:T(2,128)S(1)} copy-done((s32[1,1,2,1326]{3,2,1,0:T(2,128)S(1)}, s32[1,1,2,1326]{3,2,1,0:T(2,128)}, u32[]{:S(2)}) %copy-start.5) | copy-done | bytes 10632
  2.1 0.0 copy-start.6
  2.1 0.7 %copy-done.6 = s32[1,1,2,256]{3,2,1,0:T(2,128)S(1)} copy-done((s32[1,1,2,256]{3,2,1,0:T(2,128)S(1)}, s32[1,1,2,256]{3,2,1,0:T(2,128)}, u32[]{:S(2)}) %copy-start.6) | copy-done | bytes 2072
  2.7 0.0 copy-start.7
  2.7 0.7 %copy-done.7 = s32[1,1,2]{2,1,0:T(1,128)S(1)} copy-done((s32[1,1,2]{2,1,0:T(1,128)S(1)}, s32[1,1,2]{2,1,0:T(1,128)}, u32[]{:S(2)}) %copy-start.7) | copy-done | bytes 32
  3.4 0.6 %pack_boards.1.after_ref.refs_0_ = s32[2,1664]{1,0:T(2,128)S(1)} custom-call(s32[2]{0:T(128)S(1)} %bitcast.13, s32[2,256]{1,0:T(2,128)S(1)} %bitcast.12, s32[2,1326]{1,0:T(2,128)S(1)} %bitcast.10, s32[2,1326]{1,0:T(2,128)S(1)} %bitcast.11), custom_call_target="tpu_custom_call" | custom-call | tf_op jit(solution)/shard_map/pack_boards/pallas_call | solution.py:92
  4.0 4.0 %collective-permute-start.4 = (s32[2,1664]{1,0:T(2,128)S(1)}, s32[2,1664]{1,0:T(2,128)S(1)}, u32[]{:S(2)}, u32[]{:S(2)}) collective-permute-start(s32[2,1664]{1,0:T(2,128)S(1)} %pack_boards.1.after_ref.refs_0_), channel_id=1, source_target_pairs={{0,5},{1,4},{2,7},{3,6},{4,1},{5,0},{6,3},{7,2},{8,13},{9,12},{10,... | collective-permute-start | bytes 39944 | tf_op jit(solution)/shard_map/ppermute | solution.py:299
  8.0 0.5 %collective-permute-start.3 = (s32[2,1664]{1,0:T(2,128)S(1)}, s32[2,1664]{1,0:T(2,128)S(1)}, u32[]{:S(2)}, u32[]{:S(2)}) collective-permute-start(s32[2,1664]{1,0:T(2,128)S(1)} %pack_boards.1.after_ref.refs_0_), channel_id=1, source_target_pairs={{0,4},{1,5},{2,6},{3,7},{4,0},{5,1},{6,2},{7,3},{8,12},{9,13},{10,... | collective-permute-start | bytes 39944 | tf_op jit(solution)/shard_map/ppermute | solution.py:299
  8.5 0.1 collective-permute-start.2
  8.6 0.0 collective-permute-start.1
  8.6 0.5 %collective-permute-start = (bf16[32,1326]{1,0:T(8,128)(2,1)}, bf16[32,1326]{1,0:T(8,128)(2,1)S(1)}, u32[]{:S(2)}, u32[]{:S(2)}) collective-permute-start(bf16[32,1326]{1,0:T(8,128)(2,1)} %bitcast.14), channel_id=1, source_target_pairs={{0,2},{1,3},{2,0},{3,1},{4,6},{5,7},{6,4},{7,5},{8,10},{9,11},{10,... | collective-permute-start | bytes 254600 | tf_op jit(solution)/shard_map/ppermute | solution.py:299
  9.1 0.1 add_multiply_fusion.base_ref
  9.2 0.0 copy-start
  9.2 2.1 %copy-done = bf16[1328,1408]{1,0:T(8,128)(2,1)S(1)} copy-done((bf16[1328,1408]{1,0:T(8,128)(2,1)S(1)}, bf16[1328,1408]{1,0:T(8,128)(2,1)}, u32[]{:S(2)}) %copy-start) | copy-done | bytes 3739672
  11.3 0.0 copy-start.1
  11.3 1.0 %copy-done.1 = bf16[128,1408]{1,0:T(8,128)(2,1)S(1)} copy-done((bf16[128,1408]{1,0:T(8,128)(2,1)S(1)}, bf16[128,1408]{1,0:T(8,128)(2,1)}, u32[]{:S(2)}) %copy-start.1) | copy-done | bytes 360472
  12.2 0.0 copy-start.2
  12.2 1.0 %copy-done.2 = bf16[1408,128]{1,0:T(8,128)(2,1)S(1)} copy-done((bf16[1408,128]{1,0:T(8,128)(2,1)S(1)}, bf16[1408,128]{1,0:T(8,128)(2,1)}, u32[]{:S(2)}) %copy-start.2) | copy-done | bytes 360472
  13.2 0.0 copy-start.10
  13.2 3.0 %fetch_tables.1 = (bf16[1328,1408]{1,0:T(8,128)(2,1)S(1)}, bf16[1408,128]{1,0:T(8,128)(2,1)S(1)}, bf16[128,1408]{1,0:T(8,128)(2,1)S(1)}) custom-call(s32[2,1664]{1,0:T(2,128)S(1)} %pack_boards.1.after_ref.refs_0_, bf16[1328,1408]{1,0:T(8,128)(2,1)S(1)} %copy-done, bf16[1408,128]{1,0:T(8,128)(2,1)S(1)} %copy-done.2, bf16[128,1408]{1,0:T(8,128)(2,1)S(1)} %copy-done.1), custom_call_target="tpu_custom_call" | custom-call | bytes 8921088 | tf_op jit(solution)/shard_map/fetch_tables/pallas_call | solution.py:114
  16.3 0.0 collective-permute-done.1.mate_kind_ref
  16.3 0.0 collective-permute-done.4.refs_3_
  16.3 0.0 collective-permute-done.3.refs_2_
  16.3 0.0 collective-permute-done.2.refs_1_
  16.3 0.0 collective-permute-done.mate_ref
  16.3 0.0 copy-done.8
  16.3 0.0 copy-done.10
  16.3 0.0 copy-start.3
  16.4 0.0 copy-start.9
  16.4 7.0 %board_sums.1 = (f32[32,1408]{1,0:T(8,128)S(1)}, f32[32,1408]{1,0:T(8,128)S(1)}) custom-call(s32[2]{0:T(128)S(1)} %add_multiply_fusion.base_ref, bf16[32,1326]{1,0:T(8,128)(2,1)S(1)} %bitcast.15, bf16[32,1326]{1,0:T(8,128)(2,1)S(1)} %collective-permute-done.mate_ref, s32[1,32]{1,0:T(1,128)S(1)} %copy-done.8, ...), custom_call_target="tpu_custom_call" | custom-call | flops 2030043136 | tf_op jit(solution)/shard_map/board_sums/pallas_call | solution.py:195
  23.4 0.1 collective-permute-start.5
  23.5 1.4 %collective-permute-done.5.mate_ref = f32[32,1408]{1,0:T(8,128)S(1)} collective-permute-done((f32[32,1408]{1,0:T(8,128)S(1)}, f32[32,1408]{1,0:T(8,128)S(1)}, u32[]{:S(2)}, u32[]{:S(2)}) %collective-permute-start.5) | collective-permute-done | bytes 180256 | tf_op jit(solution)/shard_map/ppermute | solution.py:299
  24.9 0.0 copy-done.3
  24.9 0.0 copy-done.9
  24.9 0.8 %regret_update.1 = (f32[32,1326]{1,0:T(8,128)}, s16[16,1408]{1,0:T(8,128)(2,1)S(1)}) custom-call(f32[32,1408]{1,0:T(8,128)S(1)} %get-tuple-element.12.own_ref, f32[32,1408]{1,0:T(8,128)S(1)} %collective-permute-done.5.mate_ref, s32[1,32]{1,0:T(1,128)S(1)} %copy-done.9, s32[1,32]{1,0:T(1,128)S(1)} %copy-done.8, f32[32,1326]{1,0:T(8,128)S(1)} %bitcast.9), custom_call_target="tpu_custom_call" | custom-call | tf_op jit(solution)/shard_map/regret_update/pallas_call | solution.py:255
  25.8 4.0 %collective-permute-start.8 = (s16[16,1408]{1,0:T(8,128)(2,1)S(1)}, s16[16,1408]{1,0:T(8,128)(2,1)S(1)}, u32[]{:S(2)}, u32[]{:S(2)}) collective-permute-start(s16[16,1408]{1,0:T(8,128)(2,1)S(1)} %get-tuple-element.15.refs_0_), channel_id=1, source_target_pairs={{0,24},{8,16},{16,8},{24,0},{1,25},{9,17},{17,9},{25,1},{2,26},{10... | collective-permute-start | bytes 135176 | tf_op jit(solution)/shard_map/ppermute | solution.py:299
  29.8 0.0 collective-permute-start.7
  29.8 0.6 %collective-permute-start.6 = (s16[16,1408]{1,0:T(8,128)(2,1)S(1)}, s16[16,1408]{1,0:T(8,128)(2,1)S(1)}, u32[]{:S(2)}, u32[]{:S(2)}) collective-permute-start(s16[16,1408]{1,0:T(8,128)(2,1)S(1)} %get-tuple-element.15.refs_0_), channel_id=1, source_target_pairs={{0,8},{8,0},{16,24},{24,16},{1,9},{9,1},{17,25},{25,17},{2,10},{10... | collective-permute-start | bytes 135176 | tf_op jit(solution)/shard_map/ppermute | solution.py:299
  30.3 1.5 %collective-permute-done.8.refs_3_ = s16[16,1408]{1,0:T(8,128)(2,1)S(1)} collective-permute-done((s16[16,1408]{1,0:T(8,128)(2,1)S(1)}, s16[16,1408]{1,0:T(8,128)(2,1)S(1)}, u32[]{:S(2)}, u32[]{:S(2)}) %collective-permute-start.8) | collective-permute-done | bytes 45088 | tf_op jit(solution)/shard_map/ppermute | solution.py:299
  31.9 2.9 %collective-permute-done.7.refs_2_ = s16[16,1408]{1,0:T(8,128)(2,1)S(1)} collective-permute-done((s16[16,1408]{1,0:T(8,128)(2,1)S(1)}, s16[16,1408]{1,0:T(8,128)(2,1)S(1)}, u32[]{:S(2)}, u32[]{:S(2)}) %collective-permute-start.7) | collective-permute-done | bytes 45088 | tf_op jit(solution)/shard_map/ppermute | solution.py:299
  34.7 0.0 collective-permute-done.6.refs_1_
  34.7 0.8 %chance_sum.1 = f32[16,1326]{1,0:T(8,128)} custom-call(s16[16,1408]{1,0:T(8,128)(2,1)S(1)} %get-tuple-element.15.refs_0_, s16[16,1408]{1,0:T(8,128)(2,1)S(1)} %collective-permute-done.6.refs_1_, s16[16,1408]{1,0:T(8,128)(2,1)S(1)} %collective-permute-done.7.refs_2_, s16[16,1408]{1,0:T(8,128)(2,1)S(1)} %collective-permute-done.8.refs_3_), custom_call_target="tpu_custom_call" | custom-call | tf_op jit(solution)/shard_map/chance_sum/pallas_call | solution.py:288
Async XLA Ops:
  0.6 15.7 %copy-start.8 = (s32[1,32]{1,0:T(1,128)S(1)}, s32[1,32]{1,0:T(1,128)}, u32[]{:S(2)}) copy-start(s32[1,32]{1,0:T(1,128)} %kind_ref.1) | copy-start | bytes 388
  0.6 0.7 %copy-start.4 = (s32[1,1,2,1326]{3,2,1,0:T(2,128)S(1)}, s32[1,1,2,1326]{3,2,1,0:T(2,128)}, u32[]{:S(2)}) copy-start(s32[1,1,2,1326]{3,2,1,0:T(2,128)} %param.17) | copy-start | bytes 31828
  1.4 0.7 %copy-start.5 = (s32[1,1,2,1326]{3,2,1,0:T(2,128)S(1)}, s32[1,1,2,1326]{3,2,1,0:T(2,128)}, u32[]{:S(2)}) copy-start(s32[1,1,2,1326]{3,2,1,0:T(2,128)} %param.18) | copy-start | bytes 31828
  2.1 0.7 %copy-start.6 = (s32[1,1,2,256]{3,2,1,0:T(2,128)S(1)}, s32[1,1,2,256]{3,2,1,0:T(2,128)}, u32[]{:S(2)}) copy-start(s32[1,1,2,256]{3,2,1,0:T(2,128)} %param.15) | copy-start | bytes 6148
  2.7 0.7 %copy-start.7 = (s32[1,1,2]{2,1,0:T(1,128)S(1)}, s32[1,1,2]{2,1,0:T(1,128)}, u32[]{:S(2)}) copy-start(s32[1,1,2]{2,1,0:T(1,128)} %param.16) | copy-start | bytes 28
  4.0 12.3 %collective-permute-start.4 = (s32[2,1664]{1,0:T(2,128)S(1)}, s32[2,1664]{1,0:T(2,128)S(1)}, u32[]{:S(2)}, u32[]{:S(2)}) collective-permute-start(s32[2,1664]{1,0:T(2,128)S(1)} %pack_boards.1.after_ref.refs_0_), channel_id=1, source_target_pairs={{0,5},{1,4},{2,7},{3,6},{4,1},{5,0},{6,3},{7,2},{8,13},{9,12},{10,... | collective-permute-start | bytes 39944 | tf_op jit(solution)/shard_map/ppermute | solution.py:299
  8.0 8.3 %collective-permute-start.3 = (s32[2,1664]{1,0:T(2,128)S(1)}, s32[2,1664]{1,0:T(2,128)S(1)}, u32[]{:S(2)}, u32[]{:S(2)}) collective-permute-start(s32[2,1664]{1,0:T(2,128)S(1)} %pack_boards.1.after_ref.refs_0_), channel_id=1, source_target_pairs={{0,4},{1,5},{2,6},{3,7},{4,0},{5,1},{6,2},{7,3},{8,12},{9,13},{10,... | collective-permute-start | bytes 39944 | tf_op jit(solution)/shard_map/ppermute | solution.py:299
  8.5 7.8 %collective-permute-start.2 = (s32[2,1664]{1,0:T(2,128)S(1)}, s32[2,1664]{1,0:T(2,128)S(1)}, u32[]{:S(2)}, u32[]{:S(2)}) collective-permute-start(s32[2,1664]{1,0:T(2,128)S(1)} %pack_boards.1.after_ref.refs_0_), channel_id=1, source_target_pairs={{0,1},{1,0},{2,3},{3,2},{4,5},{5,4},{6,7},{7,6},{8,9},{9,8},{10,11... | collective-permute-start | bytes 39944 | tf_op jit(solution)/shard_map/ppermute | solution.py:299
  8.6 7.7 %collective-permute-start.1 = (s32[1,32]{1,0:T(1,128)}, s32[1,32]{1,0:T(1,128)S(1)}, u32[]{:S(2)}, u32[]{:S(2)}) collective-permute-start(s32[1,32]{1,0:T(1,128)} %kind_ref.1), channel_id=1, source_target_pairs={{0,2},{1,3},{2,0},{3,1},{4,6},{5,7},{6,4},{7,5},{8,10},{9,11},{10,... | collective-permute-start | bytes 392 | tf_op jit(solution)/shard_map/ppermute | solution.py:299
  8.6 7.7 %collective-permute-start = (bf16[32,1326]{1,0:T(8,128)(2,1)}, bf16[32,1326]{1,0:T(8,128)(2,1)S(1)}, u32[]{:S(2)}, u32[]{:S(2)}) collective-permute-start(bf16[32,1326]{1,0:T(8,128)(2,1)} %bitcast.14), channel_id=1, source_target_pairs={{0,2},{1,3},{2,0},{3,1},{4,6},{5,7},{6,4},{7,5},{8,10},{9,11},{10,... | collective-permute-start | bytes 254600 | tf_op jit(solution)/shard_map/ppermute | solution.py:299
  9.2 2.1 %copy-start = (bf16[1328,1408]{1,0:T(8,128)(2,1)S(1)}, bf16[1328,1408]{1,0:T(8,128)(2,1)}, u32[]{:S(2)}) copy-start(bf16[1328,1408]{1,0:T(8,128)(2,1)} %constant.19.clone.refs_0_) | copy-start | bytes 11218948
  11.3 1.0 %copy-start.1 = (bf16[128,1408]{1,0:T(8,128)(2,1)S(1)}, bf16[128,1408]{1,0:T(8,128)(2,1)}, u32[]{:S(2)}) copy-start(bf16[128,1408]{1,0:T(8,128)(2,1)} %constant.21.clone.refs_2_) | copy-start | bytes 1081348
  12.2 1.0 %copy-start.2 = (bf16[1408,128]{1,0:T(8,128)(2,1)S(1)}, bf16[1408,128]{1,0:T(8,128)(2,1)}, u32[]{:S(2)}) copy-start(bf16[1408,128]{1,0:T(8,128)(2,1)} %constant.20.clone.refs_1_) | copy-start | bytes 1081348
  13.2 3.1 %copy-start.10 = (bf16[1,32,1326]{2,1,0:T(8,128)(2,1)S(1)}, bf16[1,32,1326]{2,1,0:T(8,128)(2,1)}, u32[]{:S(2)}) copy-start(bf16[1,32,1326]{2,1,0:T(8,128)(2,1)} %param.12) | copy-start | bytes 254596
  16.3 8.6 %copy-start.3 = (f32[1,32,1326]{2,1,0:T(8,128)S(1)}, f32[1,32,1326]{2,1,0:T(8,128)}, u32[]{:S(2)}) copy-start(f32[1,32,1326]{2,1,0:T(8,128)} %param.11) | copy-start | bytes 509188
  16.4 8.6 %copy-start.9 = (s32[1,32]{1,0:T(1,128)S(1)}, s32[1,32]{1,0:T(1,128)}, u32[]{:S(2)}) copy-start(s32[1,32]{1,0:T(1,128)} %pot_ref.1) | copy-start | bytes 388
  23.4 1.5 %collective-permute-start.5 = (f32[32,1408]{1,0:T(8,128)S(1)}, f32[32,1408]{1,0:T(8,128)S(1)}, u32[]{:S(2)}, u32[]{:S(2)}) collective-permute-start(f32[32,1408]{1,0:T(8,128)S(1)} %get-tuple-element.13), channel_id=1, source_target_pairs={{0,2},{1,3},{2,0},{3,1},{4,6},{5,7},{6,4},{7,5},{8,10},{9,11},{10,... | collective-permute-start | bytes 540680 | tf_op jit(solution)/shard_map/ppermute | solution.py:299
  25.8 6.1 %collective-permute-start.8 = (s16[16,1408]{1,0:T(8,128)(2,1)S(1)}, s16[16,1408]{1,0:T(8,128)(2,1)S(1)}, u32[]{:S(2)}, u32[]{:S(2)}) collective-permute-start(s16[16,1408]{1,0:T(8,128)(2,1)S(1)} %get-tuple-element.15.refs_0_), channel_id=1, source_target_pairs={{0,24},{8,16},{16,8},{24,0},{1,25},{9,17},{17,9},{25,1},{2,26},{10... | collective-permute-start | bytes 135176 | tf_op jit(solution)/shard_map/ppermute | solution.py:299
  29.8 4.9 %collective-permute-start.7 = (s16[16,1408]{1,0:T(8,128)(2,1)S(1)}, s16[16,1408]{1,0:T(8,128)(2,1)S(1)}, u32[]{:S(2)}, u32[]{:S(2)}) collective-permute-start(s16[16,1408]{1,0:T(8,128)(2,1)S(1)} %get-tuple-element.15.refs_0_), channel_id=1, source_target_pairs={{0,16},{8,24},{16,0},{24,8},{1,17},{9,25},{17,1},{25,9},{2,18},{10... | collective-permute-start | bytes 135176 | tf_op jit(solution)/shard_map/ppermute | solution.py:299
  29.8 4.9 %collective-permute-start.6 = (s16[16,1408]{1,0:T(8,128)(2,1)S(1)}, s16[16,1408]{1,0:T(8,128)(2,1)S(1)}, u32[]{:S(2)}, u32[]{:S(2)}) collective-permute-start(s16[16,1408]{1,0:T(8,128)(2,1)S(1)} %get-tuple-element.15.refs_0_), channel_id=1, source_target_pairs={{0,8},{8,0},{16,24},{24,16},{1,9},{9,1},{17,25},{25,17},{2,10},{10... | collective-permute-start | bytes 135176 | tf_op jit(solution)/shard_map/ppermute | solution.py:299

commit v4 on v2

--- a/solution.py
+++ b/solution.py
@@ -19,8 +19,8 @@
 UNROLL = 8
 STEPS = 32767.0
 LOWEST = 100
+TABLE_TYPE = jnp.int8
 WHOLE = pl.BlockSpec(memory_space=pltpu.VMEM)
-SCALARS = pl.BlockSpec(memory_space=pltpu.SMEM)
 
 floor_share = 0.1
 
@@ -38,7 +38,7 @@
 
 
 @functools.cache
-def tables(hand_count):
+def table(hand_count):
     wide, deep = up(hand_count, LANE), up(hand_count, 16)
     first, second = np.triu_indices(CARDS, 1)
     cards = np.zeros((hand_count, CARDS), np.float32)
@@ -46,16 +46,11 @@
     cards[np.arange(hand_count), second] = 1
     apart = np.zeros((deep, wide), np.float32)
     apart[:hand_count, :hand_count] = (cards @ cards.T) == 0
-    sums = np.concatenate([np.ones((hand_count, 1), np.float32), cards], axis=1)
-    parts = sums.shape[1]
-    collect = np.zeros((wide, LANE), np.float32)
-    spread = np.zeros((LANE, wide), np.float32)
-    signed = sums.copy()
-    signed[:, 1:] *= -1
-    for copy in range(2):
-        collect[:hand_count, copy * parts : (copy + 1) * parts] = sums
-        spread[copy * parts : (copy + 1) * parts, :hand_count] = signed.T
-    return [table.astype(jnp.bfloat16) for table in (apart, collect, spread)]
+    sums = np.zeros((LANE, wide), np.float32)
+    for first in (0, 1 + CARDS):
+        sums[first, :hand_count] = 1
+        sums[first + 1 : first + 1 + CARDS, :hand_count] = cards.T
+    return np.concatenate([apart, sums]).astype(TABLE_TYPE)
 
 
 def as_column(row):
@@ -64,70 +59,114 @@
     return jnp.sum(jnp.where(at, row.astype(jnp.float32), 0.0), axis=1, keepdims=True)
 
 
-def pack_kernel(hand_count, count_ref, slots_ref, ranks_ref, live_ref, out_ref):
-    wide = up(hand_count, LANE)
-    boards = out_ref.shape[0]
-    out_ref[:, wide - LANE : wide] = jnp.zeros((boards, LANE), jnp.int32)
-    out_ref[:, :hand_count] = ranks_ref[...] + RANK_SPAN * live_ref[...]
-    slot = lax.broadcasted_iota(jnp.int32, (1, slots_ref.shape[1]), 1)
-    for board in range(boards):
-        lines = slots_ref[board : board + 1]
-        out_ref[board : board + 1, wide:] = jnp.where(slot < count_ref[board], lines, -1)
-
-
-def pack(counts, slots, ranks, live):
-    hand_count = ranks.shape[1]
-    return pl.pallas_call(
-        functools.partial(pack_kernel, hand_count),
-        out_shape=jax.ShapeDtypeStruct((slots.shape[0], up(hand_count, LANE) + slots.shape[1]), jnp.int32),
-        in_specs=[SCALARS] + [WHOLE] * 3,
+def copy_all(pairs, sems):
+    copies = [pltpu.make_async_copy(source, target, sems.at[at]) for at, (source, target) in enumerate(pairs)]
+    for copy in copies:
+        copy.start()
+    for copy in copies:
+        copy.wait()
+
+
+def bases_kernel(line_count, core, out_ref):
+    index = lax.axis_index("turn") * lax.axis_size("river") + lax.axis_index("river")
+    lane = lax.broadcasted_iota(jnp.int32, out_ref.shape, 1)
+    line = jnp.where(lane == LANE // 2, index, index ^ core) * line_count
+    out_ref[...] = jnp.where((lane == LANE // 2) | (lane == LANE // 2 + 1), line, 0)
+
+
+def first_lines(line_count, core):
+    return pl.pallas_call(
+        functools.partial(bases_kernel, line_count, core),
+        out_shape=jax.ShapeDtypeStruct((1, LANE), jnp.int32),
         out_specs=WHOLE,
         compiler_params=params(4),
-        name="pack_boards",
-    )(counts, slots, ranks, live)
-
-
-def fetch_kernel(after_ref, table_ref, out_ref, sem):
-    copy = pltpu.make_async_copy(table_ref, out_ref, sem)
-    copy.start()
-    copy.wait()
-
-
-def fetch(table, after):
-    return pl.pallas_call(
-        fetch_kernel,
-        out_shape=jax.ShapeDtypeStruct(table.shape, table.dtype),
-        in_specs=[WHOLE, pl.BlockSpec(memory_space=pl.ANY)],
-        out_specs=WHOLE,
-        scratch_shapes=[pltpu.SemaphoreType.DMA],
-        compiler_params=params(8),
-        name="fetch_table",
-        cost_estimate=pl.CostEstimate(flops=0, bytes_accessed=2 * table.size * 2, transcendentals=0),
+        name="first_lines",
+        cost_estimate=pl.CostEstimate(flops=20 * 10**9, bytes_accessed=0, transcendentals=0),
+    )()
+
+
+def pack(counts, slots, ranks, live, kinds, bases):
+    hand_count, slot_count, boards = ranks.shape[1], slots.shape[1], ranks.shape[0]
+    wide = up(hand_count, LANE)
+
+    def place(array, first):
+        after = wide + slot_count + LANE - first - array.shape[1]
+        return jnp.pad(array, ((0, boards - array.shape[0]), (first, after)))
+
+    packed = place(ranks, 0) + RANK_SPAN * place(live, 0) + place(slots, wide) + place(kinds, wide + slot_count)
+    packed += place(bases, wide + slot_count)
+    lane = lax.broadcasted_iota(jnp.int32, packed.shape, 1)
+    return jnp.where(lane == wide - 1, lax.broadcast_in_dim(counts, packed.shape, (0,)), packed)
+
+
+def unpack_kernel(after_ref, table_ref, apart_ref, collect_ref, spread_ref):
+    deep = apart_ref.shape[0]
+    apart_ref[...] = table_ref[:deep].astype(jnp.bfloat16)
+    cards = table_ref[deep:].astype(jnp.float32)
+    spread_ref[...] = cards.astype(jnp.bfloat16)
+    row = lax.broadcasted_iota(jnp.int32, (LANE, 1), 0)
+    signed = jnp.where((row == 0) | (row == 1 + CARDS), cards, -cards)
+    collect_ref[...] = jnp.transpose(signed).astype(jnp.bfloat16)
+
+
+def unpack(table, after):
+    deep, wide = table.shape[0] - LANE, table.shape[1]
+    return pl.pallas_call(
+        unpack_kernel,
+        out_shape=[jax.ShapeDtypeStruct(shape, jnp.bfloat16) for shape in ((deep, wide), (wide, LANE), (LANE, wide))],
+        in_specs=[WHOLE] * 2,
+        out_specs=[WHOLE] * 3,
+        compiler_params=params(12),
+        name="unpack_tables",
+        cost_estimate=pl.CostEstimate(flops=4 * 10**9, bytes_accessed=3 * table.size, transcendentals=0),
     )(after, table)
 
 
-def boards_kernel(hand_count, line_count, base_ref, own_ref, mate_ref, own_kind_ref, mate_kind_ref, *refs, boards_in):
-    board_refs, refs = refs[:boards_in], refs[boards_in:]
-    apart_ref, collect_ref, spread_ref, own_out, mate_out, column_ref, board_ref, reach_ref = refs
-    wide = up(hand_count, LANE)
-    deep = apart_ref.shape[0]
+def lines_kernel(hand_count, line_count, own_ref, mate_ref, mate_kind_ref, packed_ref, reach_ref, line_ref):
     rows = own_ref.shape[0]
-    parts = 1 + CARDS
+    first = packed_ref.shape[1] - LANE
+    base = packed_ref[:1, first + LANE // 2 : first + LANE // 2 + 2]
     reach_ref[...] = jnp.zeros_like(reach_ref)
     reach_ref[:rows, :hand_count] = own_ref[...]
     reach_ref[rows:, :hand_count] = mate_ref[...]
-    kind = jnp.concatenate([as_column(own_kind_ref[...]), as_column(mate_kind_ref[...])], axis=0)
+    own_kind = as_column(packed_ref[:1, first : first + rows])
+    kind = jnp.concatenate([own_kind, as_column(mate_kind_ref[...])], axis=0)
     row = lax.broadcasted_iota(jnp.int32, (2 * rows, 1), 0)
     within = jnp.where(row < rows, row, row - rows)
-    line = jnp.where(row < rows, base_ref[0], base_ref[1]) + within
+    line = jnp.where(row < rows, base[:, :1], base[:, 1:]) + within
     line = jnp.where(within < line_count, line, -2)
-    lane = lax.broadcasted_iota(jnp.int32, (2 * rows, LANE), 1)
+    lane = lax.broadcasted_iota(jnp.int32, line_ref.shape, 1)
+    line_ref[...] = jnp.where(lane == 0, line, kind.astype(jnp.int32))
+
+
+def first_kernel(hand_count, line_count, own_ref, mate_ref, mate_kind_ref, *refs):
+    tables, (packed_ref, own_out, mate_out, reach_ref, line_ref), scratch = refs[:3], refs[3:8], refs[8:]
+    lines_kernel(hand_count, line_count, own_ref, mate_ref, mate_kind_ref, packed_ref, reach_ref, line_ref)
     own_out[...] = jnp.zeros_like(own_out)
     mate_out[...] = jnp.zeros_like(mate_out)
-    board_total = 0
-    for ref in board_refs:
-        board_ref[board_total : board_total + ref.shape[0]] = ref[...]
-        board_total += ref.shape[0]
+    add_boards(reach_ref, line_ref, *tables, packed_ref, own_out, mate_out, *scratch)
+
+
+def second_kernel(reach_ref, line_ref, *refs):
+    tables, (packed_ref, own_ref, mate_ref, own_out, mate_out), scratch = refs[:3], refs[3:8], refs[8:]
+    own_out[...] = own_ref[...]
+    mate_out[...] = mate_ref[...]
+    add_boards(reach_ref, line_ref, *tables, packed_ref, own_out, mate_out, *scratch)
+
+
+def add_boards(
+    reach_ref, line_ref, apart_ref, collect_ref, spread_ref, packed_ref, own_out, mate_out, column_ref, board_ref
+):
+    wide, deep = apart_ref.shape[1], apart_ref.shape[0]
+    rows = own_out.shape[0]
+    parts = 1 + CARDS
+    line, kind = line_ref[:, :1], line_ref[:, 1:2]
+    lane = lax.broadcasted_iota(jnp.int32, (2 * rows, LANE), 1)
+    board_total = packed_ref.shape[0]
+    end = packed_ref.shape[1] - LANE
+    slot = lax.broadcasted_iota(jnp.int32, (board_total, end - wide), 1)
+    board_ref[:, :wide] = packed_ref[:, :wide]
+    board_ref[:, wide:] = jnp.where(slot < packed_ref[:, wide - 1 : wide], packed_ref[:, wide:end], -1)
 
     def add_board(board):
         keys = board_ref[pl.ds(board, 1), :wide]
@@ -169,24 +208,24 @@
         pl.loop(0, board_total)(add_board)
 
 
-def board_sums(hand_count, line_count, base, reach, kinds, boards, apart, collect, spread):
-    rows, wide = reach[0].shape[0], up(hand_count, LANE)
-    out = jax.ShapeDtypeStruct((rows, wide), jnp.float32)
-    total = sum(board.shape[0] for board in boards)
-    return pl.pallas_call(
-        functools.partial(boards_kernel, hand_count, line_count, boards_in=len(boards)),
-        out_shape=(out, out),
-        in_specs=[SCALARS] + [WHOLE] * (7 + len(boards)),
-        out_specs=(WHOLE, WHOLE),
+def board_sums(kernel, name, rows, inputs, tables, boards, sums=(), more=()):
+    deep, wide = tables[0].shape
+    out = [jax.ShapeDtypeStruct((rows, wide), jnp.float32)] * 2 + list(more)
+    return pl.pallas_call(
+        kernel,
+        out_shape=out,
+        in_specs=[WHOLE] * (len(inputs) + len(tables) + 1 + len(sums)),
+        out_specs=[WHOLE] * len(out),
         scratch_shapes=[
-            pltpu.VMEM((apart.shape[0], LANE), jnp.bfloat16),
-            pltpu.VMEM((total, boards[0].shape[1]), jnp.int32),
-            pltpu.VMEM((2 * rows, wide), jnp.bfloat16),
+            pltpu.VMEM((deep, LANE), jnp.bfloat16),
+            pltpu.VMEM((boards.shape[0], boards.shape[1] - LANE), jnp.int32),
         ],
         compiler_params=params(32),
-        name="board_sums",
-        cost_estimate=pl.CostEstimate(flops=4 * total * rows * wide * wide, bytes_accessed=0, transcendentals=0),
-    )(base, *reach, *kinds, *boards, apart, collect, spread)
+        name=name,
+        cost_estimate=pl.CostEstimate(
+            flops=4 * boards.shape[0] * rows * wide * wide, bytes_accessed=0, transcendentals=0
+        ),
+    )(*inputs, *tables, boards, *sums)
 
 
 def powers():
@@ -290,33 +329,41 @@
     core = lax.axis_size("river")
     board_total = group_size * board_lines.shape[2]
     extra = up(line_count, SUB) - line_count
-    apart, collect, spread = [jnp.asarray(table) for table in tables(hand_count)]
-
-    boards = pack(board_count[0, 0], board_lines[0, 0], hand_ranks[0, 0], live_hands[0, 0])
-    masks = [mask for mask in range(1, group_size) if not mask & core]
-    if len(masks) < 4:
-        parts = [boards] + [swap(boards, group, mask) for mask in masks]
-    else:
-        parts = boards
-        for mask in masks:
-            if mask & (mask - 1) == 0:
-                parts = jnp.concatenate([parts, swap(parts, group, mask)], axis=0)
-        parts = [parts]
+    bases = first_lines(line_count, core)
+    kinds = jnp.pad(line_kind, ((0, 0), (0, extra)))
+    boards = pack(board_count[0, 0], board_lines[0, 0], hand_ranks[0, 0], live_hands[0, 0], kinds, bases)
+    held, arrived = boards, boards
+    for bit in range(group_size.bit_length() - 1):
+        mask = 1 << bit
+        if mask != core:
+            held = boards if mask == 1 else jnp.concatenate([held, arrived], axis=0)
+            arrived = swap(held, group, mask)
     reach = jnp.pad(opp_reach[0], ((0, extra), (0, 0)))
-    kinds = jnp.pad(line_kind, ((0, 0), (0, extra)))
     pots = jnp.pad(pot_size, ((0, 0), (0, extra)))
-    held = jnp.pad(regrets[0], ((0, extra), (0, 0)))
+    old_regrets = jnp.pad(regrets[0], ((0, extra), (0, 0)))
     mate_reach, mate_kinds = swap(reach, group, core), swap(kinds, group, core)
-    apart = fetch(apart, boards)
-    index = lax.axis_index(group)
-    base = jnp.stack([index, index ^ core]).astype(jnp.int32) * line_count
+    held_tables = unpack(jnp.asarray(table(hand_count)), boards)
+    rows, wide = reach.shape[0], up(hand_count, LANE)
+    own, for_mate, all_reach, lines = board_sums(
+        functools.partial(first_kernel, hand_count, line_count),
+        "first_boards",
+        rows,
+        (reach, mate_reach, mate_kinds),
+        held_tables,
+        held,
+        more=(
+            jax.ShapeDtypeStruct((2 * rows, wide), jnp.bfloat16),
+            jax.ShapeDtypeStruct((2 * rows, LANE), jnp.int32),
+        ),
+    )
     own, for_mate = board_sums(
-        hand_count, line_count, base, (reach, mate_reach), (kinds, mate_kinds), parts, apart, collect, spread
+        second_kernel, "second_boards", rows, (all_reach, lines), held_tables, arrived, (own, for_mate)
     )
     mate = swap(for_mate, group, core)
-    updated, codes = update(hand_count, 1.0 / (board_total * hand_count), own, mate, pots, kinds, held)
+    updated, codes = update(hand_count, 1.0 / (board_total * hand_count), own, mate, pots, kinds, old_regrets)
     flops = lax.axis_size("flop")
-    total = chance(hand_count, [codes] + [swap(codes, "flop", mask) for mask in range(1, flops)])
+    arrived = {mask: swap(codes, "flop", mask) for mask in (flops - 1, *range(1, flops - 1))}
+    total = chance(hand_count, [codes] + [arrived[mask] for mask in range(1, flops)])
     return (updated[None, :line_count], total[: line_count // ACTS])
 
 

time: 31.8 us -> 27.2 us (0.86)
  local copies, waits for them, and re-layouts: 5.04 us -> 0.33 us
  Pallas kernels: 9.54 us -> 8.97 us
  waiting for transfers between devices: 6.29 us -> 6.85 us
    unnamed x22 -> x18, local copies, waits for them, and re-layouts: 5.04 us -> 0.33 us
    pallas_call x3 -> x4, Pallas kernels: 7.88 us -> 7.31 us  [the longest x2 6.9 us: board_sums(): pl.pallas_call(kernel, out_shape=out, in_specs=[WHOLE] * (len(inputs) + l...]
    ppermute x9 -> x8, waiting for transfers between devices: 6.29 us -> 6.85 us  [swap(): lax.ppermute(array, axes, [(index, index ^ mask) for index in range(lax.a...]
    ppermute x9 -> x8, starting transfers between devices: 9.75 us -> 10 us  [swap(): lax.ppermute(array, axes, [(index, index ^ mask) for index in range(lax.a...]
  transfers between devices with their start and end apart: 9 -> 8, of which waited for: 4 -> 4; matrix products, arithmetic and copies ran while one was open for 0% -> 0% of each run, Pallas kernels for 1% -> 15%
where the time goes in v4:
time: 27.2 us; the launch traced here: 27 us
  starting transfers between devices  10 us (37%)
  Pallas kernels  8.97 us (33%)
  waiting for transfers between devices  6.85 us (25%)
  between operations  0.76 us (3%)
  local copies, waits for them, and re-layouts  0.33 us (1%)
    ppermute x8, starting transfers between devices, swap(): lax.ppermute(array, axes, [(index, index ^ mask) for index in range(lax.a...  10 us
    pallas_call x2, Pallas kernels, board_sums(): pl.pallas_call(kernel, out_shape=out, in_specs=[WHOLE] * (len(inputs) + l...  6.9 us
    ppermute x8, waiting for transfers between devices, swap(): lax.ppermute(array, axes, [(index, index ^ mask) for index in range(lax.a...  6.85 us
    pallas_call x1, Pallas kernels, update(): pl.pallas_call(functools.partial(update_kernel, hand_count, scale), out_s...  0.84 us
    pallas_call x1, Pallas kernels, chance(): pl.pallas_call(functools.partial(chance_kernel, hand_count), out_shape=ja...  0.81 us
  transfers between devices with their start and end apart: 8, of which 4 were waited for; matrix products, arithmetic and copies ran while one was open for 0% of the time, Pallas kernels for 15%

profile of v4, /device:TPU:0, one launch (start us, length us, event | category | flops | bytes accessed | tf_op | source)
XLA Modules:
  0.0 27.0 jit_solution(2097454815898050880)
XLA Ops:
  0.6 0.0 copy-start.4
  0.6 0.0 copy-start.2
  0.7 0.0 copy-start.5
  0.7 0.0 copy-start.6
  0.7 0.0 copy-start.8
  0.7 0.0 copy-start.7
  0.7 0.0 copy-start.1
  0.7 0.5 %collective-permute-start.1 = (s32[1,32]{1,0:T(1,128)}, s32[1,32]{1,0:T(1,128)S(1)}, u32[]{:S(2)}, u32[]{:S(2)}) collective-permute-start(s32[1,32]{1,0:T(1,128)} %kind_ref.1), channel_id=1, source_target_pairs={{0,2},{1,3},{2,0},{3,1},{4,6},{5,7},{6,4},{7,5},{8,10},{9,11},{10,... | collective-permute-start | bytes 392 | tf_op jit(solution)/shard_map/ppermute | solution.py:319
  1.2 0.2 copy-done.2
  1.4 0.1 copy-done.5
  1.5 0.0 copy-done.6
  1.5 0.0 copy-done.8
  1.5 0.0 copy-done.7
  1.5 0.1 add_select_fusion.after_ref
  1.6 3.0 %collective-permute-start.2 = (s32[2,1792]{1,0:T(2,128)S(1)}, s32[2,1792]{1,0:T(2,128)S(1)}, u32[]{:S(2)}, u32[]{:S(2)}) collective-permute-start(s32[2,1792]{1,0:T(2,128)S(1)} %add_select_fusion.after_ref), channel_id=1, source_target_pairs={{0,1},{1,0},{2,3},{3,2},{4,5},{5,4},{6,7},{7,6},{8,9},{9,8},{10,11... | collective-permute-start | bytes 43016 | tf_op jit(solution)/shard_map/ppermute | solution.py:319
  4.6 0.0 copy-done.1
  4.6 0.0 collective-permute-start
  4.6 0.0 copy-done.4
  4.6 0.4 %unpack_tables.1 = (bf16[1328,1408]{1,0:T(8,128)(2,1)S(1)}, bf16[1408,128]{1,0:T(8,128)(2,1)S(1)}, bf16[128,1408]{1,0:T(8,128)(2,1)S(1)}) custom-call(s32[2,1792]{1,0:T(2,128)S(1)} %add_select_fusion.after_ref, s8[1456,1408]{1,0:T(8,128)(4,1)S(1)} %copy-done.4), custom_call_target="tpu_custom_call" | custom-call | flops 4000000000 | bytes 6150144 | tf_op jit(solution)/shard_map/unpack_tables/pallas_call | solution.py:114
  5.0 1.3 %collective-permute-done.2 = s32[2,1792]{1,0:T(2,128)S(1)} collective-permute-done((s32[2,1792]{1,0:T(2,128)S(1)}, s32[2,1792]{1,0:T(2,128)S(1)}, u32[]{:S(2)}, u32[]{:S(2)}) %collective-permute-start.2) | collective-permute-done | bytes 14368 | tf_op jit(solution)/shard_map/ppermute | solution.py:319
  6.3 2.1 %collective-permute-start.3 = (s32[4,1792]{1,0:T(4,128)S(1)}, s32[4,1792]{1,0:T(4,128)S(1)}, u32[]{:S(2)}, u32[]{:S(2)}) collective-permute-start(s32[4,1792]{1,0:T(4,128)S(1)} %pad_add_fusion.refs_3_), channel_id=1, source_target_pairs={{0,4},{1,5},{2,6},{3,7},{4,0},{5,1},{6,2},{7,3},{8,12},{9,13},{10,... | collective-permute-start | bytes 86024 | tf_op jit(solution)/shard_map/ppermute | solution.py:319
  8.4 0.0 collective-permute-done.1.mate_kind_ref
  8.4 0.0 collective-permute-done.mate_ref
  8.4 0.0 copy-start
  8.4 0.0 copy-start.3
  8.4 3.5 %first_boards.1 = (f32[32,1408]{1,0:T(8,128)S(1)}, f32[32,1408]{1,0:T(8,128)S(1)}, bf16[64,1408]{1,0:T(8,128)(2,1)S(1)}, s32[64,128]{1,0:T(8,128)S(1)}) custom-call(bf16[32,1326]{1,0:T(8,128)(2,1)S(1)} %bitcast.9, bf16[32,1326]{1,0:T(8,128)(2,1)S(1)} %collective-permute-done.mate_ref, s32[1,32]{1,0:T(1,128)S(1)} %collective-permute-done.1.mate_kind_ref, ...), custom_call_target="tpu_custom_call" | custom-call | flops 1015021568 | tf_op jit(solution)/shard_map/first_boards/pallas_call | solution.py:214
  11.9 0.0 collective-permute-done.3.refs_3_
  12.0 3.4 %second_boards.1 = (f32[32,1408]{1,0:T(8,128)S(1)}, f32[32,1408]{1,0:T(8,128)S(1)}) custom-call(bf16[64,1408]{1,0:T(8,128)(2,1)S(1)} %get-tuple-element.16.reach_ref, s32[64,128]{1,0:T(8,128)S(1)} %get-tuple-element.17.line_ref, bf16[1328,1408]{1,0:T(8,128)(2,1)S(1)} %get-tuple-element.13.refs_0_, bf16[1408,128]{1,0:T(8,128)(2,1)S(1)} %get-tuple-element.14.refs_1_, ...), custom_call_target="tpu_custom_call" | custom-call | flops 1015021568 | tf_op jit(solution)/shard_map/second_boards/pallas_call | solution.py:214
  15.3 0.1 collective-permute-start.4
  15.4 1.4 %collective-permute-done.4.mate_ref = f32[32,1408]{1,0:T(8,128)S(1)} collective-permute-done((f32[32,1408]{1,0:T(8,128)S(1)}, f32[32,1408]{1,0:T(8,128)S(1)}, u32[]{:S(2)}, u32[]{:S(2)}) %collective-permute-start.4) | collective-permute-done | bytes 180256 | tf_op jit(solution)/shard_map/ppermute | solution.py:319
  16.8 0.0 copy-done
  16.8 0.0 copy-done.3
  16.8 0.8 %regret_update.1 = (f32[32,1326]{1,0:T(8,128)}, s16[16,1408]{1,0:T(8,128)(2,1)S(1)}) custom-call(f32[32,1408]{1,0:T(8,128)S(1)} %get-tuple-element.20.own_ref, f32[32,1408]{1,0:T(8,128)S(1)} %collective-permute-done.4.mate_ref, s32[1,32]{1,0:T(1,128)S(1)} %copy-done.3, s32[1,32]{1,0:T(1,128)S(1)} %copy-done.2, f32[32,1326]{1,0:T(8,128)S(1)} %bitcast.7), custom_call_target="tpu_custom_call" | custom-call | tf_op jit(solution)/shard_map/regret_update/pallas_call | solution.py:275
  17.7 3.6 %collective-permute-start.7 = (s16[16,1408]{1,0:T(8,128)(2,1)S(1)}, s16[16,1408]{1,0:T(8,128)(2,1)S(1)}, u32[]{:S(2)}, u32[]{:S(2)}) collective-permute-start(s16[16,1408]{1,0:T(8,128)(2,1)S(1)} %get-tuple-element.23.refs_0_), channel_id=1, source_target_pairs={{0,24},{8,16},{16,8},{24,0},{1,25},{9,17},{17,9},{25,1},{2,26},{10... | collective-permute-start | bytes 135176 | tf_op jit(solution)/shard_map/ppermute | solution.py:319
  21.3 0.0 collective-permute-start.6
  21.3 0.8 %collective-permute-start.5 = (s16[16,1408]{1,0:T(8,128)(2,1)S(1)}, s16[16,1408]{1,0:T(8,128)(2,1)S(1)}, u32[]{:S(2)}, u32[]{:S(2)}) collective-permute-start(s16[16,1408]{1,0:T(8,128)(2,1)S(1)} %get-tuple-element.23.refs_0_), channel_id=1, source_target_pairs={{0,8},{8,0},{16,24},{24,16},{1,9},{9,1},{17,25},{25,17},{2,10},{10... | collective-permute-start | bytes 135176 | tf_op jit(solution)/shard_map/ppermute | solution.py:319
  22.1 1.5 %collective-permute-done.7.refs_3_ = s16[16,1408]{1,0:T(8,128)(2,1)S(1)} collective-permute-done((s16[16,1408]{1,0:T(8,128)(2,1)S(1)}, s16[16,1408]{1,0:T(8,128)(2,1)S(1)}, u32[]{:S(2)}, u32[]{:S(2)}) %collective-permute-start.7) | collective-permute-done | bytes 45088 | tf_op jit(solution)/shard_map/ppermute | solution.py:319
  23.6 2.7 %collective-permute-done.6.refs_2_ = s16[16,1408]{1,0:T(8,128)(2,1)S(1)} collective-permute-done((s16[16,1408]{1,0:T(8,128)(2,1)S(1)}, s16[16,1408]{1,0:T(8,128)(2,1)S(1)}, u32[]{:S(2)}, u32[]{:S(2)}) %collective-permute-start.6) | collective-permute-done | bytes 45088 | tf_op jit(solution)/shard_map/ppermute | solution.py:319
  26.2 0.0 collective-permute-done.5.refs_1_
  26.2 0.8 %chance_sum.1 = f32[16,1326]{1,0:T(8,128)} custom-call(s16[16,1408]{1,0:T(8,128)(2,1)S(1)} %get-tuple-element.23.refs_0_, s16[16,1408]{1,0:T(8,128)(2,1)S(1)} %collective-permute-done.5.refs_1_, s16[16,1408]{1,0:T(8,128)(2,1)S(1)} %collective-permute-done.6.refs_2_, s16[16,1408]{1,0:T(8,128)(2,1)S(1)} %collective-permute-done.7.refs_3_), custom_call_target="tpu_custom_call" | custom-call | tf_op jit(solution)/shard_map/chance_sum/pallas_call | solution.py:308
  (3 shorter events, 0.0 us)
Async XLA Ops:
  0.6 3.9 %copy-start.4 = (s8[1456,1408]{1,0:T(8,128)(4,1)S(1)}, s8[1456,1408]{1,0:T(8,128)(4,1)}, u32[]{:S(2)}) copy-start(s8[1456,1408]{1,0:T(8,128)(4,1)} %constant.8.clone.table_ref) | copy-start | bytes 6150148
  0.6 0.8 %copy-start.2 = (s32[1,32]{1,0:T(1,128)S(1)}, s32[1,32]{1,0:T(1,128)}, u32[]{:S(2)}) copy-start(s32[1,32]{1,0:T(1,128)} %kind_ref.1) | copy-start | bytes 388
  0.7 0.9 %copy-start.5 = (s32[1,1,2,1326]{3,2,1,0:T(2,128)S(1)}, s32[1,1,2,1326]{3,2,1,0:T(2,128)}, u32[]{:S(2)}) copy-start(s32[1,1,2,1326]{3,2,1,0:T(2,128)} %param.16) | copy-start | bytes 31828
  0.7 0.9 %copy-start.6 = (s32[1,1,2,1326]{3,2,1,0:T(2,128)S(1)}, s32[1,1,2,1326]{3,2,1,0:T(2,128)}, u32[]{:S(2)}) copy-start(s32[1,1,2,1326]{3,2,1,0:T(2,128)} %param.15) | copy-start | bytes 31828
  0.7 0.9 %copy-start.8 = (s32[1,1,2]{2,1,0:T(1,128)S(1)}, s32[1,1,2]{2,1,0:T(1,128)}, u32[]{:S(2)}) copy-start(s32[1,1,2]{2,1,0:T(1,128)} %param.14) | copy-start | bytes 28
  0.7 0.9 %copy-start.7 = (s32[1,1,2,256]{3,2,1,0:T(2,128)S(1)}, s32[1,1,2,256]{3,2,1,0:T(2,128)}, u32[]{:S(2)}) copy-start(s32[1,1,2,256]{3,2,1,0:T(2,128)} %param.13) | copy-start | bytes 6148
  0.7 3.9 %copy-start.1 = (bf16[1,32,1326]{2,1,0:T(8,128)(2,1)S(1)}, bf16[1,32,1326]{2,1,0:T(8,128)(2,1)}, u32[]{:S(2)}) copy-start(bf16[1,32,1326]{2,1,0:T(8,128)(2,1)} %param.10) | copy-start | bytes 254596
  0.7 7.7 %collective-permute-start.1 = (s32[1,32]{1,0:T(1,128)}, s32[1,32]{1,0:T(1,128)S(1)}, u32[]{:S(2)}, u32[]{:S(2)}) collective-permute-start(s32[1,32]{1,0:T(1,128)} %kind_ref.1), channel_id=1, source_target_pairs={{0,2},{1,3},{2,0},{3,1},{4,6},{5,7},{6,4},{7,5},{8,10},{9,11},{10,... | collective-permute-start | bytes 392 | tf_op jit(solution)/shard_map/ppermute | solution.py:319
  1.6 4.6 %collective-permute-start.2 = (s32[2,1792]{1,0:T(2,128)S(1)}, s32[2,1792]{1,0:T(2,128)S(1)}, u32[]{:S(2)}, u32[]{:S(2)}) collective-permute-start(s32[2,1792]{1,0:T(2,128)S(1)} %add_select_fusion.after_ref), channel_id=1, source_target_pairs={{0,1},{1,0},{2,3},{3,2},{4,5},{5,4},{6,7},{7,6},{8,9},{9,8},{10,11... | collective-permute-start | bytes 43016 | tf_op jit(solution)/shard_map/ppermute | solution.py:319
  4.6 3.8 %collective-permute-start = (bf16[32,1326]{1,0:T(8,128)(2,1)S(1)}, bf16[32,1326]{1,0:T(8,128)(2,1)S(1)}, u32[]{:S(2)}, u32[]{:S(2)}) collective-permute-start(bf16[32,1326]{1,0:T(8,128)(2,1)S(1)} %bitcast.8), channel_id=1, source_target_pairs={{0,2},{1,3},{2,0},{3,1},{4,6},{5,7},{6,4},{7,5},{8,10},{9,11},{10,... | collective-permute-start | bytes 254600 | tf_op jit(solution)/shard_map/ppermute | solution.py:319
  6.3 5.7 %collective-permute-start.3 = (s32[4,1792]{1,0:T(4,128)S(1)}, s32[4,1792]{1,0:T(4,128)S(1)}, u32[]{:S(2)}, u32[]{:S(2)}) collective-permute-start(s32[4,1792]{1,0:T(4,128)S(1)} %pad_add_fusion.refs_3_), channel_id=1, source_target_pairs={{0,4},{1,5},{2,6},{3,7},{4,0},{5,1},{6,2},{7,3},{8,12},{9,13},{10,... | collective-permute-start | bytes 86024 | tf_op jit(solution)/shard_map/ppermute | solution.py:319
  8.4 8.4 %copy-start = (f32[1,32,1326]{2,1,0:T(8,128)S(1)}, f32[1,32,1326]{2,1,0:T(8,128)}, u32[]{:S(2)}) copy-start(f32[1,32,1326]{2,1,0:T(8,128)} %param.9) | copy-start | bytes 509188
  8.4 8.4 %copy-start.3 = (s32[1,32]{1,0:T(1,128)S(1)}, s32[1,32]{1,0:T(1,128)}, u32[]{:S(2)}) copy-start(s32[1,32]{1,0:T(1,128)} %pot_ref.1) | copy-start | bytes 388
  15.3 1.5 %collective-permute-start.4 = (f32[32,1408]{1,0:T(8,128)S(1)}, f32[32,1408]{1,0:T(8,128)S(1)}, u32[]{:S(2)}, u32[]{:S(2)}) collective-permute-start(f32[32,1408]{1,0:T(8,128)S(1)} %get-tuple-element.21), channel_id=1, source_target_pairs={{0,2},{1,3},{2,0},{3,1},{4,6},{5,7},{6,4},{7,5},{8,10},{9,11},{10,... | collective-permute-start | bytes 540680 | tf_op jit(solution)/shard_map/ppermute | solution.py:319
  17.7 5.9 %collective-permute-start.7 = (s16[16,1408]{1,0:T(8,128)(2,1)S(1)}, s16[16,1408]{1,0:T(8,128)(2,1)S(1)}, u32[]{:S(2)}, u32[]{:S(2)}) collective-permute-start(s16[16,1408]{1,0:T(8,128)(2,1)S(1)} %get-tuple-element.23.refs_0_), channel_id=1, source_target_pairs={{0,24},{8,16},{16,8},{24,0},{1,25},{9,17},{17,9},{25,1},{2,26},{10... | collective-permute-start | bytes 135176 | tf_op jit(solution)/shard_map/ppermute | solution.py:319
  21.3 4.9 %collective-permute-start.6 = (s16[16,1408]{1,0:T(8,128)(2,1)S(1)}, s16[16,1408]{1,0:T(8,128)(2,1)S(1)}, u32[]{:S(2)}, u32[]{:S(2)}) collective-permute-start(s16[16,1408]{1,0:T(8,128)(2,1)S(1)} %get-tuple-element.23.refs_0_), channel_id=1, source_target_pairs={{0,16},{8,24},{16,0},{24,8},{1,17},{9,25},{17,1},{25,9},{2,18},{10... | collective-permute-start | bytes 135176 | tf_op jit(solution)/shard_map/ppermute | solution.py:319
  21.3 4.9 %collective-permute-start.5 = (s16[16,1408]{1,0:T(8,128)(2,1)S(1)}, s16[16,1408]{1,0:T(8,128)(2,1)S(1)}, u32[]{:S(2)}, u32[]{:S(2)}) collective-permute-start(s16[16,1408]{1,0:T(8,128)(2,1)S(1)} %get-tuple-element.23.refs_0_), channel_id=1, source_target_pairs={{0,8},{8,0},{16,24},{24,16},{1,9},{9,1},{17,25},{25,17},{2,10},{10... | collective-permute-start | bytes 135176 | tf_op jit(solution)/shard_map/ppermute | solution.py:319

commit v5 on v4

--- a/solution.py
+++ b/solution.py
@@ -15,7 +15,7 @@
 RANK_SPAN = 8192
 MANTISSA = 128
 ROW_TILE = 128
-COL_TILE = 768
+COL_TILE = 1408
 UNROLL = 8
 STEPS = 32767.0
 LOWEST = 100
@@ -140,14 +140,15 @@
 
 
 def first_kernel(hand_count, line_count, own_ref, mate_ref, mate_kind_ref, *refs):
-    tables, (packed_ref, own_out, mate_out, reach_ref, line_ref), scratch = refs[:3], refs[3:8], refs[8:]
+    tables, (packed_ref, own_out, mate_out, reach_ref, line_ref, same_ref), scratch = refs[:3], refs[3:9], refs[9:]
+    same_ref[...] = packed_ref[...]
     lines_kernel(hand_count, line_count, own_ref, mate_ref, mate_kind_ref, packed_ref, reach_ref, line_ref)
     own_out[...] = jnp.zeros_like(own_out)
     mate_out[...] = jnp.zeros_like(mate_out)
     add_boards(reach_ref, line_ref, *tables, packed_ref, own_out, mate_out, *scratch)
 
 
-def second_kernel(reach_ref, line_ref, *refs):
+def more_kernel(reach_ref, line_ref, *refs):
     tables, (packed_ref, own_ref, mate_ref, own_out, mate_out), scratch = refs[:3], refs[3:8], refs[8:]
     own_out[...] = own_ref[...]
     mate_out[...] = mate_ref[...]
@@ -191,12 +192,13 @@
         one = jnp.bfloat16(1)
         for first, count in tiles(wide, COL_TILE):
             at = slice(first, first + count)
-            total = jnp.dot(sums, spread_ref[:, at], preferred_element_type=jnp.float32)
+            total = 0.0
             for top, height in tiles(deep, ROW_TILE):
                 down = slice(top, top + height)
                 column = jnp.concatenate([column_ref[down]] * (count // LANE), axis=1)
                 matrix = jnp.clip(order[:, at] - column, -one, one) * apart_ref[down, at]
                 total += jnp.dot(show_reach[:, down], matrix, preferred_element_type=jnp.float32)
+            total += jnp.dot(sums, spread_ref[:, at], preferred_element_type=jnp.float32)
             total = (total + fold_reach[:, at].astype(jnp.float32)) * live[:, at]
             own_out[:, at] += total[:rows]
             mate_out[:, at] += total[rows:]
@@ -240,7 +242,7 @@
     return jnp.where(lane < LOWEST, down_size, up_size), jnp.where(lane < LOWEST, up_size, down_size)
 
 
-def update_kernel(hand_count, scale, own_ref, mate_ref, pot_ref, kind_ref, regret_ref, regret_out, code_out, node_ref):
+def decide(hand_count, scale, own_ref, mate_ref, pot_ref, kind_ref, regret_ref):
     pot = as_column(pot_ref[...])
     coef = jnp.where(as_column(kind_ref[...]) == 1, -pot, pot) * scale
     values = (own_ref[:, :hand_count] + mate_ref[:, :hand_count]) * coef
@@ -254,8 +256,18 @@
 
     positive = jnp.maximum(regrets, 0.0)
     strategy = (positive + floor_share) / (both(positive) + ACTS * floor_share)
-    node = both(strategy * values)
-    regret_out[...] = jnp.maximum(regrets + values - node, 0.0)
+    return regrets, values, both(strategy * values)
+
+
+def regrets_kernel(hand_count, scale, *refs):
+    regrets, values, node = decide(hand_count, scale, *refs[:-1])
+    refs[-1][...] = jnp.maximum(regrets + values - node, 0.0)
+
+
+def codes_kernel(hand_count, scale, *refs):
+    *inputs, code_out, node_ref = refs
+    _, _, node = decide(hand_count, scale, *inputs)
+    rows = node.shape[0]
     size, flip = powers()
     largest = jnp.max(jnp.abs(node), axis=1, keepdims=True)
     place = jnp.sum(jnp.where(size < largest, 1.0, 0.0), axis=1, keepdims=True)
@@ -270,23 +282,19 @@
         code_out[:, first : first + LANE] = jnp.floor(picked + 0.5).astype(jnp.int32).astype(jnp.int16)
 
 
-def update(hand_count, scale, own, mate, pots, kinds, regrets):
-    rows = regrets.shape[0]
+def decision_call(kernel, name, hand_count, scale, out_shape, inputs, scratch=()):
     return pl.pallas_call(
-        functools.partial(update_kernel, hand_count, scale),
-        out_shape=(
-            jax.ShapeDtypeStruct((rows, hand_count), jnp.float32),
-            jax.ShapeDtypeStruct((rows // ACTS, up(hand_count, LANE)), jnp.int16),
-        ),
-        in_specs=[WHOLE] * 5,
-        out_specs=(WHOLE, WHOLE),
-        scratch_shapes=[pltpu.VMEM((up(hand_count, LANE) // LANE, rows, LANE), jnp.float32)],
+        functools.partial(kernel, hand_count, scale),
+        out_shape=out_shape,
+        in_specs=[WHOLE] * len(inputs),
+        out_specs=WHOLE,
+        scratch_shapes=scratch,
         compiler_params=params(8),
-        name="regret_update",
-    )(own, mate, pots, kinds, regrets)
-
-
-def chance_kernel(hand_count, *refs):
+        name=name,
+    )(*inputs)
+
+
+def chance_kernel(hand_count, order, *refs):
     code_refs, out_ref = refs[:-1], refs[-1]
     size, _ = powers()
     lane = lax.broadcasted_iota(jnp.int32, (out_ref.shape[0], LANE), 1)
@@ -297,16 +305,17 @@
         gain = jnp.sum(jnp.where(lane == place, size, 0.0), axis=1, keepdims=True)
         return codes[:, :hand_count].astype(jnp.float32) * (gain * (1.0 / (STEPS * len(code_refs))))
 
+    values = {mask: value(ref) for mask, ref in zip((0, *order), code_refs)}
     total = None
-    for first, second in zip(code_refs[::2], code_refs[1::2]):
-        pair = value(first) + value(second)
+    for mask in range(0, len(values), 2):
+        pair = values[mask] + values[mask + 1]
         total = pair if total is None else total + pair
     out_ref[...] = total
 
 
-def chance(hand_count, codes):
+def chance(hand_count, order, codes):
     return pl.pallas_call(
-        functools.partial(chance_kernel, hand_count),
+        functools.partial(chance_kernel, hand_count, order),
         out_shape=jax.ShapeDtypeStruct((codes[0].shape[0], hand_count), jnp.float32),
         in_specs=[WHOLE] * len(codes),
         out_specs=WHOLE,
@@ -332,38 +341,52 @@
     bases = first_lines(line_count, core)
     kinds = jnp.pad(line_kind, ((0, 0), (0, extra)))
     boards = pack(board_count[0, 0], board_lines[0, 0], hand_ranks[0, 0], live_hands[0, 0], kinds, bases)
-    held, arrived = boards, boards
-    for bit in range(group_size.bit_length() - 1):
-        mask = 1 << bit
-        if mask != core:
-            held = boards if mask == 1 else jnp.concatenate([held, arrived], axis=0)
-            arrived = swap(held, group, mask)
+    masks = [1 << bit for bit in range(group_size.bit_length() - 1) if 1 << bit != core]
+    arrived = swap(boards, group, masks[0])
     reach = jnp.pad(opp_reach[0], ((0, extra), (0, 0)))
     pots = jnp.pad(pot_size, ((0, 0), (0, extra)))
     old_regrets = jnp.pad(regrets[0], ((0, extra), (0, 0)))
     mate_reach, mate_kinds = swap(reach, group, core), swap(kinds, group, core)
     held_tables = unpack(jnp.asarray(table(hand_count)), boards)
     rows, wide = reach.shape[0], up(hand_count, LANE)
-    own, for_mate, all_reach, lines = board_sums(
+    own, for_mate, all_reach, lines, boards = board_sums(
         functools.partial(first_kernel, hand_count, line_count),
         "first_boards",
         rows,
         (reach, mate_reach, mate_kinds),
         held_tables,
-        held,
+        boards,
         more=(
             jax.ShapeDtypeStruct((2 * rows, wide), jnp.bfloat16),
             jax.ShapeDtypeStruct((2 * rows, LANE), jnp.int32),
+            jax.ShapeDtypeStruct(boards.shape, boards.dtype),
         ),
     )
-    own, for_mate = board_sums(
-        second_kernel, "second_boards", rows, (all_reach, lines), held_tables, arrived, (own, for_mate)
+    for mask in (*masks[1:], None):
+        latest = arrived
+        if mask is not None:
+            boards = jnp.concatenate([boards, latest], axis=0)
+            arrived = swap(boards, group, mask)
+        own, for_mate = board_sums(
+            more_kernel, "more_boards", rows, (all_reach, lines), held_tables, latest, (own, for_mate)
+        )
+    mate = swap(for_mate, group, core)
+    scale = 1.0 / (board_total * hand_count)
+    inputs = (own, mate, pots, kinds, old_regrets)
+    codes = decision_call(
+        codes_kernel,
+        "node_codes",
+        hand_count,
+        scale,
+        jax.ShapeDtypeStruct((rows // ACTS, wide), jnp.int16),
+        inputs,
+        [pltpu.VMEM((wide // LANE, rows, LANE), jnp.float32)],
     )
-    mate = swap(for_mate, group, core)
-    updated, codes = update(hand_count, 1.0 / (board_total * hand_count), own, mate, pots, kinds, old_regrets)
-    flops = lax.axis_size("flop")
-    arrived = {mask: swap(codes, "flop", mask) for mask in (flops - 1, *range(1, flops - 1))}
-    total = chance(hand_count, [codes] + [arrived[mask] for mask in range(1, flops)])
+    updated = decision_call(
+        regrets_kernel, "new_regrets", hand_count, scale, jax.ShapeDtypeStruct((rows, hand_count), jnp.float32), inputs
+    )
+    order = (3, 2, 1)
+    total = chance(hand_count, order, [codes] + [swap(codes, "flop", mask) for mask in order])
     return (updated[None, :line_count], total[: line_count // ACTS])
 
 

time: 27.2 us -> 26.3 us (0.967)
  waiting for transfers between devices: 6.85 us -> 5.16 us
  Pallas kernels: 8.97 us -> 9.79 us
  starting transfers between devices: 10 us -> 9.56 us
  local copies, waits for them, and re-layouts: 0.33 us -> 0.7 us
    ppermute x8, waiting for transfers between devices: 6.85 us -> 5.16 us  [swap(): lax.ppermute(array, axes, [(index, index ^ mask) for index in range(lax.a...]
    ppermute x8, starting transfers between devices: 10 us -> 9.56 us  [swap(): lax.ppermute(array, axes, [(index, index ^ mask) for index in range(lax.a...]
    pallas_call x2 -> x3, Pallas kernels: 1.66 us -> 2.09 us  [the longest x2 1.28 us: decision_call(): pl.pallas_call(functools.partial(kernel, hand_count, scale), out_shape=ou...]
    pallas_call x2 -> x3, Pallas kernels: 6.9 us -> 7.28 us  [board_sums(): pl.pallas_call(kernel, out_shape=out, in_specs=[WHOLE] * (len(inputs) + l...]
    unnamed x18, local copies, waits for them, and re-layouts: 0.33 us -> 0.7 us
  transfers between devices with their start and end apart: 8 -> 8, of which waited for: 4 -> 4; matrix products, arithmetic and copies ran while one was open for 0% -> 0% of each run, Pallas kernels for 15% -> 20%
where the time goes in v5:
time: 26.3 us; the launch traced here: 26.1 us
  Pallas kernels  9.79 us (37%)
  starting transfers between devices  9.56 us (36%)
  waiting for transfers between devices  5.16 us (20%)
  between operations  0.78 us (3%)
  local copies, waits for them, and re-layouts  0.7 us (3%)
    ppermute x8, starting transfers between devices, swap(): lax.ppermute(array, axes, [(index, index ^ mask) for index in range(lax.a...  9.56 us
    pallas_call x3, Pallas kernels, board_sums(): pl.pallas_call(kernel, out_shape=out, in_specs=[WHOLE] * (len(inputs) + l...  7.28 us
    ppermute x8, waiting for transfers between devices, swap(): lax.ppermute(array, axes, [(index, index ^ mask) for index in range(lax.a...  5.16 us
    pallas_call x2, Pallas kernels, decision_call(): pl.pallas_call(functools.partial(kernel, hand_count, scale), out_shape=ou...  1.28 us
    pallas_call x1, Pallas kernels, chance(): pl.pallas_call(functools.partial(chance_kernel, hand_count, order), out_s...  0.81 us
    unnamed x18, local copies, waits for them, and re-layouts  0.7 us
  transfers between devices with their start and end apart: 8, of which 4 were waited for; matrix products, arithmetic and copies ran while one was open for 0% of the time, Pallas kernels for 20%

profile of v5, /device:TPU:0, one launch (start us, length us, event | category | flops | bytes accessed | tf_op | source)
XLA Modules:
  0.0 26.1 jit_solution(5200326817311524199)
XLA Ops:
  0.6 0.5 %collective-permute-start = (bf16[32,1326]{1,0:T(8,128)(2,1)}, bf16[32,1326]{1,0:T(8,128)(2,1)S(1)}, u32[]{:S(2)}, u32[]{:S(2)}) collective-permute-start(bf16[32,1326]{1,0:T(8,128)(2,1)} %bitcast.9), channel_id=1, source_target_pairs={{0,2},{1,3},{2,0},{3,1},{4,6},{5,7},{6,4},{7,5},{8,10},{9,11},{10,... | collective-permute-start | bytes 254600 | tf_op jit(solution)/shard_map/ppermute | solution.py:328
  1.1 0.1 collective-permute-start.1
  1.2 0.0 copy-start.2
  1.2 0.0 copy-start.5
  1.2 0.0 copy-start.6
  1.3 0.0 copy-start.7
  1.3 0.0 copy-start.8
  1.3 0.0 copy-start.4
  1.3 0.6 %copy-done.2 = s32[1,32]{1,0:T(1,128)S(1)} copy-done((s32[1,32]{1,0:T(1,128)S(1)}, s32[1,32]{1,0:T(1,128)}, u32[]{:S(2)}) %copy-start.2) | copy-done | bytes 152
  1.9 0.1 copy-done.5
  2.0 0.0 copy-done.6
  2.0 0.0 copy-done.7
  2.0 0.0 copy-done.8
  2.0 0.1 add_select_fusion.after_ref.refs_3_
  2.1 0.0 copy-start.1
  2.1 2.9 %collective-permute-start.2 = (s32[2,1792]{1,0:T(2,128)S(1)}, s32[2,1792]{1,0:T(2,128)S(1)}, u32[]{:S(2)}, u32[]{:S(2)}) collective-permute-start(s32[2,1792]{1,0:T(2,128)S(1)} %add_select_fusion.after_ref.refs_3_), channel_id=1, source_target_pairs={{0,1},{1,0},{2,3},{3,2},{4,5},{5,4},{6,7},{7,6},{8,9},{9,8},{10,11... | collective-permute-start | bytes 43016 | tf_op jit(solution)/shard_map/ppermute | solution.py:328
  5.0 0.0 copy-done.4
  5.0 0.4 %unpack_tables.1 = (bf16[1328,1408]{1,0:T(8,128)(2,1)S(1)}, bf16[1408,128]{1,0:T(8,128)(2,1)S(1)}, bf16[128,1408]{1,0:T(8,128)(2,1)S(1)}) custom-call(s32[2,1792]{1,0:T(2,128)S(1)} %add_select_fusion.after_ref.refs_3_, s8[1456,1408]{1,0:T(8,128)(4,1)S(1)} %copy-done.4), custom_call_target="tpu_custom_call" | custom-call | flops 4000000000 | bytes 6150144 | tf_op jit(solution)/shard_map/unpack_tables/pallas_call | solution.py:114
  5.4 0.0 collective-permute-done.1.mate_kind_ref
  5.4 0.0 collective-permute-done.mate_ref
  5.4 0.0 copy-done.1
  5.4 2.1 %first_boards.1 = (f32[32,1408]{1,0:T(8,128)S(1)}, f32[32,1408]{1,0:T(8,128)S(1)}, bf16[64,1408]{1,0:T(8,128)(2,1)S(1)}, s32[64,128]{1,0:T(8,128)S(1)}, s32[2,1792]{1,0:T(2,128)S(1)}) custom-call(bf16[32,1326]{1,0:T(8,128)(2,1)S(1)} %bitcast.10, bf16[32,1326]{1,0:T(8,128)(2,1)S(1)} %collective-permute-done.mate_ref, ...), custom_call_target="tpu_custom_call" | custom-call | flops 507510784 | tf_op jit(solution)/shard_map/first_boards/pallas_call | solution.py:216
  7.5 0.0 collective-permute-done.2.refs_3_
  7.6 1.5 %collective-permute-start.3 = (s32[4,1792]{1,0:T(4,128)S(1)}, s32[4,1792]{1,0:T(4,128)S(1)}, u32[]{:S(2)}, u32[]{:S(2)}) collective-permute-start(s32[4,1792]{1,0:T(4,128)S(1)} %pad_add_fusion), channel_id=1, source_target_pairs={{0,4},{1,5},{2,6},{3,7},{4,0},{5,1},{6,2},{7,3},{8,12},{9,13},{10,... | collective-permute-start | bytes 86024 | tf_op jit(solution)/shard_map/ppermute | solution.py:328
  9.1 1.9 %more_boards.2 = (f32[32,1408]{1,0:T(8,128)S(1)}, f32[32,1408]{1,0:T(8,128)S(1)}) custom-call(bf16[64,1408]{1,0:T(8,128)(2,1)S(1)} %get-tuple-element.17.reach_ref, s32[64,128]{1,0:T(8,128)S(1)} %get-tuple-element.18.line_ref, bf16[1328,1408]{1,0:T(8,128)(2,1)S(1)} %get-tuple-element.14.refs_0_, bf16[1408,128]{1,0:T(8,128)(2,1)S(1)} %get-tuple-element.15.refs_1_, ...), custom_call_target="tpu_custom_call" | custom-call | flops 507510784 | tf_op jit(solution)/shard_map/more_boards/pallas_call | solution.py:216
  11.0 0.0 copy-start
  11.0 0.0 copy-start.3
  11.0 0.5 %collective-permute-done.3.refs_3_ = s32[4,1792]{1,0:T(4,128)S(1)} collective-permute-done((s32[4,1792]{1,0:T(4,128)S(1)}, s32[4,1792]{1,0:T(4,128)S(1)}, u32[]{:S(2)}, u32[]{:S(2)}) %collective-permute-start.3) | collective-permute-done | bytes 28704 | tf_op jit(solution)/shard_map/ppermute | solution.py:328
  11.5 3.3 %more_boards.3 = (f32[32,1408]{1,0:T(8,128)S(1)}, f32[32,1408]{1,0:T(8,128)S(1)}) custom-call(bf16[64,1408]{1,0:T(8,128)(2,1)S(1)} %get-tuple-element.17.reach_ref, s32[64,128]{1,0:T(8,128)S(1)} %get-tuple-element.18.line_ref, bf16[1328,1408]{1,0:T(8,128)(2,1)S(1)} %get-tuple-element.14.refs_0_, bf16[1408,128]{1,0:T(8,128)(2,1)S(1)} %get-tuple-element.15.refs_1_, ...), custom_call_target="tpu_custom_call" | custom-call | flops 1015021568 | tf_op jit(solution)/shard_map/more_boards/pallas_call | solution.py:216
  14.8 0.1 collective-permute-start.4
  14.9 1.4 %collective-permute-done.4.refs_1_ = f32[32,1408]{1,0:T(8,128)S(1)} collective-permute-done((f32[32,1408]{1,0:T(8,128)S(1)}, f32[32,1408]{1,0:T(8,128)S(1)}, u32[]{:S(2)}, u32[]{:S(2)}) %collective-permute-start.4) | collective-permute-done | bytes 180256 | tf_op jit(solution)/shard_map/ppermute | solution.py:328
  16.3 0.0 copy-done
  16.3 0.0 copy-done.3
  16.3 0.4 %node_codes.1.refs_0_ = s16[16,1408]{1,0:T(8,128)(2,1)S(1)} custom-call(f32[32,1408]{1,0:T(8,128)S(1)} %get-tuple-element.24.refs_0_, f32[32,1408]{1,0:T(8,128)S(1)} %collective-permute-done.4.refs_1_, s32[1,32]{1,0:T(1,128)S(1)} %copy-done.3, s32[1,32]{1,0:T(1,128)S(1)} %copy-done.2, f32[32,1326]{1,0:T(8,128)S(1)} %bitcast.7), custom_call_target="tpu_custom_call" | custom-call | tf_op jit(solution)/shard_map/node_codes/pallas_call | solution.py:286
  16.7 3.6 %collective-permute-start.5 = (s16[16,1408]{1,0:T(8,128)(2,1)S(1)}, s16[16,1408]{1,0:T(8,128)(2,1)S(1)}, u32[]{:S(2)}, u32[]{:S(2)}) collective-permute-start(s16[16,1408]{1,0:T(8,128)(2,1)S(1)} %node_codes.1.refs_0_), channel_id=1, source_target_pairs={{0,24},{8,16},{16,8},{24,0},{1,25},{9,17},{17,9},{25,1},{2,26},{10... | collective-permute-start | bytes 135176 | tf_op jit(solution)/shard_map/ppermute | solution.py:328
  20.3 0.0 collective-permute-start.6
  20.3 0.8 %collective-permute-start.7 = (s16[16,1408]{1,0:T(8,128)(2,1)S(1)}, s16[16,1408]{1,0:T(8,128)(2,1)S(1)}, u32[]{:S(2)}, u32[]{:S(2)}) collective-permute-start(s16[16,1408]{1,0:T(8,128)(2,1)S(1)} %node_codes.1.refs_0_), channel_id=1, source_target_pairs={{0,8},{8,0},{16,24},{24,16},{1,9},{9,1},{17,25},{25,17},{2,10},{10... | collective-permute-start | bytes 135176 | tf_op jit(solution)/shard_map/ppermute | solution.py:328
  21.2 0.9 %new_regrets.1 = f32[32,1326]{1,0:T(8,128)} custom-call(f32[32,1408]{1,0:T(8,128)S(1)} %get-tuple-element.24.refs_0_, f32[32,1408]{1,0:T(8,128)S(1)} %collective-permute-done.4.refs_1_, s32[1,32]{1,0:T(1,128)S(1)} %copy-done.3, s32[1,32]{1,0:T(1,128)S(1)} %copy-done.2, f32[32,1326]{1,0:T(8,128)S(1)} %bitcast.8), custom_call_target="tpu_custom_call" | custom-call | tf_op jit(solution)/shard_map/new_regrets/pallas_call | solution.py:286
  22.0 0.6 %collective-permute-done.5.refs_1_ = s16[16,1408]{1,0:T(8,128)(2,1)S(1)} collective-permute-done((s16[16,1408]{1,0:T(8,128)(2,1)S(1)}, s16[16,1408]{1,0:T(8,128)(2,1)S(1)}, u32[]{:S(2)}, u32[]{:S(2)}) %collective-permute-start.5) | collective-permute-done | bytes 45088 | tf_op jit(solution)/shard_map/ppermute | solution.py:328
  22.7 2.6 %collective-permute-done.6.refs_2_ = s16[16,1408]{1,0:T(8,128)(2,1)S(1)} collective-permute-done((s16[16,1408]{1,0:T(8,128)(2,1)S(1)}, s16[16,1408]{1,0:T(8,128)(2,1)S(1)}, u32[]{:S(2)}, u32[]{:S(2)}) %collective-permute-start.6) | collective-permute-done | bytes 45088 | tf_op jit(solution)/shard_map/ppermute | solution.py:328
  25.3 0.0 collective-permute-done.7.refs_3_
  25.3 0.8 %chance_sum.1 = f32[16,1326]{1,0:T(8,128)} custom-call(s16[16,1408]{1,0:T(8,128)(2,1)S(1)} %node_codes.1.refs_0_, s16[16,1408]{1,0:T(8,128)(2,1)S(1)} %collective-permute-done.5.refs_1_, s16[16,1408]{1,0:T(8,128)(2,1)S(1)} %collective-permute-done.6.refs_2_, s16[16,1408]{1,0:T(8,128)(2,1)S(1)} %collective-permute-done.7.refs_3_), custom_call_target="tpu_custom_call" | custom-call | tf_op jit(solution)/shard_map/chance_sum/pallas_call | solution.py:317
  (3 shorter events, 0.0 us)
Async XLA Ops:
  0.6 4.8 %collective-permute-start = (bf16[32,1326]{1,0:T(8,128)(2,1)}, bf16[32,1326]{1,0:T(8,128)(2,1)S(1)}, u32[]{:S(2)}, u32[]{:S(2)}) collective-permute-start(bf16[32,1326]{1,0:T(8,128)(2,1)} %bitcast.9), channel_id=1, source_target_pairs={{0,2},{1,3},{2,0},{3,1},{4,6},{5,7},{6,4},{7,5},{8,10},{9,11},{10,... | collective-permute-start | bytes 254600 | tf_op jit(solution)/shard_map/ppermute | solution.py:328
  1.1 4.3 %collective-permute-start.1 = (s32[1,32]{1,0:T(1,128)}, s32[1,32]{1,0:T(1,128)S(1)}, u32[]{:S(2)}, u32[]{:S(2)}) collective-permute-start(s32[1,32]{1,0:T(1,128)} %refs_3_.3), channel_id=1, source_target_pairs={{0,2},{1,3},{2,0},{3,1},{4,6},{5,7},{6,4},{7,5},{8,10},{9,11},{10,... | collective-permute-start | bytes 392 | tf_op jit(solution)/shard_map/ppermute | solution.py:328
  1.2 0.7 %copy-start.2 = (s32[1,32]{1,0:T(1,128)S(1)}, s32[1,32]{1,0:T(1,128)}, u32[]{:S(2)}) copy-start(s32[1,32]{1,0:T(1,128)} %refs_3_.3) | copy-start | bytes 388
  1.2 0.7 %copy-start.5 = (s32[1,1,2,1326]{3,2,1,0:T(2,128)S(1)}, s32[1,1,2,1326]{3,2,1,0:T(2,128)}, u32[]{:S(2)}) copy-start(s32[1,1,2,1326]{3,2,1,0:T(2,128)} %param.16) | copy-start | bytes 31828
  1.2 0.7 %copy-start.6 = (s32[1,1,2,1326]{3,2,1,0:T(2,128)S(1)}, s32[1,1,2,1326]{3,2,1,0:T(2,128)}, u32[]{:S(2)}) copy-start(s32[1,1,2,1326]{3,2,1,0:T(2,128)} %param.15) | copy-start | bytes 31828
  1.3 0.7 %copy-start.7 = (s32[1,1,2,256]{3,2,1,0:T(2,128)S(1)}, s32[1,1,2,256]{3,2,1,0:T(2,128)}, u32[]{:S(2)}) copy-start(s32[1,1,2,256]{3,2,1,0:T(2,128)} %param.13) | copy-start | bytes 6148
  1.3 0.7 %copy-start.8 = (s32[1,1,2]{2,1,0:T(1,128)S(1)}, s32[1,1,2]{2,1,0:T(1,128)}, u32[]{:S(2)}) copy-start(s32[1,1,2]{2,1,0:T(1,128)} %param.14) | copy-start | bytes 28
  1.3 3.7 %copy-start.4 = (s8[1456,1408]{1,0:T(8,128)(4,1)S(1)}, s8[1456,1408]{1,0:T(8,128)(4,1)}, u32[]{:S(2)}) copy-start(s8[1456,1408]{1,0:T(8,128)(4,1)} %constant.8.clone.table_ref) | copy-start | bytes 6150148
  2.1 3.4 %copy-start.1 = (bf16[1,32,1326]{2,1,0:T(8,128)(2,1)S(1)}, bf16[1,32,1326]{2,1,0:T(8,128)(2,1)}, u32[]{:S(2)}) copy-start(bf16[1,32,1326]{2,1,0:T(8,128)(2,1)} %param.10) | copy-start | bytes 254596
  2.1 5.5 %collective-permute-start.2 = (s32[2,1792]{1,0:T(2,128)S(1)}, s32[2,1792]{1,0:T(2,128)S(1)}, u32[]{:S(2)}, u32[]{:S(2)}) collective-permute-start(s32[2,1792]{1,0:T(2,128)S(1)} %add_select_fusion.after_ref.refs_3_), channel_id=1, source_target_pairs={{0,1},{1,0},{2,3},{3,2},{4,5},{5,4},{6,7},{7,6},{8,9},{9,8},{10,11... | collective-permute-start | bytes 43016 | tf_op jit(solution)/shard_map/ppermute | solution.py:328
  7.6 3.9 %collective-permute-start.3 = (s32[4,1792]{1,0:T(4,128)S(1)}, s32[4,1792]{1,0:T(4,128)S(1)}, u32[]{:S(2)}, u32[]{:S(2)}) collective-permute-start(s32[4,1792]{1,0:T(4,128)S(1)} %pad_add_fusion), channel_id=1, source_target_pairs={{0,4},{1,5},{2,6},{3,7},{4,0},{5,1},{6,2},{7,3},{8,12},{9,13},{10,... | collective-permute-start | bytes 86024 | tf_op jit(solution)/shard_map/ppermute | solution.py:328
  11.0 5.3 %copy-start = (f32[1,32,1326]{2,1,0:T(8,128)S(1)}, f32[1,32,1326]{2,1,0:T(8,128)}, u32[]{:S(2)}) copy-start(f32[1,32,1326]{2,1,0:T(8,128)} %param.9) | copy-start | bytes 509188
  11.0 5.3 %copy-start.3 = (s32[1,32]{1,0:T(1,128)S(1)}, s32[1,32]{1,0:T(1,128)}, u32[]{:S(2)}) copy-start(s32[1,32]{1,0:T(1,128)} %refs_2_.3) | copy-start | bytes 388
  14.8 1.5 %collective-permute-start.4 = (f32[32,1408]{1,0:T(8,128)S(1)}, f32[32,1408]{1,0:T(8,128)S(1)}, u32[]{:S(2)}, u32[]{:S(2)}) collective-permute-start(f32[32,1408]{1,0:T(8,128)S(1)} %get-tuple-element.25), channel_id=1, source_target_pairs={{0,2},{1,3},{2,0},{3,1},{4,6},{5,7},{6,4},{7,5},{8,10},{9,11},{10,... | collective-permute-start | bytes 540680 | tf_op jit(solution)/shard_map/ppermute | solution.py:328
  16.7 6.0 %collective-permute-start.5 = (s16[16,1408]{1,0:T(8,128)(2,1)S(1)}, s16[16,1408]{1,0:T(8,128)(2,1)S(1)}, u32[]{:S(2)}, u32[]{:S(2)}) collective-permute-start(s16[16,1408]{1,0:T(8,128)(2,1)S(1)} %node_codes.1.refs_0_), channel_id=1, source_target_pairs={{0,24},{8,16},{16,8},{24,0},{1,25},{9,17},{17,9},{25,1},{2,26},{10... | collective-permute-start | bytes 135176 | tf_op jit(solution)/shard_map/ppermute | solution.py:328
  20.3 4.9 %collective-permute-start.6 = (s16[16,1408]{1,0:T(8,128)(2,1)S(1)}, s16[16,1408]{1,0:T(8,128)(2,1)S(1)}, u32[]{:S(2)}, u32[]{:S(2)}) collective-permute-start(s16[16,1408]{1,0:T(8,128)(2,1)S(1)} %node_codes.1.refs_0_), channel_id=1, source_target_pairs={{0,16},{8,24},{16,0},{24,8},{1,17},{9,25},{17,1},{25,9},{2,18},{10... | collective-permute-start | bytes 135176 | tf_op jit(solution)/shard_map/ppermute | solution.py:328
  20.3 4.9 %collective-permute-start.7 = (s16[16,1408]{1,0:T(8,128)(2,1)S(1)}, s16[16,1408]{1,0:T(8,128)(2,1)S(1)}, u32[]{:S(2)}, u32[]{:S(2)}) collective-permute-start(s16[16,1408]{1,0:T(8,128)(2,1)S(1)} %node_codes.1.refs_0_), channel_id=1, source_target_pairs={{0,8},{8,0},{16,24},{24,16},{1,9},{9,1},{17,25},{25,17},{2,10},{10... | collective-permute-start | bytes 135176 | tf_op jit(solution)/shard_map/ppermute | solution.py:328

commit v6 on v5

--- a/solution.py
+++ b/solution.py
@@ -19,7 +19,6 @@
 UNROLL = 8
 STEPS = 32767.0
 LOWEST = 100
-TABLE_TYPE = jnp.int8
 WHOLE = pl.BlockSpec(memory_space=pltpu.VMEM)
 
 floor_share = 0.1
@@ -38,7 +37,7 @@
 
 
 @functools.cache
-def table(hand_count):
+def tables(hand_count):
     wide, deep = up(hand_count, LANE), up(hand_count, 16)
     first, second = np.triu_indices(CARDS, 1)
     cards = np.zeros((hand_count, CARDS), np.float32)
@@ -46,11 +45,13 @@
     cards[np.arange(hand_count), second] = 1
     apart = np.zeros((deep, wide), np.float32)
     apart[:hand_count, :hand_count] = (cards @ cards.T) == 0
-    sums = np.zeros((LANE, wide), np.float32)
+    spread = np.zeros((LANE, wide), np.float32)
     for first in (0, 1 + CARDS):
-        sums[first, :hand_count] = 1
-        sums[first + 1 : first + 1 + CARDS, :hand_count] = cards.T
-    return np.concatenate([apart, sums]).astype(TABLE_TYPE)
+        spread[first, :hand_count] = 1
+        spread[first + 1 : first + 1 + CARDS, :hand_count] = cards.T
+    collect = -spread.T
+    collect[:, [0, 1 + CARDS]] *= -1
+    return [part.astype(jnp.bfloat16) for part in (apart, collect, spread)]
 
 
 def as_column(row):
@@ -81,11 +82,11 @@
         out_specs=WHOLE,
         compiler_params=params(4),
         name="first_lines",
-        cost_estimate=pl.CostEstimate(flops=20 * 10**9, bytes_accessed=0, transcendentals=0),
+        cost_estimate=pl.CostEstimate(flops=60 * 10**9, bytes_accessed=0, transcendentals=0),
     )()
 
 
-def pack(counts, slots, ranks, live, kinds, bases):
+def pack(counts, slots, ranks, live, bases):
     hand_count, slot_count, boards = ranks.shape[1], slots.shape[1], ranks.shape[0]
     wide = up(hand_count, LANE)
 
@@ -93,56 +94,28 @@
         after = wide + slot_count + LANE - first - array.shape[1]
         return jnp.pad(array, ((0, boards - array.shape[0]), (first, after)))
 
-    packed = place(ranks, 0) + RANK_SPAN * place(live, 0) + place(slots, wide) + place(kinds, wide + slot_count)
-    packed += place(bases, wide + slot_count)
+    packed = place(ranks, 0) + RANK_SPAN * place(live, 0) + place(slots, wide) + place(bases, wide + slot_count)
     lane = lax.broadcasted_iota(jnp.int32, packed.shape, 1)
     return jnp.where(lane == wide - 1, lax.broadcast_in_dim(counts, packed.shape, (0,)), packed)
 
 
-def unpack_kernel(after_ref, table_ref, apart_ref, collect_ref, spread_ref):
-    deep = apart_ref.shape[0]
-    apart_ref[...] = table_ref[:deep].astype(jnp.bfloat16)
-    cards = table_ref[deep:].astype(jnp.float32)
-    spread_ref[...] = cards.astype(jnp.bfloat16)
-    row = lax.broadcasted_iota(jnp.int32, (LANE, 1), 0)
-    signed = jnp.where((row == 0) | (row == 1 + CARDS), cards, -cards)
-    collect_ref[...] = jnp.transpose(signed).astype(jnp.bfloat16)
-
-
-def unpack(table, after):
-    deep, wide = table.shape[0] - LANE, table.shape[1]
-    return pl.pallas_call(
-        unpack_kernel,
-        out_shape=[jax.ShapeDtypeStruct(shape, jnp.bfloat16) for shape in ((deep, wide), (wide, LANE), (LANE, wide))],
-        in_specs=[WHOLE] * 2,
-        out_specs=[WHOLE] * 3,
-        compiler_params=params(12),
-        name="unpack_tables",
-        cost_estimate=pl.CostEstimate(flops=4 * 10**9, bytes_accessed=3 * table.size, transcendentals=0),
-    )(after, table)
-
-
-def lines_kernel(hand_count, line_count, own_ref, mate_ref, mate_kind_ref, packed_ref, reach_ref, line_ref):
+def lines_kernel(hand_count, line_count, own_ref, mate_ref, packed_ref, reach_ref, line_ref):
     rows = own_ref.shape[0]
-    first = packed_ref.shape[1] - LANE
-    base = packed_ref[:1, first + LANE // 2 : first + LANE // 2 + 2]
+    first = packed_ref.shape[1] - LANE // 2
+    base = packed_ref[:1, first : first + 2]
     reach_ref[...] = jnp.zeros_like(reach_ref)
     reach_ref[:rows, :hand_count] = own_ref[...]
     reach_ref[rows:, :hand_count] = mate_ref[...]
-    own_kind = as_column(packed_ref[:1, first : first + rows])
-    kind = jnp.concatenate([own_kind, as_column(mate_kind_ref[...])], axis=0)
-    row = lax.broadcasted_iota(jnp.int32, (2 * rows, 1), 0)
+    row = lax.broadcasted_iota(jnp.int32, line_ref.shape, 0)
     within = jnp.where(row < rows, row, row - rows)
     line = jnp.where(row < rows, base[:, :1], base[:, 1:]) + within
-    line = jnp.where(within < line_count, line, -2)
-    lane = lax.broadcasted_iota(jnp.int32, line_ref.shape, 1)
-    line_ref[...] = jnp.where(lane == 0, line, kind.astype(jnp.int32))
-
-
-def first_kernel(hand_count, line_count, own_ref, mate_ref, mate_kind_ref, *refs):
+    line_ref[...] = jnp.where(within < line_count, line, -2)
+
+
+def first_kernel(hand_count, line_count, own_ref, mate_ref, *refs):
     tables, (packed_ref, own_out, mate_out, reach_ref, line_ref, same_ref), scratch = refs[:3], refs[3:9], refs[9:]
     same_ref[...] = packed_ref[...]
-    lines_kernel(hand_count, line_count, own_ref, mate_ref, mate_kind_ref, packed_ref, reach_ref, line_ref)
+    lines_kernel(hand_count, line_count, own_ref, mate_ref, packed_ref, reach_ref, line_ref)
     own_out[...] = jnp.zeros_like(own_out)
     mate_out[...] = jnp.zeros_like(mate_out)
     add_boards(reach_ref, line_ref, *tables, packed_ref, own_out, mate_out, *scratch)
@@ -161,13 +134,15 @@
     wide, deep = apart_ref.shape[1], apart_ref.shape[0]
     rows = own_out.shape[0]
     parts = 1 + CARDS
-    line, kind = line_ref[:, :1], line_ref[:, 1:2]
+    line = jnp.concatenate([line_ref[...]] * ((packed_ref.shape[1] - LANE - wide) // LANE), axis=1)
     lane = lax.broadcasted_iota(jnp.int32, (2 * rows, LANE), 1)
     board_total = packed_ref.shape[0]
     end = packed_ref.shape[1] - LANE
     slot = lax.broadcasted_iota(jnp.int32, (board_total, end - wide), 1)
     board_ref[:, :wide] = packed_ref[:, :wide]
     board_ref[:, wide:] = jnp.where(slot < packed_ref[:, wide - 1 : wide], packed_ref[:, wide:end], -1)
+
+    zero, one = jnp.bfloat16(0), jnp.bfloat16(1)
 
     def add_board(board):
         keys = board_ref[pl.ds(board, 1), :wide]
@@ -181,15 +156,12 @@
         column_ref[...] = jnp.transpose(jnp.broadcast_to(order, (LANE, wide)))[:deep].astype(jnp.bfloat16)
         order = order.astype(jnp.bfloat16)
         keep = jnp.max(jnp.where(slots == line, 1.0, 0.0), axis=1, keepdims=True)
-        show_keep = jnp.where(kind == 0, keep, 0.0).astype(jnp.bfloat16)
-        fold_keep = jnp.where(kind == 0, 0.0, keep).astype(jnp.bfloat16)
-        held = reach_ref[...] * live.astype(jnp.bfloat16)
-        show_reach = held * show_keep
-        fold_reach = held * fold_keep
+        held = reach_ref[...] * live.astype(jnp.bfloat16) * keep.astype(jnp.bfloat16)
+        show_reach = jnp.maximum(held, zero)
+        fold_reach = jnp.maximum(-held, zero)
         sums = jnp.dot(fold_reach, collect_ref[...], preferred_element_type=jnp.float32)
         high = sums.astype(jnp.bfloat16).astype(jnp.float32)
         sums = jnp.where(lane < parts, high, sums - high).astype(jnp.bfloat16)
-        one = jnp.bfloat16(1)
         for first, count in tiles(wide, COL_TILE):
             at = slice(first, first + count)
             total = 0.0
@@ -340,20 +312,22 @@
     extra = up(line_count, SUB) - line_count
     bases = first_lines(line_count, core)
     kinds = jnp.pad(line_kind, ((0, 0), (0, extra)))
-    boards = pack(board_count[0, 0], board_lines[0, 0], hand_ranks[0, 0], live_hands[0, 0], kinds, bases)
+    boards = pack(board_count[0, 0], board_lines[0, 0], hand_ranks[0, 0], live_hands[0, 0], bases)
     masks = [1 << bit for bit in range(group_size.bit_length() - 1) if 1 << bit != core]
     arrived = swap(boards, group, masks[0])
-    reach = jnp.pad(opp_reach[0], ((0, extra), (0, 0)))
+    reach, late_kinds, _ = lax.optimization_barrier((jnp.pad(opp_reach[0], ((0, extra), (0, 0))), kinds, bases))
+    showdown = lax.broadcast_in_dim(late_kinds[0], reach.shape, (0,)) == 0
+    reach = jnp.where(showdown, reach, -reach)
     pots = jnp.pad(pot_size, ((0, 0), (0, extra)))
     old_regrets = jnp.pad(regrets[0], ((0, extra), (0, 0)))
-    mate_reach, mate_kinds = swap(reach, group, core), swap(kinds, group, core)
-    held_tables = unpack(jnp.asarray(table(hand_count)), boards)
+    mate_reach = swap(reach, group, core)
+    held_tables = [jnp.asarray(table) for table in tables(hand_count)]
     rows, wide = reach.shape[0], up(hand_count, LANE)
     own, for_mate, all_reach, lines, boards = board_sums(
         functools.partial(first_kernel, hand_count, line_count),
         "first_boards",
         rows,
-        (reach, mate_reach, mate_kinds),
+        (reach, mate_reach),
         held_tables,
         boards,
         more=(

time: 26.3 us -> 25.9 us (0.985)
  Pallas kernels: 9.79 us -> 9.03 us
  local copies, waits for them, and re-layouts: 0.7 us -> 1.02 us
  waiting for transfers between devices: 5.16 us -> 4.87 us
    pallas_call x1 -> x0, Pallas kernels: 0.4 us -> none  [unpack(): pl.pallas_call(unpack_kernel, out_shape=[jax.ShapeDtypeStruct(shape, jnp....]
    pallas_call x3, Pallas kernels: 7.28 us -> 6.92 us  [board_sums(): pl.pallas_call(kernel, out_shape=out, in_specs=[WHOLE] * (len(inputs) + l...]
    unnamed x18 -> x22, local copies, waits for them, and re-layouts: 0.7 us -> 1.02 us
    ppermute x8 -> x7, waiting for transfers between devices: 5.16 us -> 4.87 us  [swap(): lax.ppermute(array, axes, [(index, index ^ mask) for index in range(lax.a...]
    ppermute x8 -> x7, starting transfers between devices: 9.56 us -> 9.79 us  [swap(): lax.ppermute(array, axes, [(index, index ^ mask) for index in range(lax.a...]
  transfers between devices with their start and end apart: 8 -> 7, of which waited for: 4 -> 3; matrix products, arithmetic and copies ran while one was open for 0% -> 0% of each run, Pallas kernels for 20% -> 18%
where the time goes in v6:
time: 25.9 us; the launch traced here: 25.7 us
  starting transfers between devices  9.79 us (38%)
  Pallas kernels  9.03 us (35%)
  waiting for transfers between devices  4.87 us (19%)
  local copies, waits for them, and re-layouts  1.02 us (4%)
  between operations  0.83 us (3%)
    ppermute x7, starting transfers between devices, swap(): lax.ppermute(array, axes, [(index, index ^ mask) for index in range(lax.a...  9.79 us
    pallas_call x3, Pallas kernels, board_sums(): pl.pallas_call(kernel, out_shape=out, in_specs=[WHOLE] * (len(inputs) + l...  6.92 us
    ppermute x7, waiting for transfers between devices, swap(): lax.ppermute(array, axes, [(index, index ^ mask) for index in range(lax.a...  4.87 us
    pallas_call x2, Pallas kernels, decision_call(): pl.pallas_call(functools.partial(kernel, hand_count, scale), out_shape=ou...  1.28 us
    unnamed x22, local copies, waits for them, and re-layouts  1.02 us
    pallas_call x1, Pallas kernels, chance(): pl.pallas_call(functools.partial(chance_kernel, hand_count, order), out_s...  0.81 us
  transfers between devices with their start and end apart: 7, of which 3 were waited for; matrix products, arithmetic and copies ran while one was open for 0% of the time, Pallas kernels for 18%

profile of v6, /device:TPU:0, one launch (start us, length us, event | category | flops | bytes accessed | tf_op | source)
XLA Modules:
  0.0 25.7 jit_solution(3855716622381620132)
XLA Ops:
  0.6 0.0 copy-start
  0.6 0.0 copy-start.1
  0.7 0.0 copy-start.2
  0.7 0.0 copy-start.6
  0.7 0.0 copy-start.4
  0.7 0.0 copy-start.10
  0.7 0.0 copy-start.8
  0.7 0.0 copy-start.7
  0.7 0.0 copy-start.9
  0.8 0.8 %copy-done.4 = s32[1,32]{1,0:T(1,128)S(1)} copy-done((s32[1,32]{1,0:T(1,128)S(1)}, s32[1,32]{1,0:T(1,128)}, u32[]{:S(2)}) %copy-start.4) | copy-done | bytes 152
  1.5 0.2 copy-done.6
  1.7 0.1 negate_select_fusion.own_ref
  1.8 0.5 %collective-permute-start = (bf16[32,1326]{1,0:T(8,128)(2,1)S(1)}, bf16[32,1326]{1,0:T(8,128)(2,1)S(1)}, u32[]{:S(2)}, u32[]{:S(2)}) collective-permute-start(bf16[32,1326]{1,0:T(8,128)(2,1)S(1)} %negate_select_fusion.own_ref), channel_id=1, source_target_pairs={{0,2},{1,3},{2,0},{3,1},{4,6},{5,7},{6,4},{7,5},{8,10},{9,11},{10,... | collective-permute-start | bytes 254600 | tf_op jit(solution)/shard_map/ppermute | solution.py:300
  2.3 0.0 copy-done.10
  2.3 0.0 copy-done.8
  2.4 0.0 copy-done.7
  2.4 0.0 copy-done.9
  2.4 0.1 add_select_fusion.refs_3_
  2.4 2.5 %collective-permute-start.1 = (s32[2,1792]{1,0:T(2,128)S(1)}, s32[2,1792]{1,0:T(2,128)S(1)}, u32[]{:S(2)}, u32[]{:S(2)}) collective-permute-start(s32[2,1792]{1,0:T(2,128)S(1)} %add_select_fusion.refs_3_), channel_id=1, source_target_pairs={{0,1},{1,0},{2,3},{3,2},{4,5},{5,4},{6,7},{7,6},{8,9},{9,8},{10,11... | collective-permute-start | bytes 43016 | tf_op jit(solution)/shard_map/ppermute | solution.py:300
  5.0 0.0 collective-permute-done.mate_ref
  5.0 0.0 copy-done
  5.0 0.0 copy-done.1
  5.0 0.0 copy-done.2
  5.0 1.8 %first_boards.1 = (f32[32,1408]{1,0:T(8,128)S(1)}, f32[32,1408]{1,0:T(8,128)S(1)}, bf16[64,1408]{1,0:T(8,128)(2,1)S(1)}, s32[64,128]{1,0:T(8,128)S(1)}, s32[2,1792]{1,0:T(2,128)S(1)}) custom-call(bf16[32,1326]{1,0:T(8,128)(2,1)S(1)} %negate_select_fusion.own_ref, bf16[32,1326]{1,0:T(8,128)(2,1)S(1)} %collective-permute-done.mate_ref, ...), custom_call_target="tpu_custom_call" | custom-call | flops 507510784 | tf_op jit(solution)/shard_map/first_boards/pallas_call | solution.py:188
  6.8 0.0 collective-permute-done.1.refs_3_
  6.8 2.0 %collective-permute-start.2 = (s32[4,1792]{1,0:T(4,128)S(1)}, s32[4,1792]{1,0:T(4,128)S(1)}, u32[]{:S(2)}, u32[]{:S(2)}) collective-permute-start(s32[4,1792]{1,0:T(4,128)S(1)} %pad_add_fusion), channel_id=1, source_target_pairs={{0,4},{1,5},{2,6},{3,7},{4,0},{5,1},{6,2},{7,3},{8,12},{9,13},{10,... | collective-permute-start | bytes 86024 | tf_op jit(solution)/shard_map/ppermute | solution.py:300
  8.8 1.9 %more_boards.2 = (f32[32,1408]{1,0:T(8,128)S(1)}, f32[32,1408]{1,0:T(8,128)S(1)}) custom-call(bf16[64,1408]{1,0:T(8,128)(2,1)S(1)} %get-tuple-element.15.reach_ref, s32[64,128]{1,0:T(8,128)S(1)} %get-tuple-element.16.line_ref, bf16[1328,1408]{1,0:T(8,128)(2,1)S(1)} %copy-done, bf16[1408,128]{1,0:T(8,128)(2,1)S(1)} %copy-done.1, ...), custom_call_target="tpu_custom_call" | custom-call | flops 507510784 | tf_op jit(solution)/shard_map/more_boards/pallas_call | solution.py:188
  10.7 0.0 copy-start.3
  10.7 0.0 copy-start.5
  10.8 0.0 collective-permute-done.2.refs_3_
  10.8 3.2 %more_boards.3 = (f32[32,1408]{1,0:T(8,128)S(1)}, f32[32,1408]{1,0:T(8,128)S(1)}) custom-call(bf16[64,1408]{1,0:T(8,128)(2,1)S(1)} %get-tuple-element.15.reach_ref, s32[64,128]{1,0:T(8,128)S(1)} %get-tuple-element.16.line_ref, bf16[1328,1408]{1,0:T(8,128)(2,1)S(1)} %copy-done, bf16[1408,128]{1,0:T(8,128)(2,1)S(1)} %copy-done.1, ...), custom_call_target="tpu_custom_call" | custom-call | flops 1015021568 | tf_op jit(solution)/shard_map/more_boards/pallas_call | solution.py:188
  14.0 0.1 collective-permute-start.3
  14.1 1.4 %collective-permute-done.3.refs_1_ = f32[32,1408]{1,0:T(8,128)S(1)} collective-permute-done((f32[32,1408]{1,0:T(8,128)S(1)}, f32[32,1408]{1,0:T(8,128)S(1)}, u32[]{:S(2)}, u32[]{:S(2)}) %collective-permute-start.3) | collective-permute-done | bytes 180256 | tf_op jit(solution)/shard_map/ppermute | solution.py:300
  15.5 0.0 copy-done.3
  15.5 0.0 copy-done.5
  15.5 0.4 %node_codes.1.refs_0_ = s16[16,1408]{1,0:T(8,128)(2,1)S(1)} custom-call(f32[32,1408]{1,0:T(8,128)S(1)} %get-tuple-element.22.refs_0_, f32[32,1408]{1,0:T(8,128)S(1)} %collective-permute-done.3.refs_1_, s32[1,32]{1,0:T(1,128)S(1)} %copy-done.5, s32[1,32]{1,0:T(1,128)S(1)} %copy-done.4, f32[32,1326]{1,0:T(8,128)S(1)} %bitcast.9), custom_call_target="tpu_custom_call" | custom-call | tf_op jit(solution)/shard_map/node_codes/pallas_call | solution.py:258
  15.9 4.1 %collective-permute-start.4 = (s16[16,1408]{1,0:T(8,128)(2,1)S(1)}, s16[16,1408]{1,0:T(8,128)(2,1)S(1)}, u32[]{:S(2)}, u32[]{:S(2)}) collective-permute-start(s16[16,1408]{1,0:T(8,128)(2,1)S(1)} %node_codes.1.refs_0_), channel_id=1, source_target_pairs={{0,24},{8,16},{16,8},{24,0},{1,25},{9,17},{17,9},{25,1},{2,26},{10... | collective-permute-start | bytes 135176 | tf_op jit(solution)/shard_map/ppermute | solution.py:300
  20.0 0.0 collective-permute-start.5
  20.0 0.6 %collective-permute-start.6 = (s16[16,1408]{1,0:T(8,128)(2,1)S(1)}, s16[16,1408]{1,0:T(8,128)(2,1)S(1)}, u32[]{:S(2)}, u32[]{:S(2)}) collective-permute-start(s16[16,1408]{1,0:T(8,128)(2,1)S(1)} %node_codes.1.refs_0_), channel_id=1, source_target_pairs={{0,8},{8,0},{16,24},{24,16},{1,9},{9,1},{17,25},{25,17},{2,10},{10... | collective-permute-start | bytes 135176 | tf_op jit(solution)/shard_map/ppermute | solution.py:300
  20.6 0.9 %new_regrets.1 = f32[32,1326]{1,0:T(8,128)} custom-call(f32[32,1408]{1,0:T(8,128)S(1)} %get-tuple-element.22.refs_0_, f32[32,1408]{1,0:T(8,128)S(1)} %collective-permute-done.3.refs_1_, s32[1,32]{1,0:T(1,128)S(1)} %copy-done.5, s32[1,32]{1,0:T(1,128)S(1)} %copy-done.4, f32[32,1326]{1,0:T(8,128)S(1)} %bitcast.10), custom_call_target="tpu_custom_call" | custom-call | tf_op jit(solution)/shard_map/new_regrets/pallas_call | solution.py:258
  21.5 0.6 %collective-permute-done.4.refs_1_ = s16[16,1408]{1,0:T(8,128)(2,1)S(1)} collective-permute-done((s16[16,1408]{1,0:T(8,128)(2,1)S(1)}, s16[16,1408]{1,0:T(8,128)(2,1)S(1)}, u32[]{:S(2)}, u32[]{:S(2)}) %collective-permute-start.4) | collective-permute-done | bytes 45088 | tf_op jit(solution)/shard_map/ppermute | solution.py:300
  22.0 2.9 %collective-permute-done.5.refs_2_ = s16[16,1408]{1,0:T(8,128)(2,1)S(1)} collective-permute-done((s16[16,1408]{1,0:T(8,128)(2,1)S(1)}, s16[16,1408]{1,0:T(8,128)(2,1)S(1)}, u32[]{:S(2)}, u32[]{:S(2)}) %collective-permute-start.5) | collective-permute-done | bytes 45088 | tf_op jit(solution)/shard_map/ppermute | solution.py:300
  24.9 0.0 collective-permute-done.6.refs_3_
  24.9 0.8 %chance_sum.1 = f32[16,1326]{1,0:T(8,128)} custom-call(s16[16,1408]{1,0:T(8,128)(2,1)S(1)} %node_codes.1.refs_0_, s16[16,1408]{1,0:T(8,128)(2,1)S(1)} %collective-permute-done.4.refs_1_, s16[16,1408]{1,0:T(8,128)(2,1)S(1)} %collective-permute-done.5.refs_2_, s16[16,1408]{1,0:T(8,128)(2,1)S(1)} %collective-permute-done.6.refs_3_), custom_call_target="tpu_custom_call" | custom-call | tf_op jit(solution)/shard_map/chance_sum/pallas_call | solution.py:289
  (4 shorter events, 0.0 us)
Async XLA Ops:
  0.6 4.4 %copy-start = (bf16[1328,1408]{1,0:T(8,128)(2,1)S(1)}, bf16[1328,1408]{1,0:T(8,128)(2,1)}, u32[]{:S(2)}) copy-start(bf16[1328,1408]{1,0:T(8,128)(2,1)} %constant.5.clone.refs_0_) | copy-start | bytes 11218948
  0.6 4.3 %copy-start.1 = (bf16[1408,128]{1,0:T(8,128)(2,1)S(1)}, bf16[1408,128]{1,0:T(8,128)(2,1)}, u32[]{:S(2)}) copy-start(bf16[1408,128]{1,0:T(8,128)(2,1)} %constant.14.clone.refs_1_) | copy-start | bytes 1081348
  0.7 4.3 %copy-start.2 = (bf16[128,1408]{1,0:T(8,128)(2,1)S(1)}, bf16[128,1408]{1,0:T(8,128)(2,1)}, u32[]{:S(2)}) copy-start(bf16[128,1408]{1,0:T(8,128)(2,1)} %constant.15.clone.refs_2_) | copy-start | bytes 1081348
  0.7 1.1 %copy-start.6 = (bf16[1,32,1326]{2,1,0:T(8,128)(2,1)S(1)}, bf16[1,32,1326]{2,1,0:T(8,128)(2,1)}, u32[]{:S(2)}) copy-start(bf16[1,32,1326]{2,1,0:T(8,128)(2,1)} %param.12) | copy-start | bytes 254596
  0.7 0.8 %copy-start.4 = (s32[1,32]{1,0:T(1,128)S(1)}, s32[1,32]{1,0:T(1,128)}, u32[]{:S(2)}) copy-start(s32[1,32]{1,0:T(1,128)} %refs_3_.3) | copy-start | bytes 388
  0.7 1.7 %copy-start.10 = (s32[1,1,2]{2,1,0:T(1,128)S(1)}, s32[1,1,2]{2,1,0:T(1,128)}, u32[]{:S(2)}) copy-start(s32[1,1,2]{2,1,0:T(1,128)} %param.16) | copy-start | bytes 28
  0.7 1.6 %copy-start.8 = (s32[1,1,2,1326]{3,2,1,0:T(2,128)S(1)}, s32[1,1,2,1326]{3,2,1,0:T(2,128)}, u32[]{:S(2)}) copy-start(s32[1,1,2,1326]{3,2,1,0:T(2,128)} %param.17) | copy-start | bytes 31828
  0.7 1.6 %copy-start.7 = (s32[1,1,2,1326]{3,2,1,0:T(2,128)S(1)}, s32[1,1,2,1326]{3,2,1,0:T(2,128)}, u32[]{:S(2)}) copy-start(s32[1,1,2,1326]{3,2,1,0:T(2,128)} %param.18) | copy-start | bytes 31828
  0.7 1.6 %copy-start.9 = (s32[1,1,2,256]{3,2,1,0:T(2,128)S(1)}, s32[1,1,2,256]{3,2,1,0:T(2,128)}, u32[]{:S(2)}) copy-start(s32[1,1,2,256]{3,2,1,0:T(2,128)} %param.15) | copy-start | bytes 6148
  1.8 3.2 %collective-permute-start = (bf16[32,1326]{1,0:T(8,128)(2,1)S(1)}, bf16[32,1326]{1,0:T(8,128)(2,1)S(1)}, u32[]{:S(2)}, u32[]{:S(2)}) collective-permute-start(bf16[32,1326]{1,0:T(8,128)(2,1)S(1)} %negate_select_fusion.own_ref), channel_id=1, source_target_pairs={{0,2},{1,3},{2,0},{3,1},{4,6},{5,7},{6,4},{7,5},{8,10},{9,11},{10,... | collective-permute-start | bytes 254600 | tf_op jit(solution)/shard_map/ppermute | solution.py:300
  2.4 4.4 %collective-permute-start.1 = (s32[2,1792]{1,0:T(2,128)S(1)}, s32[2,1792]{1,0:T(2,128)S(1)}, u32[]{:S(2)}, u32[]{:S(2)}) collective-permute-start(s32[2,1792]{1,0:T(2,128)S(1)} %add_select_fusion.refs_3_), channel_id=1, source_target_pairs={{0,1},{1,0},{2,3},{3,2},{4,5},{5,4},{6,7},{7,6},{8,9},{9,8},{10,11... | collective-permute-start | bytes 43016 | tf_op jit(solution)/shard_map/ppermute | solution.py:300
  6.8 3.9 %collective-permute-start.2 = (s32[4,1792]{1,0:T(4,128)S(1)}, s32[4,1792]{1,0:T(4,128)S(1)}, u32[]{:S(2)}, u32[]{:S(2)}) collective-permute-start(s32[4,1792]{1,0:T(4,128)S(1)} %pad_add_fusion), channel_id=1, source_target_pairs={{0,4},{1,5},{2,6},{3,7},{4,0},{5,1},{6,2},{7,3},{8,12},{9,13},{10,... | collective-permute-start | bytes 86024 | tf_op jit(solution)/shard_map/ppermute | solution.py:300
  10.7 4.8 %copy-start.3 = (f32[1,32,1326]{2,1,0:T(8,128)S(1)}, f32[1,32,1326]{2,1,0:T(8,128)}, u32[]{:S(2)}) copy-start(f32[1,32,1326]{2,1,0:T(8,128)} %param.11) | copy-start | bytes 509188
  10.7 4.7 %copy-start.5 = (s32[1,32]{1,0:T(1,128)S(1)}, s32[1,32]{1,0:T(1,128)}, u32[]{:S(2)}) copy-start(s32[1,32]{1,0:T(1,128)} %refs_2_.6) | copy-start | bytes 388
  14.0 1.5 %collective-permute-start.3 = (f32[32,1408]{1,0:T(8,128)S(1)}, f32[32,1408]{1,0:T(8,128)S(1)}, u32[]{:S(2)}, u32[]{:S(2)}) collective-permute-start(f32[32,1408]{1,0:T(8,128)S(1)} %get-tuple-element.23), channel_id=1, source_target_pairs={{0,2},{1,3},{2,0},{3,1},{4,6},{5,7},{6,4},{7,5},{8,10},{9,11},{10,... | collective-permute-start | bytes 540680 | tf_op jit(solution)/shard_map/ppermute | solution.py:300
  15.9 6.1 %collective-permute-start.4 = (s16[16,1408]{1,0:T(8,128)(2,1)S(1)}, s16[16,1408]{1,0:T(8,128)(2,1)S(1)}, u32[]{:S(2)}, u32[]{:S(2)}) collective-permute-start(s16[16,1408]{1,0:T(8,128)(2,1)S(1)} %node_codes.1.refs_0_), channel_id=1, source_target_pairs={{0,24},{8,16},{16,8},{24,0},{1,25},{9,17},{17,9},{25,1},{2,26},{10... | collective-permute-start | bytes 135176 | tf_op jit(solution)/shard_map/ppermute | solution.py:300
  20.0 4.9 %collective-permute-start.5 = (s16[16,1408]{1,0:T(8,128)(2,1)S(1)}, s16[16,1408]{1,0:T(8,128)(2,1)S(1)}, u32[]{:S(2)}, u32[]{:S(2)}) collective-permute-start(s16[16,1408]{1,0:T(8,128)(2,1)S(1)} %node_codes.1.refs_0_), channel_id=1, source_target_pairs={{0,16},{8,24},{16,0},{24,8},{1,17},{9,25},{17,1},{25,9},{2,18},{10... | collective-permute-start | bytes 135176 | tf_op jit(solution)/shard_map/ppermute | solution.py:300
  20.0 4.9 %collective-permute-start.6 = (s16[16,1408]{1,0:T(8,128)(2,1)S(1)}, s16[16,1408]{1,0:T(8,128)(2,1)S(1)}, u32[]{:S(2)}, u32[]{:S(2)}) collective-permute-start(s16[16,1408]{1,0:T(8,128)(2,1)S(1)} %node_codes.1.refs_0_), channel_id=1, source_target_pairs={{0,8},{8,0},{16,24},{24,16},{1,9},{9,1},{17,25},{25,17},{2,10},{10... | collective-permute-start | bytes 135176 | tf_op jit(solution)/shard_map/ppermute | solution.py:300

commit v7 on v6

--- a/solution.py
+++ b/solution.py
@@ -82,8 +82,24 @@
         out_specs=WHOLE,
         compiler_params=params(4),
         name="first_lines",
+        cost_estimate=pl.CostEstimate(flops=10 * 10**9, bytes_accessed=0, transcendentals=0),
+    )()
+
+
+def pass_kernel(in_ref, out_ref):
+    out_ref[...] = in_ref[...]
+
+
+def pass_on(array):
+    return pl.pallas_call(
+        pass_kernel,
+        out_shape=jax.ShapeDtypeStruct(array.shape, array.dtype),
+        in_specs=[WHOLE],
+        out_specs=WHOLE,
+        compiler_params=params(4),
+        name="pass_on",
         cost_estimate=pl.CostEstimate(flops=60 * 10**9, bytes_accessed=0, transcendentals=0),
-    )()
+    )(array)
 
 
 def pack(counts, slots, ranks, live, bases):
@@ -310,7 +326,7 @@
     core = lax.axis_size("river")
     board_total = group_size * board_lines.shape[2]
     extra = up(line_count, SUB) - line_count
-    bases = first_lines(line_count, core)
+    bases = pass_on(first_lines(line_count, core))
     kinds = jnp.pad(line_kind, ((0, 0), (0, extra)))
     boards = pack(board_count[0, 0], board_lines[0, 0], hand_ranks[0, 0], live_hands[0, 0], bases)
     masks = [1 << bit for bit in range(group_size.bit_length() - 1) if 1 << bit != core]

time: 25.9 us -> 25.7 us (level)
  transfers between devices with their start and end apart: 7 -> 7, of which waited for: 3 -> 4; matrix products, arithmetic and copies ran while one was open for 0% -> 0% of each run, Pallas kernels for 18% -> 18%
where the time goes in v7:
time: 25.7 us; the launch traced here: 25.6 us
  starting transfers between devices  9.59 us (37%)
  Pallas kernels  9.19 us (36%)
  waiting for transfers between devices  4.91 us (19%)
  local copies, waits for them, and re-layouts  0.85 us (3%)
  between operations  0.84 us (3%)
    ppermute x7, starting transfers between devices, swap(): lax.ppermute(array, axes, [(index, index ^ mask) for index in range(lax.a...  9.59 us
    pallas_call x3, Pallas kernels, board_sums(): pl.pallas_call(kernel, out_shape=out, in_specs=[WHOLE] * (len(inputs) + l...  7.08 us
    ppermute x7, waiting for transfers between devices, swap(): lax.ppermute(array, axes, [(index, index ^ mask) for index in range(lax.a...  4.91 us
    pallas_call x2, Pallas kernels, decision_call(): pl.pallas_call(functools.partial(kernel, hand_count, scale), out_shape=ou...  1.28 us
    unnamed x22, local copies, waits for them, and re-layouts  0.85 us
    pallas_call x1, Pallas kernels, chance(): pl.pallas_call(functools.partial(chance_kernel, hand_count, order), out_s...  0.81 us
  transfers between devices with their start and end apart: 7, of which 4 were waited for; matrix products, arithmetic and copies ran while one was open for 0% of the time, Pallas kernels for 18%

profile of v7, /device:TPU:0, one launch (start us, length us, event | category | flops | bytes accessed | tf_op | source)
XLA Modules:
  0.0 25.6 jit_solution(10256230973080441609)
XLA Ops:
  0.7 0.0 copy-start.4
  0.7 0.0 copy-start.6
  0.7 0.0 copy-start.7
  0.7 0.0 copy-start.8
  0.7 0.0 copy-start.9
  0.7 0.0 copy-start.10
  0.7 0.0 copy-start
  0.7 0.0 copy-start.1
  0.7 0.0 copy-start.2
  0.8 0.5 %copy-done.4 = s32[1,32]{1,0:T(1,128)S(1)} copy-done((s32[1,32]{1,0:T(1,128)S(1)}, s32[1,32]{1,0:T(1,128)}, u32[]{:S(2)}) %copy-start.4) | copy-done | bytes 152
  1.3 0.2 copy-done.6
  1.6 0.1 negate_select_fusion.own_ref
  1.6 0.5 %collective-permute-start = (bf16[32,1326]{1,0:T(8,128)(2,1)S(1)}, bf16[32,1326]{1,0:T(8,128)(2,1)S(1)}, u32[]{:S(2)}, u32[]{:S(2)}) collective-permute-start(bf16[32,1326]{1,0:T(8,128)(2,1)S(1)} %negate_select_fusion.own_ref), channel_id=1, source_target_pairs={{0,2},{1,3},{2,0},{3,1},{4,6},{5,7},{6,4},{7,5},{8,10},{9,11},{10,... | collective-permute-start | bytes 254600 | tf_op jit(solution)/shard_map/ppermute | solution.py:316
  2.2 0.0 copy-done.7
  2.2 0.0 copy-done.8
  2.2 0.0 copy-done.9
  2.2 0.0 copy-done.10
  2.2 0.1 add_select_fusion.refs_3_
  2.3 2.5 %collective-permute-start.1 = (s32[2,1792]{1,0:T(2,128)S(1)}, s32[2,1792]{1,0:T(2,128)S(1)}, u32[]{:S(2)}, u32[]{:S(2)}) collective-permute-start(s32[2,1792]{1,0:T(2,128)S(1)} %add_select_fusion.refs_3_), channel_id=1, source_target_pairs={{0,1},{1,0},{2,3},{3,2},{4,5},{5,4},{6,7},{7,6},{8,9},{9,8},{10,11... | collective-permute-start | bytes 43016 | tf_op jit(solution)/shard_map/ppermute | solution.py:316
  4.8 0.0 collective-permute-done.mate_ref
  4.8 0.0 copy-done
  4.8 0.0 copy-done.1
  4.8 0.0 copy-done.2
  4.8 1.9 %first_boards.1 = (f32[32,1408]{1,0:T(8,128)S(1)}, f32[32,1408]{1,0:T(8,128)S(1)}, bf16[64,1408]{1,0:T(8,128)(2,1)S(1)}, s32[64,128]{1,0:T(8,128)S(1)}, s32[2,1792]{1,0:T(2,128)S(1)}) custom-call(bf16[32,1326]{1,0:T(8,128)(2,1)S(1)} %negate_select_fusion.own_ref, bf16[32,1326]{1,0:T(8,128)(2,1)S(1)} %collective-permute-done.mate_ref, ...), custom_call_target="tpu_custom_call" | custom-call | flops 507510784 | tf_op jit(solution)/shard_map/first_boards/pallas_call | solution.py:204
  6.7 0.0 collective-permute-done.1.refs_3_
  6.8 1.9 %collective-permute-start.2 = (s32[4,1792]{1,0:T(4,128)S(1)}, s32[4,1792]{1,0:T(4,128)S(1)}, u32[]{:S(2)}, u32[]{:S(2)}) collective-permute-start(s32[4,1792]{1,0:T(4,128)S(1)} %pad_add_fusion), channel_id=1, source_target_pairs={{0,4},{1,5},{2,6},{3,7},{4,0},{5,1},{6,2},{7,3},{8,12},{9,13},{10,... | collective-permute-start | bytes 86024 | tf_op jit(solution)/shard_map/ppermute | solution.py:316
  8.6 2.0 %more_boards.2 = (f32[32,1408]{1,0:T(8,128)S(1)}, f32[32,1408]{1,0:T(8,128)S(1)}) custom-call(bf16[64,1408]{1,0:T(8,128)(2,1)S(1)} %get-tuple-element.15.reach_ref, s32[64,128]{1,0:T(8,128)S(1)} %get-tuple-element.16.line_ref, bf16[1328,1408]{1,0:T(8,128)(2,1)S(1)} %copy-done, bf16[1408,128]{1,0:T(8,128)(2,1)S(1)} %copy-done.1, ...), custom_call_target="tpu_custom_call" | custom-call | flops 507510784 | tf_op jit(solution)/shard_map/more_boards/pallas_call | solution.py:204
  10.6 0.0 copy-start.3
  10.6 0.0 copy-start.5
  10.6 0.1 collective-permute-done.2.refs_3_
  10.7 3.2 %more_boards.3 = (f32[32,1408]{1,0:T(8,128)S(1)}, f32[32,1408]{1,0:T(8,128)S(1)}) custom-call(bf16[64,1408]{1,0:T(8,128)(2,1)S(1)} %get-tuple-element.15.reach_ref, s32[64,128]{1,0:T(8,128)S(1)} %get-tuple-element.16.line_ref, bf16[1328,1408]{1,0:T(8,128)(2,1)S(1)} %copy-done, bf16[1408,128]{1,0:T(8,128)(2,1)S(1)} %copy-done.1, ...), custom_call_target="tpu_custom_call" | custom-call | flops 1015021568 | tf_op jit(solution)/shard_map/more_boards/pallas_call | solution.py:204
  13.9 0.1 collective-permute-start.3
  14.0 1.4 %collective-permute-done.3.refs_1_ = f32[32,1408]{1,0:T(8,128)S(1)} collective-permute-done((f32[32,1408]{1,0:T(8,128)S(1)}, f32[32,1408]{1,0:T(8,128)S(1)}, u32[]{:S(2)}, u32[]{:S(2)}) %collective-permute-start.3) | collective-permute-done | bytes 180256 | tf_op jit(solution)/shard_map/ppermute | solution.py:316
  15.4 0.0 copy-done.3
  15.4 0.0 copy-done.5
  15.4 0.4 %node_codes.1.refs_0_ = s16[16,1408]{1,0:T(8,128)(2,1)S(1)} custom-call(f32[32,1408]{1,0:T(8,128)S(1)} %get-tuple-element.22.refs_0_, f32[32,1408]{1,0:T(8,128)S(1)} %collective-permute-done.3.refs_1_, s32[1,32]{1,0:T(1,128)S(1)} %copy-done.5, s32[1,32]{1,0:T(1,128)S(1)} %copy-done.4, f32[32,1326]{1,0:T(8,128)S(1)} %bitcast.9), custom_call_target="tpu_custom_call" | custom-call | tf_op jit(solution)/shard_map/node_codes/pallas_call | solution.py:274
  15.8 4.0 %collective-permute-start.4 = (s16[16,1408]{1,0:T(8,128)(2,1)S(1)}, s16[16,1408]{1,0:T(8,128)(2,1)S(1)}, u32[]{:S(2)}, u32[]{:S(2)}) collective-permute-start(s16[16,1408]{1,0:T(8,128)(2,1)S(1)} %node_codes.1.refs_0_), channel_id=1, source_target_pairs={{0,24},{8,16},{16,8},{24,0},{1,25},{9,17},{17,9},{25,1},{2,26},{10... | collective-permute-start | bytes 135176 | tf_op jit(solution)/shard_map/ppermute | solution.py:316
  19.8 0.0 collective-permute-start.5
  19.8 0.6 %collective-permute-start.6 = (s16[16,1408]{1,0:T(8,128)(2,1)S(1)}, s16[16,1408]{1,0:T(8,128)(2,1)S(1)}, u32[]{:S(2)}, u32[]{:S(2)}) collective-permute-start(s16[16,1408]{1,0:T(8,128)(2,1)S(1)} %node_codes.1.refs_0_), channel_id=1, source_target_pairs={{0,8},{8,0},{16,24},{24,16},{1,9},{9,1},{17,25},{25,17},{2,10},{10... | collective-permute-start | bytes 135176 | tf_op jit(solution)/shard_map/ppermute | solution.py:316
  20.4 0.9 %new_regrets.1 = f32[32,1326]{1,0:T(8,128)} custom-call(f32[32,1408]{1,0:T(8,128)S(1)} %get-tuple-element.22.refs_0_, f32[32,1408]{1,0:T(8,128)S(1)} %collective-permute-done.3.refs_1_, s32[1,32]{1,0:T(1,128)S(1)} %copy-done.5, s32[1,32]{1,0:T(1,128)S(1)} %copy-done.4, f32[32,1326]{1,0:T(8,128)S(1)} %bitcast.10), custom_call_target="tpu_custom_call" | custom-call | tf_op jit(solution)/shard_map/new_regrets/pallas_call | solution.py:274
  21.3 0.6 %collective-permute-done.4.refs_1_ = s16[16,1408]{1,0:T(8,128)(2,1)S(1)} collective-permute-done((s16[16,1408]{1,0:T(8,128)(2,1)S(1)}, s16[16,1408]{1,0:T(8,128)(2,1)S(1)}, u32[]{:S(2)}, u32[]{:S(2)}) %collective-permute-start.4) | collective-permute-done | bytes 45088 | tf_op jit(solution)/shard_map/ppermute | solution.py:316
  21.9 2.9 %collective-permute-done.5.refs_2_ = s16[16,1408]{1,0:T(8,128)(2,1)S(1)} collective-permute-done((s16[16,1408]{1,0:T(8,128)(2,1)S(1)}, s16[16,1408]{1,0:T(8,128)(2,1)S(1)}, u32[]{:S(2)}, u32[]{:S(2)}) %collective-permute-start.5) | collective-permute-done | bytes 45088 | tf_op jit(solution)/shard_map/ppermute | solution.py:316
  24.7 0.0 collective-permute-done.6.refs_3_
  24.7 0.8 %chance_sum.1 = f32[16,1326]{1,0:T(8,128)} custom-call(s16[16,1408]{1,0:T(8,128)(2,1)S(1)} %node_codes.1.refs_0_, s16[16,1408]{1,0:T(8,128)(2,1)S(1)} %collective-permute-done.4.refs_1_, s16[16,1408]{1,0:T(8,128)(2,1)S(1)} %collective-permute-done.5.refs_2_, s16[16,1408]{1,0:T(8,128)(2,1)S(1)} %collective-permute-done.6.refs_3_), custom_call_target="tpu_custom_call" | custom-call | tf_op jit(solution)/shard_map/chance_sum/pallas_call | solution.py:305
  (5 shorter events, 0.0 us)
Async XLA Ops:
  0.7 0.7 %copy-start.4 = (s32[1,32]{1,0:T(1,128)S(1)}, s32[1,32]{1,0:T(1,128)}, u32[]{:S(2)}) copy-start(s32[1,32]{1,0:T(1,128)} %refs_3_.3) | copy-start | bytes 388
  0.7 0.9 %copy-start.6 = (bf16[1,32,1326]{2,1,0:T(8,128)(2,1)S(1)}, bf16[1,32,1326]{2,1,0:T(8,128)(2,1)}, u32[]{:S(2)}) copy-start(bf16[1,32,1326]{2,1,0:T(8,128)(2,1)} %param.12) | copy-start | bytes 254596
  0.7 1.5 %copy-start.7 = (s32[1,1,2,1326]{3,2,1,0:T(2,128)S(1)}, s32[1,1,2,1326]{3,2,1,0:T(2,128)}, u32[]{:S(2)}) copy-start(s32[1,1,2,1326]{3,2,1,0:T(2,128)} %param.18) | copy-start | bytes 31828
  0.7 1.5 %copy-start.8 = (s32[1,1,2,1326]{3,2,1,0:T(2,128)S(1)}, s32[1,1,2,1326]{3,2,1,0:T(2,128)}, u32[]{:S(2)}) copy-start(s32[1,1,2,1326]{3,2,1,0:T(2,128)} %param.17) | copy-start | bytes 31828
  0.7 1.5 %copy-start.9 = (s32[1,1,2,256]{3,2,1,0:T(2,128)S(1)}, s32[1,1,2,256]{3,2,1,0:T(2,128)}, u32[]{:S(2)}) copy-start(s32[1,1,2,256]{3,2,1,0:T(2,128)} %param.15) | copy-start | bytes 6148
  0.7 1.5 %copy-start.10 = (s32[1,1,2]{2,1,0:T(1,128)S(1)}, s32[1,1,2]{2,1,0:T(1,128)}, u32[]{:S(2)}) copy-start(s32[1,1,2]{2,1,0:T(1,128)} %param.16) | copy-start | bytes 28
  0.7 4.1 %copy-start = (bf16[1328,1408]{1,0:T(8,128)(2,1)S(1)}, bf16[1328,1408]{1,0:T(8,128)(2,1)}, u32[]{:S(2)}) copy-start(bf16[1328,1408]{1,0:T(8,128)(2,1)} %constant.5.clone.refs_0_) | copy-start | bytes 11218948
  0.7 4.1 %copy-start.1 = (bf16[1408,128]{1,0:T(8,128)(2,1)S(1)}, bf16[1408,128]{1,0:T(8,128)(2,1)}, u32[]{:S(2)}) copy-start(bf16[1408,128]{1,0:T(8,128)(2,1)} %constant.14.clone.refs_1_) | copy-start | bytes 1081348
  0.7 4.1 %copy-start.2 = (bf16[128,1408]{1,0:T(8,128)(2,1)S(1)}, bf16[128,1408]{1,0:T(8,128)(2,1)}, u32[]{:S(2)}) copy-start(bf16[128,1408]{1,0:T(8,128)(2,1)} %constant.15.clone.refs_2_) | copy-start | bytes 1081348
  1.6 3.2 %collective-permute-start = (bf16[32,1326]{1,0:T(8,128)(2,1)S(1)}, bf16[32,1326]{1,0:T(8,128)(2,1)S(1)}, u32[]{:S(2)}, u32[]{:S(2)}) collective-permute-start(bf16[32,1326]{1,0:T(8,128)(2,1)S(1)} %negate_select_fusion.own_ref), channel_id=1, source_target_pairs={{0,2},{1,3},{2,0},{3,1},{4,6},{5,7},{6,4},{7,5},{8,10},{9,11},{10,... | collective-permute-start | bytes 254600 | tf_op jit(solution)/shard_map/ppermute | solution.py:316
  2.3 4.5 %collective-permute-start.1 = (s32[2,1792]{1,0:T(2,128)S(1)}, s32[2,1792]{1,0:T(2,128)S(1)}, u32[]{:S(2)}, u32[]{:S(2)}) collective-permute-start(s32[2,1792]{1,0:T(2,128)S(1)} %add_select_fusion.refs_3_), channel_id=1, source_target_pairs={{0,1},{1,0},{2,3},{3,2},{4,5},{5,4},{6,7},{7,6},{8,9},{9,8},{10,11... | collective-permute-start | bytes 43016 | tf_op jit(solution)/shard_map/ppermute | solution.py:316
  6.8 3.9 %collective-permute-start.2 = (s32[4,1792]{1,0:T(4,128)S(1)}, s32[4,1792]{1,0:T(4,128)S(1)}, u32[]{:S(2)}, u32[]{:S(2)}) collective-permute-start(s32[4,1792]{1,0:T(4,128)S(1)} %pad_add_fusion), channel_id=1, source_target_pairs={{0,4},{1,5},{2,6},{3,7},{4,0},{5,1},{6,2},{7,3},{8,12},{9,13},{10,... | collective-permute-start | bytes 86024 | tf_op jit(solution)/shard_map/ppermute | solution.py:316
  10.6 4.8 %copy-start.3 = (f32[1,32,1326]{2,1,0:T(8,128)S(1)}, f32[1,32,1326]{2,1,0:T(8,128)}, u32[]{:S(2)}) copy-start(f32[1,32,1326]{2,1,0:T(8,128)} %param.11) | copy-start | bytes 509188
  10.6 4.8 %copy-start.5 = (s32[1,32]{1,0:T(1,128)S(1)}, s32[1,32]{1,0:T(1,128)}, u32[]{:S(2)}) copy-start(s32[1,32]{1,0:T(1,128)} %refs_2_.6) | copy-start | bytes 388
  13.9 1.5 %collective-permute-start.3 = (f32[32,1408]{1,0:T(8,128)S(1)}, f32[32,1408]{1,0:T(8,128)S(1)}, u32[]{:S(2)}, u32[]{:S(2)}) collective-permute-start(f32[32,1408]{1,0:T(8,128)S(1)} %get-tuple-element.23), channel_id=1, source_target_pairs={{0,2},{1,3},{2,0},{3,1},{4,6},{5,7},{6,4},{7,5},{8,10},{9,11},{10,... | collective-permute-start | bytes 540680 | tf_op jit(solution)/shard_map/ppermute | solution.py:316
  15.8 6.0 %collective-permute-start.4 = (s16[16,1408]{1,0:T(8,128)(2,1)S(1)}, s16[16,1408]{1,0:T(8,128)(2,1)S(1)}, u32[]{:S(2)}, u32[]{:S(2)}) collective-permute-start(s16[16,1408]{1,0:T(8,128)(2,1)S(1)} %node_codes.1.refs_0_), channel_id=1, source_target_pairs={{0,24},{8,16},{16,8},{24,0},{1,25},{9,17},{17,9},{25,1},{2,26},{10... | collective-permute-start | bytes 135176 | tf_op jit(solution)/shard_map/ppermute | solution.py:316
  19.8 4.9 %collective-permute-start.5 = (s16[16,1408]{1,0:T(8,128)(2,1)S(1)}, s16[16,1408]{1,0:T(8,128)(2,1)S(1)}, u32[]{:S(2)}, u32[]{:S(2)}) collective-permute-start(s16[16,1408]{1,0:T(8,128)(2,1)S(1)} %node_codes.1.refs_0_), channel_id=1, source_target_pairs={{0,16},{8,24},{16,0},{24,8},{1,17},{9,25},{17,1},{25,9},{2,18},{10... | collective-permute-start | bytes 135176 | tf_op jit(solution)/shard_map/ppermute | solution.py:316
  19.8 4.9 %collective-permute-start.6 = (s16[16,1408]{1,0:T(8,128)(2,1)S(1)}, s16[16,1408]{1,0:T(8,128)(2,1)S(1)}, u32[]{:S(2)}, u32[]{:S(2)}) collective-permute-start(s16[16,1408]{1,0:T(8,128)(2,1)S(1)} %node_codes.1.refs_0_), channel_id=1, source_target_pairs={{0,8},{8,0},{16,24},{24,16},{1,9},{9,1},{17,25},{25,17},{2,10},{10... | collective-permute-start | bytes 135176 | tf_op jit(solution)/shard_map/ppermute | solution.py:316

commit v8 on v7

--- a/solution.py
+++ b/solution.py
@@ -15,7 +15,7 @@
 RANK_SPAN = 8192
 MANTISSA = 128
 ROW_TILE = 128
-COL_TILE = 1408
+COL_TILE = 768
 UNROLL = 8
 STEPS = 32767.0
 LOWEST = 100
@@ -132,20 +132,16 @@
     tables, (packed_ref, own_out, mate_out, reach_ref, line_ref, same_ref), scratch = refs[:3], refs[3:9], refs[9:]
     same_ref[...] = packed_ref[...]
     lines_kernel(hand_count, line_count, own_ref, mate_ref, packed_ref, reach_ref, line_ref)
-    own_out[...] = jnp.zeros_like(own_out)
-    mate_out[...] = jnp.zeros_like(mate_out)
-    add_boards(reach_ref, line_ref, *tables, packed_ref, own_out, mate_out, *scratch)
+    add_boards(reach_ref, line_ref, *tables, packed_ref, None, own_out, mate_out, *scratch)
 
 
 def more_kernel(reach_ref, line_ref, *refs):
     tables, (packed_ref, own_ref, mate_ref, own_out, mate_out), scratch = refs[:3], refs[3:8], refs[8:]
-    own_out[...] = own_ref[...]
-    mate_out[...] = mate_ref[...]
-    add_boards(reach_ref, line_ref, *tables, packed_ref, own_out, mate_out, *scratch)
+    add_boards(reach_ref, line_ref, *tables, packed_ref, (own_ref, mate_ref), own_out, mate_out, *scratch)
 
 
 def add_boards(
-    reach_ref, line_ref, apart_ref, collect_ref, spread_ref, packed_ref, own_out, mate_out, column_ref, board_ref
+    reach_ref, line_ref, apart_ref, collect_ref, spread_ref, packed_ref, earlier, own_out, mate_out, column_ref, board_ref
 ):
     wide, deep = apart_ref.shape[1], apart_ref.shape[0]
     rows = own_out.shape[0]
@@ -160,16 +156,15 @@
 
     zero, one = jnp.bfloat16(0), jnp.bfloat16(1)
 
-    def add_board(board):
-        keys = board_ref[pl.ds(board, 1), :wide]
-        slots = board_ref[pl.ds(board, 1), wide:]
+    def order_keys(keys):
         ranks = keys & (RANK_SPAN - 1)
         live = (keys >> (RANK_SPAN.bit_length() - 1)).astype(jnp.float32)
         power = ranks >> (MANTISSA.bit_length() - 1)
         near = jnp.left_shift(1, jnp.minimum(power, 29)).astype(jnp.float32)
         far = jnp.left_shift(1, jnp.maximum(power - 29, 0)).astype(jnp.float32)
-        order = ((ranks & (MANTISSA - 1)) + MANTISSA).astype(jnp.float32) * near * far
-        column_ref[...] = jnp.transpose(jnp.broadcast_to(order, (LANE, wide)))[:deep].astype(jnp.bfloat16)
+        return ((ranks & (MANTISSA - 1)) + MANTISSA).astype(jnp.float32) * near * far, live
+
+    def add_board(column_ref, order, live, slots, before):
         order = order.astype(jnp.bfloat16)
         keep = jnp.max(jnp.where(slots == line, 1.0, 0.0), axis=1, keepdims=True)
         held = reach_ref[...] * live.astype(jnp.bfloat16) * keep.astype(jnp.bfloat16)
@@ -188,14 +183,31 @@
                 total += jnp.dot(show_reach[:, down], matrix, preferred_element_type=jnp.float32)
             total += jnp.dot(sums, spread_ref[:, at], preferred_element_type=jnp.float32)
             total = (total + fold_reach[:, at].astype(jnp.float32)) * live[:, at]
-            own_out[:, at] += total[:rows]
-            mate_out[:, at] += total[rows:]
-
+            if before is None:
+                own_out[:, at] = total[:rows]
+                mate_out[:, at] = total[rows:]
+            else:
+                own_out[:, at] = before[0][:, at] + total[:rows]
+                mate_out[:, at] = before[1][:, at] + total[rows:]
+
+    sums_here = (own_out, mate_out)
     if board_total <= UNROLL:
+        orders, lives = order_keys(packed_ref[:, :wide])
         for board in range(board_total):
-            add_board(board)
+            row = slice(board, board + 1)
+            turned = jnp.transpose(jnp.broadcast_to(orders[row], (LANE, wide)))
+            column_ref[board] = turned[:deep].astype(jnp.bfloat16)
+            slots = board_ref[row, wide:]
+            add_board(column_ref.at[board], orders[row], lives[row], slots, sums_here if board else earlier)
     else:
-        pl.loop(0, board_total)(add_board)
+        own_out[...] = jnp.zeros_like(own_out) if earlier is None else earlier[0][...]
+        mate_out[...] = jnp.zeros_like(mate_out) if earlier is None else earlier[1][...]
+
+        @pl.loop(0, board_total)
+        def add_next(board):
+            order, live = order_keys(board_ref[pl.ds(board, 1), :wide])
+            column_ref[0] = jnp.transpose(jnp.broadcast_to(order, (LANE, wide)))[:deep].astype(jnp.bfloat16)
+            add_board(column_ref.at[0], order, live, board_ref[pl.ds(board, 1), wide:], sums_here)
 
 
 def board_sums(kernel, name, rows, inputs, tables, boards, sums=(), more=()):
@@ -207,7 +219,7 @@
         in_specs=[WHOLE] * (len(inputs) + len(tables) + 1 + len(sums)),
         out_specs=[WHOLE] * len(out),
         scratch_shapes=[
-            pltpu.VMEM((deep, LANE), jnp.bfloat16),
+            pltpu.VMEM((min(boards.shape[0], UNROLL), deep, LANE), jnp.bfloat16),
             pltpu.VMEM((boards.shape[0], boards.shape[1] - LANE), jnp.int32),
         ],
         compiler_params=params(32),
@@ -375,7 +387,7 @@
     updated = decision_call(
         regrets_kernel, "new_regrets", hand_count, scale, jax.ShapeDtypeStruct((rows, hand_count), jnp.float32), inputs
     )
-    order = (3, 2, 1)
+    order = (2, 3, 1)
     total = chance(hand_count, order, [codes] + [swap(codes, "flop", mask) for mask in order])
     return (updated[None, :line_count], total[: line_count // ACTS])
 

time: 25.7 us -> 25.5 us (level)
  Pallas kernels: 9.19 us -> 8.76 us
    pallas_call x3, Pallas kernels: 7.08 us -> 6.65 us  [board_sums(): pl.pallas_call(kernel, out_shape=out, in_specs=[WHOLE] * (len(inputs) + l...]
  transfers between devices with their start and end apart: 7 -> 7, of which waited for: 4 -> 3; matrix products, arithmetic and copies ran while one was open for 0% -> 0% of each run, Pallas kernels for 18% -> 18%
where the time goes in v8:
time: 25.5 us; the launch traced here: 25.3 us
  starting transfers between devices  9.73 us (38%)
  Pallas kernels  8.76 us (34%)
  waiting for transfers between devices  4.97 us (19%)
  local copies, waits for them, and re-layouts  0.85 us (3%)
  between operations  0.84 us (3%)
    ppermute x7, starting transfers between devices, swap(): lax.ppermute(array, axes, [(index, index ^ mask) for index in range(lax.a...  9.73 us
    pallas_call x3, Pallas kernels, board_sums(): pl.pallas_call(kernel, out_shape=out, in_specs=[WHOLE] * (len(inputs) + l...  6.65 us
    ppermute x7, waiting for transfers between devices, swap(): lax.ppermute(array, axes, [(index, index ^ mask) for index in range(lax.a...  4.97 us
    pallas_call x2, Pallas kernels, decision_call(): pl.pallas_call(functools.partial(kernel, hand_count, scale), out_shape=ou...  1.28 us
    unnamed x22, local copies, waits for them, and re-layouts  0.85 us
    pallas_call x1, Pallas kernels, chance(): pl.pallas_call(functools.partial(chance_kernel, hand_count, order), out_s...  0.81 us
  transfers between devices with their start and end apart: 7, of which 3 were waited for; matrix products, arithmetic and copies ran while one was open for 0% of the time, Pallas kernels for 18%

profile of v8, /device:TPU:0, one launch (start us, length us, event | category | flops | bytes accessed | tf_op | source)
XLA Modules:
  0.0 25.3 jit_solution(11910525428558374257)
XLA Ops:
  0.7 0.0 copy-start.4
  0.7 0.0 copy-start.6
  0.7 0.0 copy-start.7
  0.7 0.0 copy-start.8
  0.7 0.0 copy-start.9
  0.7 0.0 copy-start.10
  0.7 0.0 copy-start
  0.7 0.0 copy-start.1
  0.7 0.0 copy-start.2
  0.8 0.5 %copy-done.4 = s32[1,32]{1,0:T(1,128)S(1)} copy-done((s32[1,32]{1,0:T(1,128)S(1)}, s32[1,32]{1,0:T(1,128)}, u32[]{:S(2)}) %copy-start.4) | copy-done | bytes 152
  1.3 0.2 copy-done.6
  1.6 0.1 negate_select_fusion.own_ref
  1.6 0.5 %collective-permute-start = (bf16[32,1326]{1,0:T(8,128)(2,1)S(1)}, bf16[32,1326]{1,0:T(8,128)(2,1)S(1)}, u32[]{:S(2)}, u32[]{:S(2)}) collective-permute-start(bf16[32,1326]{1,0:T(8,128)(2,1)S(1)} %negate_select_fusion.own_ref), channel_id=1, source_target_pairs={{0,2},{1,3},{2,0},{3,1},{4,6},{5,7},{6,4},{7,5},{8,10},{9,11},{10,... | collective-permute-start | bytes 254600 | tf_op jit(solution)/shard_map/ppermute | solution.py:328
  2.2 0.0 copy-done.7
  2.2 0.0 copy-done.8
  2.2 0.0 copy-done.9
  2.2 0.0 copy-done.10
  2.2 0.1 add_select_fusion.refs_3_
  2.3 2.5 %collective-permute-start.1 = (s32[2,1792]{1,0:T(2,128)S(1)}, s32[2,1792]{1,0:T(2,128)S(1)}, u32[]{:S(2)}, u32[]{:S(2)}) collective-permute-start(s32[2,1792]{1,0:T(2,128)S(1)} %add_select_fusion.refs_3_), channel_id=1, source_target_pairs={{0,1},{1,0},{2,3},{3,2},{4,5},{5,4},{6,7},{7,6},{8,9},{9,8},{10,11... | collective-permute-start | bytes 43016 | tf_op jit(solution)/shard_map/ppermute | solution.py:328
  4.8 0.0 collective-permute-done.mate_ref
  4.8 0.0 copy-done
  4.8 0.0 copy-done.1
  4.8 0.0 copy-done.2
  4.8 1.8 %first_boards.1 = (f32[32,1408]{1,0:T(8,128)S(1)}, f32[32,1408]{1,0:T(8,128)S(1)}, bf16[64,1408]{1,0:T(8,128)(2,1)S(1)}, s32[64,128]{1,0:T(8,128)S(1)}, s32[2,1792]{1,0:T(2,128)S(1)}) custom-call(bf16[32,1326]{1,0:T(8,128)(2,1)S(1)} %negate_select_fusion.own_ref, bf16[32,1326]{1,0:T(8,128)(2,1)S(1)} %collective-permute-done.mate_ref, ...), custom_call_target="tpu_custom_call" | custom-call | flops 507510784 | tf_op jit(solution)/shard_map/first_boards/pallas_call | solution.py:216
  6.6 0.0 collective-permute-done.1.refs_3_
  6.7 2.0 %collective-permute-start.2 = (s32[4,1792]{1,0:T(4,128)S(1)}, s32[4,1792]{1,0:T(4,128)S(1)}, u32[]{:S(2)}, u32[]{:S(2)}) collective-permute-start(s32[4,1792]{1,0:T(4,128)S(1)} %pad_add_fusion), channel_id=1, source_target_pairs={{0,4},{1,5},{2,6},{3,7},{4,0},{5,1},{6,2},{7,3},{8,12},{9,13},{10,... | collective-permute-start | bytes 86024 | tf_op jit(solution)/shard_map/ppermute | solution.py:328
  8.6 1.8 %more_boards.2 = (f32[32,1408]{1,0:T(8,128)S(1)}, f32[32,1408]{1,0:T(8,128)S(1)}) custom-call(bf16[64,1408]{1,0:T(8,128)(2,1)S(1)} %get-tuple-element.15.reach_ref, s32[64,128]{1,0:T(8,128)S(1)} %get-tuple-element.16.line_ref, bf16[1328,1408]{1,0:T(8,128)(2,1)S(1)} %copy-done, bf16[1408,128]{1,0:T(8,128)(2,1)S(1)} %copy-done.1, ...), custom_call_target="tpu_custom_call" | custom-call | flops 507510784 | tf_op jit(solution)/shard_map/more_boards/pallas_call | solution.py:216
  10.4 0.0 copy-start.3
  10.5 0.0 copy-start.5
  10.5 0.1 collective-permute-done.2.refs_3_
  10.6 3.1 %more_boards.3 = (f32[32,1408]{1,0:T(8,128)S(1)}, f32[32,1408]{1,0:T(8,128)S(1)}) custom-call(bf16[64,1408]{1,0:T(8,128)(2,1)S(1)} %get-tuple-element.15.reach_ref, s32[64,128]{1,0:T(8,128)S(1)} %get-tuple-element.16.line_ref, bf16[1328,1408]{1,0:T(8,128)(2,1)S(1)} %copy-done, bf16[1408,128]{1,0:T(8,128)(2,1)S(1)} %copy-done.1, ...), custom_call_target="tpu_custom_call" | custom-call | flops 1015021568 | tf_op jit(solution)/shard_map/more_boards/pallas_call | solution.py:216
  13.7 0.1 collective-permute-start.3
  13.8 1.4 %collective-permute-done.3.refs_1_ = f32[32,1408]{1,0:T(8,128)S(1)} collective-permute-done((f32[32,1408]{1,0:T(8,128)S(1)}, f32[32,1408]{1,0:T(8,128)S(1)}, u32[]{:S(2)}, u32[]{:S(2)}) %collective-permute-start.3) | collective-permute-done | bytes 180256 | tf_op jit(solution)/shard_map/ppermute | solution.py:328
  15.2 0.0 copy-done.3
  15.2 0.0 copy-done.5
  15.2 0.4 %node_codes.1.refs_0_ = s16[16,1408]{1,0:T(8,128)(2,1)S(1)} custom-call(f32[32,1408]{1,0:T(8,128)S(1)} %get-tuple-element.22.refs_0_, f32[32,1408]{1,0:T(8,128)S(1)} %collective-permute-done.3.refs_1_, s32[1,32]{1,0:T(1,128)S(1)} %copy-done.5, s32[1,32]{1,0:T(1,128)S(1)} %copy-done.4, f32[32,1326]{1,0:T(8,128)S(1)} %bitcast.9), custom_call_target="tpu_custom_call" | custom-call | tf_op jit(solution)/shard_map/node_codes/pallas_call | solution.py:286
  15.6 3.0 %collective-permute-start.4 = (s16[16,1408]{1,0:T(8,128)(2,1)S(1)}, s16[16,1408]{1,0:T(8,128)(2,1)S(1)}, u32[]{:S(2)}, u32[]{:S(2)}) collective-permute-start(s16[16,1408]{1,0:T(8,128)(2,1)S(1)} %node_codes.1.refs_0_), channel_id=1, source_target_pairs={{0,16},{8,24},{16,0},{24,8},{1,17},{9,25},{17,1},{25,9},{2,18},{10... | collective-permute-start | bytes 135176 | tf_op jit(solution)/shard_map/ppermute | solution.py:328
  18.6 1.3 %collective-permute-start.5 = (s16[16,1408]{1,0:T(8,128)(2,1)S(1)}, s16[16,1408]{1,0:T(8,128)(2,1)S(1)}, u32[]{:S(2)}, u32[]{:S(2)}) collective-permute-start(s16[16,1408]{1,0:T(8,128)(2,1)S(1)} %node_codes.1.refs_0_), channel_id=1, source_target_pairs={{0,24},{8,16},{16,8},{24,0},{1,25},{9,17},{17,9},{25,1},{2,26},{10... | collective-permute-start | bytes 135176 | tf_op jit(solution)/shard_map/ppermute | solution.py:328
  20.0 0.2 collective-permute-start.6
  20.2 0.9 %new_regrets.1 = f32[32,1326]{1,0:T(8,128)} custom-call(f32[32,1408]{1,0:T(8,128)S(1)} %get-tuple-element.22.refs_0_, f32[32,1408]{1,0:T(8,128)S(1)} %collective-permute-done.3.refs_1_, s32[1,32]{1,0:T(1,128)S(1)} %copy-done.5, s32[1,32]{1,0:T(1,128)S(1)} %copy-done.4, f32[32,1326]{1,0:T(8,128)S(1)} %bitcast.10), custom_call_target="tpu_custom_call" | custom-call | tf_op jit(solution)/shard_map/new_regrets/pallas_call | solution.py:286
  21.1 0.0 collective-permute-done.4.refs_1_
  21.1 3.4 %collective-permute-done.5.refs_2_ = s16[16,1408]{1,0:T(8,128)(2,1)S(1)} collective-permute-done((s16[16,1408]{1,0:T(8,128)(2,1)S(1)}, s16[16,1408]{1,0:T(8,128)(2,1)S(1)}, u32[]{:S(2)}, u32[]{:S(2)}) %collective-permute-start.5) | collective-permute-done | bytes 45088 | tf_op jit(solution)/shard_map/ppermute | solution.py:328
  24.5 0.0 collective-permute-done.6.refs_3_
  24.5 0.8 %chance_sum.1 = f32[16,1326]{1,0:T(8,128)} custom-call(s16[16,1408]{1,0:T(8,128)(2,1)S(1)} %node_codes.1.refs_0_, s16[16,1408]{1,0:T(8,128)(2,1)S(1)} %collective-permute-done.4.refs_1_, s16[16,1408]{1,0:T(8,128)(2,1)S(1)} %collective-permute-done.5.refs_2_, s16[16,1408]{1,0:T(8,128)(2,1)S(1)} %collective-permute-done.6.refs_3_), custom_call_target="tpu_custom_call" | custom-call | tf_op jit(solution)/shard_map/chance_sum/pallas_call | solution.py:317
  (5 shorter events, 0.0 us)
Async XLA Ops:
  0.7 0.7 %copy-start.4 = (s32[1,32]{1,0:T(1,128)S(1)}, s32[1,32]{1,0:T(1,128)}, u32[]{:S(2)}) copy-start(s32[1,32]{1,0:T(1,128)} %refs_3_.3) | copy-start | bytes 388
  0.7 0.9 %copy-start.6 = (bf16[1,32,1326]{2,1,0:T(8,128)(2,1)S(1)}, bf16[1,32,1326]{2,1,0:T(8,128)(2,1)}, u32[]{:S(2)}) copy-start(bf16[1,32,1326]{2,1,0:T(8,128)(2,1)} %param.12) | copy-start | bytes 254596
  0.7 1.5 %copy-start.7 = (s32[1,1,2,1326]{3,2,1,0:T(2,128)S(1)}, s32[1,1,2,1326]{3,2,1,0:T(2,128)}, u32[]{:S(2)}) copy-start(s32[1,1,2,1326]{3,2,1,0:T(2,128)} %param.18) | copy-start | bytes 31828
  0.7 1.5 %copy-start.8 = (s32[1,1,2,1326]{3,2,1,0:T(2,128)S(1)}, s32[1,1,2,1326]{3,2,1,0:T(2,128)}, u32[]{:S(2)}) copy-start(s32[1,1,2,1326]{3,2,1,0:T(2,128)} %param.17) | copy-start | bytes 31828
  0.7 1.5 %copy-start.9 = (s32[1,1,2,256]{3,2,1,0:T(2,128)S(1)}, s32[1,1,2,256]{3,2,1,0:T(2,128)}, u32[]{:S(2)}) copy-start(s32[1,1,2,256]{3,2,1,0:T(2,128)} %param.15) | copy-start | bytes 6148
  0.7 1.5 %copy-start.10 = (s32[1,1,2]{2,1,0:T(1,128)S(1)}, s32[1,1,2]{2,1,0:T(1,128)}, u32[]{:S(2)}) copy-start(s32[1,1,2]{2,1,0:T(1,128)} %param.16) | copy-start | bytes 28
  0.7 4.1 %copy-start = (bf16[1328,1408]{1,0:T(8,128)(2,1)S(1)}, bf16[1328,1408]{1,0:T(8,128)(2,1)}, u32[]{:S(2)}) copy-start(bf16[1328,1408]{1,0:T(8,128)(2,1)} %constant.5.clone.refs_0_) | copy-start | bytes 11218948
  0.7 4.1 %copy-start.1 = (bf16[1408,128]{1,0:T(8,128)(2,1)S(1)}, bf16[1408,128]{1,0:T(8,128)(2,1)}, u32[]{:S(2)}) copy-start(bf16[1408,128]{1,0:T(8,128)(2,1)} %constant.14.clone.refs_1_) | copy-start | bytes 1081348
  0.7 4.1 %copy-start.2 = (bf16[128,1408]{1,0:T(8,128)(2,1)S(1)}, bf16[128,1408]{1,0:T(8,128)(2,1)}, u32[]{:S(2)}) copy-start(bf16[128,1408]{1,0:T(8,128)(2,1)} %constant.15.clone.refs_2_) | copy-start | bytes 1081348
  1.6 3.2 %collective-permute-start = (bf16[32,1326]{1,0:T(8,128)(2,1)S(1)}, bf16[32,1326]{1,0:T(8,128)(2,1)S(1)}, u32[]{:S(2)}, u32[]{:S(2)}) collective-permute-start(bf16[32,1326]{1,0:T(8,128)(2,1)S(1)} %negate_select_fusion.own_ref), channel_id=1, source_target_pairs={{0,2},{1,3},{2,0},{3,1},{4,6},{5,7},{6,4},{7,5},{8,10},{9,11},{10,... | collective-permute-start | bytes 254600 | tf_op jit(solution)/shard_map/ppermute | solution.py:328
  2.3 4.3 %collective-permute-start.1 = (s32[2,1792]{1,0:T(2,128)S(1)}, s32[2,1792]{1,0:T(2,128)S(1)}, u32[]{:S(2)}, u32[]{:S(2)}) collective-permute-start(s32[2,1792]{1,0:T(2,128)S(1)} %add_select_fusion.refs_3_), channel_id=1, source_target_pairs={{0,1},{1,0},{2,3},{3,2},{4,5},{5,4},{6,7},{7,6},{8,9},{9,8},{10,11... | collective-permute-start | bytes 43016 | tf_op jit(solution)/shard_map/ppermute | solution.py:328
  6.7 3.9 %collective-permute-start.2 = (s32[4,1792]{1,0:T(4,128)S(1)}, s32[4,1792]{1,0:T(4,128)S(1)}, u32[]{:S(2)}, u32[]{:S(2)}) collective-permute-start(s32[4,1792]{1,0:T(4,128)S(1)} %pad_add_fusion), channel_id=1, source_target_pairs={{0,4},{1,5},{2,6},{3,7},{4,0},{5,1},{6,2},{7,3},{8,12},{9,13},{10,... | collective-permute-start | bytes 86024 | tf_op jit(solution)/shard_map/ppermute | solution.py:328
  10.4 4.7 %copy-start.3 = (f32[1,32,1326]{2,1,0:T(8,128)S(1)}, f32[1,32,1326]{2,1,0:T(8,128)}, u32[]{:S(2)}) copy-start(f32[1,32,1326]{2,1,0:T(8,128)} %param.11) | copy-start | bytes 509188
  10.5 4.7 %copy-start.5 = (s32[1,32]{1,0:T(1,128)S(1)}, s32[1,32]{1,0:T(1,128)}, u32[]{:S(2)}) copy-start(s32[1,32]{1,0:T(1,128)} %refs_2_.6) | copy-start | bytes 388
  13.7 1.5 %collective-permute-start.3 = (f32[32,1408]{1,0:T(8,128)S(1)}, f32[32,1408]{1,0:T(8,128)S(1)}, u32[]{:S(2)}, u32[]{:S(2)}) collective-permute-start(f32[32,1408]{1,0:T(8,128)S(1)} %get-tuple-element.23), channel_id=1, source_target_pairs={{0,2},{1,3},{2,0},{3,1},{4,6},{5,7},{6,4},{7,5},{8,10},{9,11},{10,... | collective-permute-start | bytes 540680 | tf_op jit(solution)/shard_map/ppermute | solution.py:328
  15.6 5.5 %collective-permute-start.4 = (s16[16,1408]{1,0:T(8,128)(2,1)S(1)}, s16[16,1408]{1,0:T(8,128)(2,1)S(1)}, u32[]{:S(2)}, u32[]{:S(2)}) collective-permute-start(s16[16,1408]{1,0:T(8,128)(2,1)S(1)} %node_codes.1.refs_0_), channel_id=1, source_target_pairs={{0,16},{8,24},{16,0},{24,8},{1,17},{9,25},{17,1},{25,9},{2,18},{10... | collective-permute-start | bytes 135176 | tf_op jit(solution)/shard_map/ppermute | solution.py:328
  18.6 5.9 %collective-permute-start.5 = (s16[16,1408]{1,0:T(8,128)(2,1)S(1)}, s16[16,1408]{1,0:T(8,128)(2,1)S(1)}, u32[]{:S(2)}, u32[]{:S(2)}) collective-permute-start(s16[16,1408]{1,0:T(8,128)(2,1)S(1)} %node_codes.1.refs_0_), channel_id=1, source_target_pairs={{0,24},{8,16},{16,8},{24,0},{1,25},{9,17},{17,9},{25,1},{2,26},{10... | collective-permute-start | bytes 135176 | tf_op jit(solution)/shard_map/ppermute | solution.py:328
  20.0 4.5 %collective-permute-start.6 = (s16[16,1408]{1,0:T(8,128)(2,1)S(1)}, s16[16,1408]{1,0:T(8,128)(2,1)S(1)}, u32[]{:S(2)}, u32[]{:S(2)}) collective-permute-start(s16[16,1408]{1,0:T(8,128)(2,1)S(1)} %node_codes.1.refs_0_), channel_id=1, source_target_pairs={{0,8},{8,0},{16,24},{24,16},{1,9},{9,1},{17,25},{25,17},{2,10},{10... | collective-permute-start | bytes 135176 | tf_op jit(solution)/shard_map/ppermute | solution.py:328

commit v9 on v8

--- a/solution.py
+++ b/solution.py
@@ -264,9 +264,21 @@
     refs[-1][...] = jnp.maximum(regrets + values - node, 0.0)
 
 
-def codes_kernel(hand_count, scale, *refs):
-    *inputs, code_out, node_ref = refs
-    _, _, node = decide(hand_count, scale, *inputs)
+def both(array):
+    rows = array.shape[0]
+    even = lax.broadcasted_iota(jnp.int32, (rows, 1), 0) % ACTS == 0
+    return array + jnp.where(even, pltpu.roll(array, rows - 1, 0), pltpu.roll(array, 1, 0))
+
+
+def weights_kernel(hand_count, scale, pot_ref, kind_ref, regret_ref, out_ref):
+    pot = as_column(pot_ref[...])
+    coef = jnp.where(as_column(kind_ref[...]) == 1, -pot, pot) * scale
+    positive = jnp.maximum(regret_ref[...], 0.0)
+    out_ref[...] = (positive + floor_share) * coef / (both(positive) + ACTS * floor_share)
+
+
+def codes_kernel(hand_count, scale, own_ref, mate_ref, weight_ref, code_out, node_ref):
+    node = both((own_ref[:, :hand_count] + mate_ref[:, :hand_count]) * weight_ref[...])
     rows = node.shape[0]
     size, flip = powers()
     largest = jnp.max(jnp.abs(node), axis=1, keepdims=True)
@@ -364,8 +376,19 @@
             jax.ShapeDtypeStruct(boards.shape, boards.dtype),
         ),
     )
+    scale = 1.0 / (board_total * hand_count)
     for mask in (*masks[1:], None):
         latest = arrived
+        if mask is None:
+            own, late_regrets, late_pots, late_kinds = lax.optimization_barrier((own, old_regrets, pots, kinds))
+            weights = decision_call(
+                weights_kernel,
+                "line_weights",
+                hand_count,
+                scale,
+                jax.ShapeDtypeStruct((rows, hand_count), jnp.float32),
+                (late_pots, late_kinds, late_regrets),
+            )
         if mask is not None:
             boards = jnp.concatenate([boards, latest], axis=0)
             arrived = swap(boards, group, mask)
@@ -373,7 +396,6 @@
             more_kernel, "more_boards", rows, (all_reach, lines), held_tables, latest, (own, for_mate)
         )
     mate = swap(for_mate, group, core)
-    scale = 1.0 / (board_total * hand_count)
     inputs = (own, mate, pots, kinds, old_regrets)
     codes = decision_call(
         codes_kernel,
@@ -381,13 +403,13 @@
         hand_count,
         scale,
         jax.ShapeDtypeStruct((rows // ACTS, wide), jnp.int16),
-        inputs,
+        (own, mate, weights),
         [pltpu.VMEM((wide // LANE, rows, LANE), jnp.float32)],
     )
     updated = decision_call(
         regrets_kernel, "new_regrets", hand_count, scale, jax.ShapeDtypeStruct((rows, hand_count), jnp.float32), inputs
     )
-    order = (2, 3, 1)
+    order = (1, 3, 2)
     total = chance(hand_count, order, [codes] + [swap(codes, "flop", mask) for mask in order])
     return (updated[None, :line_count], total[: line_count // ACTS])
 

time: 25.5 us -> 25.5 us (level)
    pallas_call x2 -> x3, Pallas kernels: 1.28 us -> 1.34 us  [decision_call(): pl.pallas_call(functools.partial(kernel, hand_count, scale), out_shape=ou...]
where the time goes in v9:
time: 25.5 us; the launch traced here: 25.3 us
  starting transfers between devices  9.69 us (38%)
  Pallas kernels  8.93 us (35%)
  waiting for transfers between devices  4.79 us (19%)
  local copies, waits for them, and re-layouts  0.85 us (3%)
  between operations  0.85 us (3%)
    ppermute x7, starting transfers between devices, swap(): lax.ppermute(array, axes, [(index, index ^ mask) for index in range(lax.a...  9.69 us
    pallas_call x3, Pallas kernels, board_sums(): pl.pallas_call(kernel, out_shape=out, in_specs=[WHOLE] * (len(inputs) + l...  6.75 us
    ppermute x7, waiting for transfers between devices, swap(): lax.ppermute(array, axes, [(index, index ^ mask) for index in range(lax.a...  4.79 us
    pallas_call x3, Pallas kernels, decision_call(): pl.pallas_call(functools.partial(kernel, hand_count, scale), out_shape=ou...  1.34 us
    unnamed x22, local copies, waits for them, and re-layouts  0.85 us
    pallas_call x1, Pallas kernels, chance(): pl.pallas_call(functools.partial(chance_kernel, hand_count, order), out_s...  0.81 us
  transfers between devices with their start and end apart: 7, of which 3 were waited for; matrix products, arithmetic and copies ran while one was open for 0% of the time, Pallas kernels for 18%

profile of v9, /device:TPU:0, one launch (start us, length us, event | category | flops | bytes accessed | tf_op | source)
XLA Modules:
  0.0 25.3 jit_solution(15918200958874895407)
XLA Ops:
  0.7 0.0 copy-start.4
  0.7 0.0 copy-start.6
  0.7 0.0 copy-start.7
  0.7 0.0 copy-start.8
  0.7 0.0 copy-start.9
  0.7 0.0 copy-start.10
  0.7 0.0 copy-start
  0.7 0.0 copy-start.1
  0.7 0.0 copy-start.2
  0.8 0.5 %copy-done.4 = s32[1,32]{1,0:T(1,128)S(1)} copy-done((s32[1,32]{1,0:T(1,128)S(1)}, s32[1,32]{1,0:T(1,128)}, u32[]{:S(2)}) %copy-start.4) | copy-done | bytes 152
  1.3 0.2 copy-done.6
  1.6 0.1 negate_select_fusion.own_ref
  1.6 0.5 %collective-permute-start = (bf16[32,1326]{1,0:T(8,128)(2,1)S(1)}, bf16[32,1326]{1,0:T(8,128)(2,1)S(1)}, u32[]{:S(2)}, u32[]{:S(2)}) collective-permute-start(bf16[32,1326]{1,0:T(8,128)(2,1)S(1)} %negate_select_fusion.own_ref), channel_id=1, source_target_pairs={{0,2},{1,3},{2,0},{3,1},{4,6},{5,7},{6,4},{7,5},{8,10},{9,11},{10,... | collective-permute-start | bytes 254600 | tf_op jit(solution)/shard_map/ppermute | solution.py:340
  2.2 0.0 copy-done.7
  2.2 0.0 copy-done.8
  2.2 0.0 copy-done.9
  2.2 0.0 copy-done.10
  2.2 0.1 add_select_fusion.refs_3_
  2.3 2.5 %collective-permute-start.1 = (s32[2,1792]{1,0:T(2,128)S(1)}, s32[2,1792]{1,0:T(2,128)S(1)}, u32[]{:S(2)}, u32[]{:S(2)}) collective-permute-start(s32[2,1792]{1,0:T(2,128)S(1)} %add_select_fusion.refs_3_), channel_id=1, source_target_pairs={{0,1},{1,0},{2,3},{3,2},{4,5},{5,4},{6,7},{7,6},{8,9},{9,8},{10,11... | collective-permute-start | bytes 43016 | tf_op jit(solution)/shard_map/ppermute | solution.py:340
  4.8 0.0 collective-permute-done.mate_ref
  4.8 0.0 copy-done
  4.8 0.0 copy-done.1
  4.8 0.0 copy-done.2
  4.8 1.8 %first_boards.1 = (f32[32,1408]{1,0:T(8,128)S(1)}, f32[32,1408]{1,0:T(8,128)S(1)}, bf16[64,1408]{1,0:T(8,128)(2,1)S(1)}, s32[64,128]{1,0:T(8,128)S(1)}, s32[2,1792]{1,0:T(2,128)S(1)}) custom-call(bf16[32,1326]{1,0:T(8,128)(2,1)S(1)} %negate_select_fusion.own_ref, bf16[32,1326]{1,0:T(8,128)(2,1)S(1)} %collective-permute-done.mate_ref, ...), custom_call_target="tpu_custom_call" | custom-call | flops 507510784 | tf_op jit(solution)/shard_map/first_boards/pallas_call | solution.py:216
  6.6 0.0 collective-permute-done.1.refs_3_
  6.7 2.0 %collective-permute-start.2 = (s32[4,1792]{1,0:T(4,128)S(1)}, s32[4,1792]{1,0:T(4,128)S(1)}, u32[]{:S(2)}, u32[]{:S(2)}) collective-permute-start(s32[4,1792]{1,0:T(4,128)S(1)} %pad_add_fusion), channel_id=1, source_target_pairs={{0,4},{1,5},{2,6},{3,7},{4,0},{5,1},{6,2},{7,3},{8,12},{9,13},{10,... | collective-permute-start | bytes 86024 | tf_op jit(solution)/shard_map/ppermute | solution.py:340
  8.6 1.8 %more_boards.2 = (f32[32,1408]{1,0:T(8,128)S(1)}, f32[32,1408]{1,0:T(8,128)S(1)}) custom-call(bf16[64,1408]{1,0:T(8,128)(2,1)S(1)} %get-tuple-element.19.reach_ref, s32[64,128]{1,0:T(8,128)S(1)} %get-tuple-element.20.line_ref, bf16[1328,1408]{1,0:T(8,128)(2,1)S(1)} %copy-done, bf16[1408,128]{1,0:T(8,128)(2,1)S(1)} %copy-done.2, ...), custom_call_target="tpu_custom_call" | custom-call | flops 507510784 | tf_op jit(solution)/shard_map/more_boards/pallas_call | solution.py:216
  10.5 0.0 copy-start.3
  10.5 0.0 copy-start.5
  10.5 0.1 collective-permute-done.2.refs_3_
  10.6 3.1 %more_boards.3 = (f32[32,1408]{1,0:T(8,128)S(1)}, f32[32,1408]{1,0:T(8,128)S(1)}) custom-call(bf16[64,1408]{1,0:T(8,128)(2,1)S(1)} %get-tuple-element.19.reach_ref, s32[64,128]{1,0:T(8,128)S(1)} %get-tuple-element.20.line_ref, bf16[1328,1408]{1,0:T(8,128)(2,1)S(1)} %copy-done, bf16[1408,128]{1,0:T(8,128)(2,1)S(1)} %copy-done.2, ...), custom_call_target="tpu_custom_call" | custom-call | flops 1015021568 | tf_op jit(solution)/shard_map/more_boards/pallas_call | solution.py:216
  13.8 0.1 collective-permute-start.3
  13.8 0.0 copy-done.3
  13.8 0.0 copy-done.5
  13.9 0.1 line_weights.1.weight_ref
  14.0 1.2 %collective-permute-done.3.refs_1_.mate_ref = f32[32,1408]{1,0:T(8,128)S(1)} collective-permute-done((f32[32,1408]{1,0:T(8,128)S(1)}, f32[32,1408]{1,0:T(8,128)S(1)}, u32[]{:S(2)}, u32[]{:S(2)}) %collective-permute-start.3) | collective-permute-done | bytes 180256 | tf_op jit(solution)/shard_map/ppermute | solution.py:340
  15.2 0.3 %node_codes.1.refs_0_ = s16[16,1408]{1,0:T(8,128)(2,1)S(1)} custom-call(f32[32,1408]{1,0:T(8,128)S(1)} %get-tuple-element.27.refs_0_.own_ref, f32[32,1408]{1,0:T(8,128)S(1)} %collective-permute-done.3.refs_1_.mate_ref, f32[32,1326]{1,0:T(8,128)S(1)} %line_weights.1.weight_ref), custom_call_target="tpu_custom_call" | custom-call | tf_op jit(solution)/shard_map/node_codes/pallas_call | solution.py:298
  15.6 3.0 %collective-permute-start.6 = (s16[16,1408]{1,0:T(8,128)(2,1)S(1)}, s16[16,1408]{1,0:T(8,128)(2,1)S(1)}, u32[]{:S(2)}, u32[]{:S(2)}) collective-permute-start(s16[16,1408]{1,0:T(8,128)(2,1)S(1)} %node_codes.1.refs_0_), channel_id=1, source_target_pairs={{0,16},{8,24},{16,0},{24,8},{1,17},{9,25},{17,1},{25,9},{2,18},{10... | collective-permute-start | bytes 135176 | tf_op jit(solution)/shard_map/ppermute | solution.py:340
  18.6 1.3 %collective-permute-start.5 = (s16[16,1408]{1,0:T(8,128)(2,1)S(1)}, s16[16,1408]{1,0:T(8,128)(2,1)S(1)}, u32[]{:S(2)}, u32[]{:S(2)}) collective-permute-start(s16[16,1408]{1,0:T(8,128)(2,1)S(1)} %node_codes.1.refs_0_), channel_id=1, source_target_pairs={{0,24},{8,16},{16,8},{24,0},{1,25},{9,17},{17,9},{25,1},{2,26},{10... | collective-permute-start | bytes 135176 | tf_op jit(solution)/shard_map/ppermute | solution.py:340
  20.0 0.2 collective-permute-start.4
  20.2 0.9 %new_regrets.1 = f32[32,1326]{1,0:T(8,128)} custom-call(f32[32,1408]{1,0:T(8,128)S(1)} %get-tuple-element.27.refs_0_.own_ref, f32[32,1408]{1,0:T(8,128)S(1)} %collective-permute-done.3.refs_1_.mate_ref, s32[1,32]{1,0:T(1,128)S(1)} %copy-done.5, s32[1,32]{1,0:T(1,128)S(1)} %copy-done.4, f32[32,1326]{1,0:T(8,128)S(1)} %bitcast.10), custom_call_target="tpu_custom_call" | custom-call | tf_op jit(solution)/shard_map/new_regrets/pallas_call | solution.py:298
  21.1 0.0 collective-permute-done.6.refs_3_
  21.1 3.4 %collective-permute-done.5.refs_2_ = s16[16,1408]{1,0:T(8,128)(2,1)S(1)} collective-permute-done((s16[16,1408]{1,0:T(8,128)(2,1)S(1)}, s16[16,1408]{1,0:T(8,128)(2,1)S(1)}, u32[]{:S(2)}, u32[]{:S(2)}) %collective-permute-start.5) | collective-permute-done | bytes 45088 | tf_op jit(solution)/shard_map/ppermute | solution.py:340
  24.5 0.0 collective-permute-done.4.refs_1_
  24.5 0.8 %chance_sum.1 = f32[16,1326]{1,0:T(8,128)} custom-call(s16[16,1408]{1,0:T(8,128)(2,1)S(1)} %node_codes.1.refs_0_, s16[16,1408]{1,0:T(8,128)(2,1)S(1)} %collective-permute-done.4.refs_1_, s16[16,1408]{1,0:T(8,128)(2,1)S(1)} %collective-permute-done.5.refs_2_, s16[16,1408]{1,0:T(8,128)(2,1)S(1)} %collective-permute-done.6.refs_3_), custom_call_target="tpu_custom_call" | custom-call | tf_op jit(solution)/shard_map/chance_sum/pallas_call | solution.py:329
  (5 shorter events, 0.0 us)
Async XLA Ops:
  0.7 0.7 %copy-start.4 = (s32[1,32]{1,0:T(1,128)S(1)}, s32[1,32]{1,0:T(1,128)}, u32[]{:S(2)}) copy-start(s32[1,32]{1,0:T(1,128)} %kind_ref) | copy-start | bytes 388
  0.7 0.9 %copy-start.6 = (bf16[1,32,1326]{2,1,0:T(8,128)(2,1)S(1)}, bf16[1,32,1326]{2,1,0:T(8,128)(2,1)}, u32[]{:S(2)}) copy-start(bf16[1,32,1326]{2,1,0:T(8,128)(2,1)} %param.12) | copy-start | bytes 254596
  0.7 1.5 %copy-start.7 = (s32[1,1,2,1326]{3,2,1,0:T(2,128)S(1)}, s32[1,1,2,1326]{3,2,1,0:T(2,128)}, u32[]{:S(2)}) copy-start(s32[1,1,2,1326]{3,2,1,0:T(2,128)} %param.18) | copy-start | bytes 31828
  0.7 1.5 %copy-start.8 = (s32[1,1,2,1326]{3,2,1,0:T(2,128)S(1)}, s32[1,1,2,1326]{3,2,1,0:T(2,128)}, u32[]{:S(2)}) copy-start(s32[1,1,2,1326]{3,2,1,0:T(2,128)} %param.17) | copy-start | bytes 31828
  0.7 1.5 %copy-start.9 = (s32[1,1,2,256]{3,2,1,0:T(2,128)S(1)}, s32[1,1,2,256]{3,2,1,0:T(2,128)}, u32[]{:S(2)}) copy-start(s32[1,1,2,256]{3,2,1,0:T(2,128)} %param.15) | copy-start | bytes 6148
  0.7 1.5 %copy-start.10 = (s32[1,1,2]{2,1,0:T(1,128)S(1)}, s32[1,1,2]{2,1,0:T(1,128)}, u32[]{:S(2)}) copy-start(s32[1,1,2]{2,1,0:T(1,128)} %param.16) | copy-start | bytes 28
  0.7 4.1 %copy-start = (bf16[1328,1408]{1,0:T(8,128)(2,1)S(1)}, bf16[1328,1408]{1,0:T(8,128)(2,1)}, u32[]{:S(2)}) copy-start(bf16[1328,1408]{1,0:T(8,128)(2,1)} %constant.5.clone.refs_0_) | copy-start | bytes 11218948
  0.7 4.1 %copy-start.1 = (bf16[128,1408]{1,0:T(8,128)(2,1)S(1)}, bf16[128,1408]{1,0:T(8,128)(2,1)}, u32[]{:S(2)}) copy-start(bf16[128,1408]{1,0:T(8,128)(2,1)} %constant.15.clone.refs_2_) | copy-start | bytes 1081348
  0.7 4.1 %copy-start.2 = (bf16[1408,128]{1,0:T(8,128)(2,1)S(1)}, bf16[1408,128]{1,0:T(8,128)(2,1)}, u32[]{:S(2)}) copy-start(bf16[1408,128]{1,0:T(8,128)(2,1)} %constant.14.clone.refs_1_) | copy-start | bytes 1081348
  1.6 3.2 %collective-permute-start = (bf16[32,1326]{1,0:T(8,128)(2,1)S(1)}, bf16[32,1326]{1,0:T(8,128)(2,1)S(1)}, u32[]{:S(2)}, u32[]{:S(2)}) collective-permute-start(bf16[32,1326]{1,0:T(8,128)(2,1)S(1)} %negate_select_fusion.own_ref), channel_id=1, source_target_pairs={{0,2},{1,3},{2,0},{3,1},{4,6},{5,7},{6,4},{7,5},{8,10},{9,11},{10,... | collective-permute-start | bytes 254600 | tf_op jit(solution)/shard_map/ppermute | solution.py:340
  2.3 4.4 %collective-permute-start.1 = (s32[2,1792]{1,0:T(2,128)S(1)}, s32[2,1792]{1,0:T(2,128)S(1)}, u32[]{:S(2)}, u32[]{:S(2)}) collective-permute-start(s32[2,1792]{1,0:T(2,128)S(1)} %add_select_fusion.refs_3_), channel_id=1, source_target_pairs={{0,1},{1,0},{2,3},{3,2},{4,5},{5,4},{6,7},{7,6},{8,9},{9,8},{10,11... | collective-permute-start | bytes 43016 | tf_op jit(solution)/shard_map/ppermute | solution.py:340
  6.7 3.9 %collective-permute-start.2 = (s32[4,1792]{1,0:T(4,128)S(1)}, s32[4,1792]{1,0:T(4,128)S(1)}, u32[]{:S(2)}, u32[]{:S(2)}) collective-permute-start(s32[4,1792]{1,0:T(4,128)S(1)} %pad_add_fusion), channel_id=1, source_target_pairs={{0,4},{1,5},{2,6},{3,7},{4,0},{5,1},{6,2},{7,3},{8,12},{9,13},{10,... | collective-permute-start | bytes 86024 | tf_op jit(solution)/shard_map/ppermute | solution.py:340
  10.5 3.4 %copy-start.3 = (f32[1,32,1326]{2,1,0:T(8,128)S(1)}, f32[1,32,1326]{2,1,0:T(8,128)}, u32[]{:S(2)}) copy-start(f32[1,32,1326]{2,1,0:T(8,128)} %param.11) | copy-start | bytes 509188
  10.5 3.4 %copy-start.5 = (s32[1,32]{1,0:T(1,128)S(1)}, s32[1,32]{1,0:T(1,128)}, u32[]{:S(2)}) copy-start(s32[1,32]{1,0:T(1,128)} %pot_ref) | copy-start | bytes 388
  13.8 1.5 %collective-permute-start.3 = (f32[32,1408]{1,0:T(8,128)S(1)}, f32[32,1408]{1,0:T(8,128)S(1)}, u32[]{:S(2)}, u32[]{:S(2)}) collective-permute-start(f32[32,1408]{1,0:T(8,128)S(1)} %get-tuple-element.28), channel_id=1, source_target_pairs={{0,2},{1,3},{2,0},{3,1},{4,6},{5,7},{6,4},{7,5},{8,10},{9,11},{10,... | collective-permute-start | bytes 540680 | tf_op jit(solution)/shard_map/ppermute | solution.py:340
  15.6 5.5 %collective-permute-start.6 = (s16[16,1408]{1,0:T(8,128)(2,1)S(1)}, s16[16,1408]{1,0:T(8,128)(2,1)S(1)}, u32[]{:S(2)}, u32[]{:S(2)}) collective-permute-start(s16[16,1408]{1,0:T(8,128)(2,1)S(1)} %node_codes.1.refs_0_), channel_id=1, source_target_pairs={{0,16},{8,24},{16,0},{24,8},{1,17},{9,25},{17,1},{25,9},{2,18},{10... | collective-permute-start | bytes 135176 | tf_op jit(solution)/shard_map/ppermute | solution.py:340
  18.6 5.9 %collective-permute-start.5 = (s16[16,1408]{1,0:T(8,128)(2,1)S(1)}, s16[16,1408]{1,0:T(8,128)(2,1)S(1)}, u32[]{:S(2)}, u32[]{:S(2)}) collective-permute-start(s16[16,1408]{1,0:T(8,128)(2,1)S(1)} %node_codes.1.refs_0_), channel_id=1, source_target_pairs={{0,24},{8,16},{16,8},{24,0},{1,25},{9,17},{17,9},{25,1},{2,26},{10... | collective-permute-start | bytes 135176 | tf_op jit(solution)/shard_map/ppermute | solution.py:340
  20.0 4.5 %collective-permute-start.4 = (s16[16,1408]{1,0:T(8,128)(2,1)S(1)}, s16[16,1408]{1,0:T(8,128)(2,1)S(1)}, u32[]{:S(2)}, u32[]{:S(2)}) collective-permute-start(s16[16,1408]{1,0:T(8,128)(2,1)S(1)} %node_codes.1.refs_0_), channel_id=1, source_target_pairs={{0,8},{8,0},{16,24},{24,16},{1,9},{9,1},{17,25},{25,17},{2,10},{10... | collective-permute-start | bytes 135176 | tf_op jit(solution)/shard_map/ppermute | solution.py:340
